TPU v7x, 512 devices: a whole 4x4x16 slice. The times are simulated.
512 devices in a mesh: space: 128 (over y, z, core), chan: 4 (over x).
Axes of the slice: x: 4, y: 4, z: 16, core: 2. Of those that a mesh axis runs over, the one named last changes fastest.
Arguments:
- features: bfloat16 [512, 128, 512], P('space', 'chan'), may hold values from -6 to 6
- occupancy: int32 [512, 512], P('space'), may hold values 0 or 1
- weight: bfloat16 [256, 27, 128], P('chan'), may hold values from -0.109375 to 0.109375
- cotangent: bfloat16 [512, 256, 512], P('space', 'chan'), may hold values from -6 to 6
- neighbours: int32 [512, 26], P('space'), may hold values from -1 to 511, as said below
Outputs:
- activation: bfloat16 [512, 256, 512], P('space', 'chan')
- input_grad: bfloat16 [512, 128, 512], P('space', 'chan')
- weight_grad: float32 [256, 27, 128], P('chan')
Inputs may be any that keep to these rules, and one draw needn't show every extreme that they name: `neighbours`: each entry is -1 or a block id. With o = id // 4 the listing block's owner, an entry names a block of owner o, or, only for a listing block among the first 1 of its owner and only in columns 0 to 12, one of the last 1 block of owner o - 1, or, only for a listing block among the last 1 of its owner and only in columns 13 to 25, one of the first 1 block of owner o + 1. The same block may appear in several directions.
All inputs are finite; a program needn't handle non-finite values. No bound on the sum of `occupancy` on one device may be relied on, other than what follows from the above.
Results may differ from a plain program's by a relative error of at most 0.0049.
Values may be sent and summed in bfloat16 or wider, within the bound.
No kernel may reach another device: no remote copies, remote signals or barrier semaphores. Data moves between devices by JAX's collectives and lax.ppermute only.
A program may use at most 64 MiB of HBM per device.

v0:
```python
import jax
import jax.numpy as jnp
from jax import lax
from jax.sharding import PartitionSpec as P


def with_halo(block, sides, width):
    for axis, dim in sides:
        count = lax.axis_size(axis)
        forward = [(i, i + 1) for i in range(count - 1)]
        backward = [(target, source) for source, target in forward]
        low = lax.ppermute(
            lax.slice_in_dim(block, block.shape[dim] - width, None, axis=dim), axis, forward
        )
        high = lax.ppermute(lax.slice_in_dim(block, 0, width, axis=dim), axis, backward)
        block = jnp.concatenate([low, block, high], axis=dim)
    return block


def shifted(value, axis, steps):
    count = lax.axis_size(axis)
    first, last = (max(0, -steps), min(count, count - steps))
    return lax.ppermute(value, axis, [(source, source + steps) for source in range(first, last)])


def offset_list():
    return [(a, b, c) for a in (-1, 0, 1) for b in (-1, 0, 1) for c in (-1, 0, 1)]


def build_patches(blocks):
    channels = blocks.shape[1]
    cube_grid = blocks.reshape(3, 3, 3, channels, 8, 8, 8)
    cube_grid = jnp.transpose(cube_grid, (3, 0, 4, 1, 5, 2, 6)).reshape(channels, 24, 24, 24)
    padded = cube_grid[:, 7:17, 7:17, 7:17]
    pieces = [padded[:, 1 + a : 9 + a, 1 + b : 9 + b, 1 + c : 9 + c] for a, b, c in offset_list()]
    return jnp.stack(pieces).reshape(27 * channels, 512)


def fold_back(grad_patches, channels):
    terms = grad_patches.reshape(27, channels, 8, 8, 8)
    padded_grad = jnp.zeros((channels, 10, 10, 10), jnp.float32)
    for offset_id, (a, b, c) in enumerate(offset_list()):
        padded_grad = padded_grad + jnp.pad(
            terms[offset_id], ((0, 0), (1 + a, 1 - a), (1 + b, 1 - b), (1 + c, 1 - c))
        )
    wide_grid = jnp.pad(padded_grad, ((0, 0), (7, 7), (7, 7), (7, 7))).reshape(
        channels, 3, 8, 3, 8, 3, 8
    )
    return jnp.transpose(wide_grid, (1, 3, 5, 0, 2, 4, 6)).reshape(27, channels, 512)


def on_device(features, occupancy, weight, cotangent, neighbours):
    block_count = features.shape[0]
    active_voxel_mask = occupancy.astype(jnp.bfloat16)
    mask_applied = features * active_voxel_mask[:, None, :]
    widened = lax.all_gather(mask_applied, "chan", axis=1, tiled=True)
    enlarged_block = with_halo(widened, (("space", 0),), block_count)
    place = lax.axis_index("space")
    first_local = place * block_count - block_count
    self_ids = (place * block_count + jnp.arange(block_count, dtype=jnp.int32))[:, None]
    every_index_list = jnp.concatenate([neighbours[:, :13], self_ids, neighbours[:, 13:]], axis=1)
    present_all = every_index_list >= 0
    slot_ids = jnp.where(present_all, every_index_list - first_local, 0)
    cout_local = weight.shape[0]
    cin = weight.shape[2]
    weight_flat = weight.reshape(cout_local, 27 * cin)
    contract_last = (((1,), (1,)), ((), ()))
    contract_first = (((0,), (0,)), ((), ()))

    def visit(totals, position):
        weight_running_sum, grad_cubes = totals
        slots = slot_ids[position]
        present = present_all[position]
        blocks = enlarged_block[slots] * present.astype(jnp.bfloat16)[:, None, None]
        patches = build_patches(blocks)
        pre_act = jnp.dot(weight_flat, patches, preferred_element_type=jnp.float32)
        live_row = occupancy[position].astype(jnp.float32)[None, :]
        output = (jax.nn.silu(pre_act) * live_row).astype(jnp.bfloat16)
        sigma = jax.nn.sigmoid(pre_act)
        slope = sigma * (1.0 + pre_act * (1.0 - sigma))
        grad_pre = (cotangent[position].astype(jnp.float32) * slope * live_row).astype(jnp.bfloat16)
        weight_terms = lax.dot_general(
            grad_pre, patches, contract_last, preferred_element_type=jnp.float32
        )
        grad_patches = lax.dot_general(
            weight_flat, grad_pre, contract_first, preferred_element_type=jnp.float32
        )
        pieces = fold_back(grad_patches, cin) * present.astype(jnp.float32)[:, None, None]
        grad_cubes = grad_cubes.at[slots].add(pieces)
        return ((weight_running_sum + weight_terms, grad_cubes), output)

    start = (
        jnp.zeros((cout_local, 27 * cin), jnp.float32),
        jnp.zeros((block_count + 2 * block_count, cin, 512), jnp.float32),
    )
    (weight_running_sum, grad_acc), activation = lax.scan(
        visit, start, jnp.arange(block_count, dtype=jnp.int32)
    )
    rest = block_count - block_count
    sum_reduced = grad_acc[block_count : block_count + block_count]
    for stride, rim_part, spacing in (
        (1, grad_acc[block_count + block_count :], (0, rest)),
        (-1, grad_acc[:block_count], (rest, 0)),
    ):
        arrived = shifted(rim_part.astype(jnp.bfloat16), "space", stride).astype(rim_part.dtype)
        sum_reduced = sum_reduced + arrived
    reduced_own = lax.psum_scatter(sum_reduced, "chan", scatter_dimension=1, tiled=True)
    input_grad = (reduced_own * occupancy.astype(jnp.float32)[:, None, :]).astype(jnp.bfloat16)
    weight_total = lax.psum(weight_running_sum.reshape(cout_local, 27, cin), "space")
    weight_grad = weight_total * lax.rsqrt(jnp.float32(lax.axis_size("space") * block_count * 512))
    return (activation, input_grad, weight_grad)


def solution(mesh):
    placed = (
        P("space", "chan", None),
        P("space", None),
        P("chan", None, None),
        P("space", "chan", None),
        P("space", None),
    )
    return jax.shard_map(
        on_device,
        mesh=mesh,
        in_specs=placed,
        out_specs=(P("space", "chan", None), P("space", "chan", None), P("chan", None, None)),
        check_vma=False,
    )
```

profile of v0, /device:TPU:1, one launch (start us, length us, event | category | flops | bytes accessed | tf_op | source)
XLA Modules:
  0.0 641.4 jit_solution(4298751308414270795)
XLA Ops:
  10.4 11.1 %all_gather.3 = bf16[4,128,512]{2,1,0:T(8,128)(2,1)S(1)} all-gather(bf16[4,32,512]{2,1,0:T(8,128)(2,1)S(1)} %broadcast_multiply_fusion.2), channel_id=1, replica_groups=mesh['space'=128,'chan'=4] {'chan'}, dimensions={1}, use_global_device_ids=true | all-gather | bytes 655360 | tf_op jit(solution)/shard_map/all_gather | solution.py:56
  21.4 10.5 %collective-permute-start.1 = (bf16[4,128,512]{2,1,0:T(8,128)(2,1)S(1)}, bf16[4,128,512]{2,1,0:T(8,128)(2,1)S(1)}, u32[]{:S(2)}, u32[]{:S(2)}) collective-permute-start(bf16[4,128,512]{2,1,0:T(8,128)(2,1)S(1)} %all_gather.3), channel_id=1, source_target_pairs={{4,0},{8,4},{12,8},{16,12},{20,16},{24,20},{28,24},{32,28},{36,32}... | collective-permute-start | bytes 1572872 | tf_op jit(solution)/shard_map/ppermute | solution.py:15
  36.1 3.9 collective-permute-done
  41.5 2.0 broadcast_in_dim.27
  43.5 238.3 %while.17 = (s32[]{:T(128)}, f32[64,3456]{1,0:T(8,128)S(1)}, f32[12,128,512]{2,1,0:T(8,128)}, bf16[4,64,512]{2,1,0:T(8,128)(2,1)}, s32[4]{0:T(128)S(1)}, /*index...) while((s32[]{:T(128)}, f32[64,3456]{1,0:T(8,128)S(1)}, ...), condition=%wide.region_2.3_spmd.clone, body=%wide.region_0.2_spmd.clone.sunk | while | flops 689475200 | bytes 152919280 | solution.py:96
  46.9 2.6 gather_fusion
  49.5 5.7 copy.45
  55.2 2.3 multiply_bitcast_fusion.2
  59.7 4.0 copy.47
  63.8 2.7 bitcast_dynamic-update-slice_fusion.2
  66.4 2.3 convolution_add_fusion.2
  68.7 2.0 convolution_bitcast_fusion.2
  74.2 3.8 broadcast_multiply_fusion.4
  77.9 8.0 %copy.49 = f32[27,128,512]{2,1,0:T(8,128)} copy(f32[27,128,512]{1,2,0:T(8,128)} %broadcast_multiply_fusion.4) | data formatting | bytes 14155776 | tf_op jit(solution)/shard_map/while/body/eval_jaxpr/mul | solution.py:88
  85.9 17.2 %scatter_fusion = f32[12,128,512]{2,1,0:T(8,128)} fusion(f32[12,128,512]{2,1,0:T(8,128)} %get-tuple-element.386, s32[27]{0:T(128)S(1)} %fusion.89, f32[27,128,512]{2,1,0:T(8,128)} %copy.49), kind=kCustom, calls=%fused_computation.1.clone.clone.1 | custom fusion | flops 1769472 | bytes 21233772 | tf_op jit(solution)/shard_map/while/body/eval_jaxpr/scatter-add | solution.py:89
  106.5 2.6 gather_fusion
  109.1 5.7 copy.45
  114.8 2.3 multiply_bitcast_fusion.2
  119.3 4.0 copy.47
  123.3 2.7 bitcast_dynamic-update-slice_fusion.2
  126.0 2.3 convolution_add_fusion.2
  133.7 3.8 broadcast_multiply_fusion.4
  137.5 8.0 %copy.49 = f32[27,128,512]{2,1,0:T(8,128)} copy(f32[27,128,512]{1,2,0:T(8,128)} %broadcast_multiply_fusion.4) | data formatting | bytes 14155776 | tf_op jit(solution)/shard_map/while/body/eval_jaxpr/mul | solution.py:88
  145.5 17.0 %scatter_fusion = f32[12,128,512]{2,1,0:T(8,128)} fusion(f32[12,128,512]{2,1,0:T(8,128)} %get-tuple-element.386, s32[27]{0:T(128)S(1)} %fusion.89, f32[27,128,512]{2,1,0:T(8,128)} %copy.49), kind=kCustom, calls=%fused_computation.1.clone.clone.1 | custom fusion | flops 1769472 | bytes 21233772 | tf_op jit(solution)/shard_map/while/body/eval_jaxpr/scatter-add | solution.py:89
  165.8 2.6 gather_fusion
  168.4 5.7 copy.45
  174.2 2.3 multiply_bitcast_fusion.2
  178.7 4.0 copy.47
  182.7 2.7 bitcast_dynamic-update-slice_fusion.2
  185.3 2.3 convolution_add_fusion.2
  193.1 3.8 broadcast_multiply_fusion.4
  196.8 8.0 %copy.49 = f32[27,128,512]{2,1,0:T(8,128)} copy(f32[27,128,512]{1,2,0:T(8,128)} %broadcast_multiply_fusion.4) | data formatting | bytes 14155776 | tf_op jit(solution)/shard_map/while/body/eval_jaxpr/mul | solution.py:88
  204.8 17.2 %scatter_fusion = f32[12,128,512]{2,1,0:T(8,128)} fusion(f32[12,128,512]{2,1,0:T(8,128)} %get-tuple-element.386, s32[27]{0:T(128)S(1)} %fusion.89, f32[27,128,512]{2,1,0:T(8,128)} %copy.49), kind=kCustom, calls=%fused_computation.1.clone.clone.1 | custom fusion | flops 1769472 | bytes 21233772 | tf_op jit(solution)/shard_map/while/body/eval_jaxpr/scatter-add | solution.py:89
  225.5 2.6 gather_fusion
  228.1 5.7 copy.45
  233.8 2.3 multiply_bitcast_fusion.2
  238.3 4.0 copy.47
  242.3 2.7 bitcast_dynamic-update-slice_fusion.2
  245.0 2.3 convolution_add_fusion.2
  252.7 3.8 broadcast_multiply_fusion.4
  256.5 8.0 %copy.49 = f32[27,128,512]{2,1,0:T(8,128)} copy(f32[27,128,512]{1,2,0:T(8,128)} %broadcast_multiply_fusion.4) | data formatting | bytes 14155776 | tf_op jit(solution)/shard_map/while/body/eval_jaxpr/mul | solution.py:88
  264.5 17.3 %scatter_fusion = f32[12,128,512]{2,1,0:T(8,128)} fusion(f32[12,128,512]{2,1,0:T(8,128)} %get-tuple-element.386, s32[27]{0:T(128)S(1)} %fusion.89, f32[27,128,512]{2,1,0:T(8,128)} %copy.49), kind=kCustom, calls=%fused_computation.1.clone.clone.1 | custom fusion | flops 1769472 | bytes 21233772 | tf_op jit(solution)/shard_map/while/body/eval_jaxpr/scatter-add | solution.py:89
  281.8 2.1 convert.7
  284.0 3.6 collective-permute-start.2
  290.9 2.9 collective-permute-done.2
  293.8 4.4 collective-permute-done.3
  298.2 2.5 convert_add_fusion
  300.7 328.9 %all-reduce.30.cloned.1.call-done = f32[64,27,128]{2,1,0:T(8,128)} async-done(((f32[64,27,128]{2,1,0:T(8,128)}), f32[64,27,128]{2,1,0:T(8,128)}) %all-reduce.30.cloned.1.call-update) | async-done | bytes 884752 | tf_op jit(solution)/shard_map/psum | solution.py:109
  (197 shorter events, 49.4 us)
Async XLA Ops:
  8.0 26.9 %copy-start = (bf16[64,27,128]{2,0,1:T(8,128)(2,1)S(1)}, bf16[64,27,128]{2,0,1:T(8,128)(2,1)}, u32[]{:S(2)}) copy-start(bf16[64,27,128]{2,0,1:T(8,128)(2,1)} %param.9) | copy-start | bytes 1327108
  8.0 621.5 %all-reduce.30.cloned.1.call-start = ((), (), s32[]{:S(2)}) async-start(), calls=%async_computation.2 | async-start | bytes 2097152 | tf_op jit(solution)/shard_map/psum | solution.py:109
  21.4 13.8 %copy-start.2 = (bf16[4,128,512]{2,1,0:T(8,128)(2,1)}, bf16[4,128,512]{2,1,0:T(8,128)(2,1)S(1)}, u32[]{:S(2)}) copy-start(bf16[4,128,512]{2,1,0:T(8,128)(2,1)S(1)} %all_gather.3) | copy-start | bytes 1572868
  21.4 13.8 %collective-permute-start.1 = (bf16[4,128,512]{2,1,0:T(8,128)(2,1)S(1)}, bf16[4,128,512]{2,1,0:T(8,128)(2,1)S(1)}, u32[]{:S(2)}, u32[]{:S(2)}) collective-permute-start(bf16[4,128,512]{2,1,0:T(8,128)(2,1)S(1)} %all_gather.3), channel_id=1, source_target_pairs={{4,0},{8,4},{12,8},{16,12},{20,16},{24,20},{28,24},{32,28},{36,32}... | collective-permute-start | bytes 1572872 | tf_op jit(solution)/shard_map/ppermute | solution.py:15
  31.9 8.0 %collective-permute-start = (bf16[4,128,512]{2,1,0:T(8,128)(2,1)S(1)}, bf16[4,128,512]{2,1,0:T(8,128)(2,1)}, u32[]{:S(2)}, u32[]{:S(2)}) collective-permute-start(bf16[4,128,512]{2,1,0:T(8,128)(2,1)S(1)} %all_gather.3), channel_id=1, source_target_pairs={{0,4},{4,8},{8,12},{12,16},{16,20},{20,24},{24,28},{28,32},{32,36}... | collective-permute-start | bytes 1572872 | tf_op jit(solution)/shard_map/ppermute | solution.py:12
  35.3 0.8 copy-start.3
  284.0 9.7 %collective-permute-start.2 = (bf16[4,128,512]{2,1,0:T(8,128)(2,1)S(1)}, bf16[4,128,512]{2,1,0:T(8,128)(2,1)S(1)}, u32[]{:S(2)}, u32[]{:S(2)}) collective-permute-start(bf16[4,128,512]{2,1,0:T(8,128)(2,1)S(1)} %get-tuple-element.238), channel_id=1, source_target_pairs={{0,4},{4,8},{8,12},{12,16},{16,20},{20,24},{24,28},{28,32},{32,36}... | collective-permute-start | bytes 1572872 | tf_op jit(solution)/shard_map/ppermute | solution.py:23
  287.7 10.5 %collective-permute-start.3 = (bf16[4,128,512]{2,1,0:T(8,128)(2,1)S(1)}, bf16[4,128,512]{2,1,0:T(8,128)(2,1)S(1)}, u32[]{:S(2)}, u32[]{:S(2)}) collective-permute-start(bf16[4,128,512]{2,1,0:T(8,128)(2,1)S(1)} %get-tuple-element.239), channel_id=1, source_target_pairs={{4,0},{8,4},{12,8},{16,12},{20,16},{24,20},{28,24},{32,28},{36,32}... | collective-permute-start | bytes 1572872 | tf_op jit(solution)/shard_map/ppermute | solution.py:23
  290.8 341.5 %copy-start.4 = (f32[4,512]{1,0:T(4,128)S(1)}, f32[4,512]{1,0:T(4,128)}, u32[]{:S(2)}) copy-start(f32[4,512]{1,0:T(4,128)} %get-tuple-element.240) | copy-start | bytes 24580
  290.8 343.1 %copy-start.1 = (bf16[64,27,128]{2,0,1:T(8,128)(2,1)S(1)}, bf16[64,27,128]{2,0,1:T(8,128)(2,1)}, u32[]{:S(2)}) copy-start(bf16[64,27,128]{2,0,1:T(8,128)(2,1)} %param.9) | copy-start | bytes 1327108
  290.8 341.5 %reduce-scatter.2.cloned.1.call-start = ((), (), s32[]{:S(2)}) async-start(), calls=%async_computation.1 | async-start | bytes 1310720 | tf_op jit(solution)/shard_map/reduce_scatter | solution.py:107
Sparse Core Ops, SparseCore 0:
  290.9 338.5 all-reduce.29
Sparse Core Ops, SparseCore 1:
  300.7 31.9 reduce-scatter.1
where the time goes:
time: 644 us; the launch traced here: 641 us
  waiting for transfers between devices  340 us (53%)
  other arithmetic  111 us (17%)
  local copies, waits for them, and re-layouts  109 us (17%)
  matrix products  27.6 us (4%)
  starting transfers between devices  18 us (3%)
  between operations  15.6 us (2%)
  blocking collectives  11.1 us (2%)
  loops' own time  8.5 us (1%)
    psum x1, waiting for transfers between devices, on_device(): lax.psum(weight_running_sum.reshape(cout_local, 27, cin), 'space')  329 us
    scatter-add x4, other arithmetic, visit(): grad_cubes = grad_cubes.at[slots].add(pieces)  68.7 us
    gather x8, local copies, waits for them, and re-layouts, visit(): blocks = enlarged_block[slots] * present.astype(jnp.bfloat16)[:, None, None]  33.3 us
    mul x4, local copies, waits for them, and re-layouts, visit(): fold_back(grad_patches, cin) * present.astype(jnp.float32)[:, None, None]  32 us
    another operation x8, local copies, waits for them, and re-layouts, build_patches(): return jnp.stack(pieces).reshape(27 * channels, 512)  16.4 us
    mul x4, other arithmetic, visit(): fold_back(grad_patches, cin) * present.astype(jnp.float32)[:, None, None]  15 us
  transfers between devices with their start and end apart: 6, of which 5 were waited for; matrix products, arithmetic and copies ran while one was open for 1% of the time, Pallas kernels for 0%

commit v1 on v0

v1 whole, which is shorter than its diff:
```python
import functools

import jax
import jax.numpy as jnp
from jax import lax
from jax.experimental import pallas as pl
from jax.experimental.pallas import tpu as pltpu
from jax.sharding import PartitionSpec as P

F32 = jnp.float32
BF16 = jnp.bfloat16
OFFSETS = [(a, b, c) for a in (-1, 0, 1) for b in (-1, 0, 1) for c in (-1, 0, 1)]
NT = (((1,), (1,)), ((), ()))
CUBE = 1616
WIDE = 640
VMEM = pl.BlockSpec(memory_space=pltpu.VMEM)
SMEM = pl.BlockSpec(memory_space=pltpu.SMEM)
PARAMS = pltpu.CompilerParams(vmem_limit_bytes=48 * 1024 * 1024)


def spans(shift):
    if shift < 0:
        return [(0, 7)]
    if shift > 0:
        return [(9, 0)]
    return [(1 + i, i) for i in range(8)]


def fill_cube(slots, block, voxels, cube, base):
    for number, (a, b, c) in enumerate(OFFSETS):
        first = pl.multiple_of(slots[block, number] * 512, 512)
        for i_to, i_from in spans(a):
            if c == 0:
                for j_to, j_from in spans(b):
                    row = base + (i_to * 10 + j_to) * 16 + 8
                    cube[row : row + 8, :] = voxels[pl.ds(first + i_from * 64 + j_from * 8, 8), :]
                continue
            k_from, k_to = (7, 7) if c < 0 else (0, 16)
            if b == 0:
                source = pl.ds(first + i_from * 64 + k_from, 8, stride=8)
                cube[pl.ds(base + (i_to * 10 + 1) * 16 + k_to, 8, stride=16), :] = voxels[source, :]
            else:
                ((j_to, j_from),) = spans(b)
                row = base + (i_to * 10 + j_to) * 16 + k_to
                source = pl.ds(first + i_from * 64 + j_from * 8 + k_from, 1)
                cube[row : row + 1, :] = voxels[source, :]


def pack_patches(cube, base, patches, top):
    for i in range(10):
        for c in range(3):
            rows = [
                cube[base + (i * 10 + j) * 16 + 7 + c : base + (i * 10 + j) * 16 + 15 + c, :]
                for j in range(10)
            ]
            pairs = [
                jnp.concatenate([rows[j], rows[j + 1]], axis=0).astype(BF16) for j in range(9)
            ]
            for b in range(3):
                lanes = (3 * b + c) * 128
                for t in range(4):
                    row = top + i * 64 + t * 16
                    patches[row : row + 16, lanes : lanes + 128] = pairs[2 * t + b]


def stack_weight(weight, stacked):
    out = weight.shape[1]
    for number in range(27):
        a, lanes = number // 9, number % 9 * 128
        stacked[a * out : (a + 1) * out, lanes : lanes + 128] = weight[number]


def forward_kernel(
    blocks, slots, gathered, weight, cotangent, occupancy,
    activation, stacked, grads, tiles,
    voxels, cube, patches,
):
    stack_weight(weight, stacked)
    for slot in range(blocks + 2):
        block = jnp.concatenate([gathered[c, slot] for c in range(gathered.shape[0])], axis=0)
        voxels[slot * 512 : (slot + 1) * 512, :] = block.astype(F32).T
    voxels[(blocks + 2) * 512 : (blocks + 3) * 512, :] = jnp.zeros((512, 128), F32)
    for p in range(blocks):
        fill_cube(slots, p, voxels, cube, p * CUBE)
        pack_patches(cube, p * CUBE, patches, p * WIDE)
        wide = lax.dot_general(
            stacked[...], patches[p * WIDE : (p + 1) * WIDE, :], NT, preferred_element_type=F32
        )
        pre = (
            wide[0:64, 0:512]
            + pltpu.roll(wide[64:128], WIDE - 64, 1)[:, 0:512]
            + wide[128:192, 128:640]
        )
        live = occupancy[p : p + 1, :].astype(F32)
        sigma = jax.nn.sigmoid(pre)
        activation[p] = (pre * sigma * live).astype(BF16)
        slope = sigma * (1.0 + pre * (1.0 - sigma))
        grad = (cotangent[p].astype(F32) * slope * live).astype(BF16).astype(F32)
        grad = jnp.concatenate([grad, jnp.zeros((64, 128), F32)], axis=1)
        lanes = slice(p * WIDE, (p + 1) * WIDE)
        grads[0:64, lanes] = grad.astype(BF16)
        grads[64:128, lanes] = pltpu.roll(grad, 64, 1).astype(BF16)
        grads[128:192, lanes] = pltpu.roll(grad, 128, 1).astype(BF16)
    for first in range(0, 9, 2):
        count = min(2, 9 - first)
        part = jnp.dot(
            grads[...],
            patches[:, first * 128 : (first + count) * 128],
            preferred_element_type=F32,
        )
        for t in range(count):
            for r in range(12):
                corner = part[r * 16 : (r + 1) * 16, t * 128 : (t + 1) * 128]
                tiles[(r // 4 * 9 + first + t) * 4 + r % 4] = corner.astype(BF16)
    for t in range(108, 128):
        tiles[t] = jnp.zeros((16, 128), BF16)


def backward_kernel(
    blocks, slots, stacked, grads, own, rims, sums, wide
):
    sums[...] = jnp.zeros_like(sums)
    row_index = lax.broadcasted_iota(jnp.int32, (64, 128), 0) % 8
    edge = lax.broadcasted_iota(jnp.int32, (8, 128), 0)
    for p in range(blocks):
        turn = grads[:, p * WIDE : (p + 1) * WIDE].astype(F32).T.astype(BF16)
        wide[...] = jnp.dot(turn, stacked[...], preferred_element_type=F32)
        for i in range(10):
            a, i_to = (-1, 7) if i == 0 else ((1, 0) if i == 9 else (0, i - 1))

            def line(j, c):
                total = None
                for b in range(3):
                    if 0 <= j - b < 8:
                        row = i * 64 + (j - b) * 8
                        lanes = (3 * b + c) * 128
                        term = wide[row : row + 8, lanes : lanes + 128]
                        total = term if total is None else total + term
                return total

            for b, js in ((-1, [0]), (0, list(range(1, 9))), (1, [9])):
                before = [pltpu.roll(line(j, 0), 7, 0) for j in js]
                centre = [line(j, 1) for j in js]
                after = [pltpu.roll(line(j, 2), 1, 0) for j in js]
                j_to = 7 if b < 0 else 0
                for c in (-1, 0, 1):
                    if c < 0:
                        parts = [jnp.where(edge == 7, x, 0.0) for x in before]
                    elif c > 0:
                        parts = [jnp.where(edge == 0, x, 0.0) for x in after]
                    else:
                        parts = [
                            y + jnp.where(edge < 7, x, 0.0) + jnp.where(edge > 0, z, 0.0)
                            for x, y, z in zip(before, centre, after)
                        ]
                    part = parts[0] if len(parts) == 1 else jnp.concatenate(parts, axis=0)
                    number = 9 * (a + 1) + 3 * (b + 1) + c + 1
                    first = pl.multiple_of(slots[p, number] * 512, 512)
                    rows = pl.ds(first + i_to * 64 + j_to * 8, 8 * len(js))
                    sums[rows, :] = sums[rows, :] + part
    share = own.shape[2]
    for slot in range(blocks):
        turned = sums[slot * 512 : (slot + 1) * 512, :].T
        for c in range(own.shape[0]):
            own[c, slot] = turned[c * share : (c + 1) * share, :]
    for rim in range(2):
        slot = blocks + rim
        turned = sums[slot * 512 : (slot + 1) * 512, :].T.astype(BF16)
        for c in range(own.shape[0]):
            rims[rim, c] = turned[c * share : (c + 1) * share, :]


def shape(*dims, dtype=BF16):
    return jax.ShapeDtypeStruct(dims, dtype)


def call_forward(slots, gathered, weight, cotangent, occupancy):
    blocks, out = cotangent.shape[:2]
    return pl.pallas_call(
        functools.partial(forward_kernel, blocks),
        out_shape=[
            shape(blocks, out, 512),
            shape(3 * out, 1152),
            shape(3 * out, blocks * WIDE),
            shape(128, 16, 128),
        ],
        in_specs=[SMEM] + [VMEM] * 4,
        out_specs=[VMEM] * 4,
        scratch_shapes=[
            pltpu.VMEM(((blocks + 3) * 512, 128), F32),
            pltpu.VMEM((blocks * CUBE, 128), F32),
            pltpu.VMEM((blocks * WIDE, 1152), BF16),
        ],
        compiler_params=PARAMS,
    )(slots, gathered, weight, cotangent, occupancy)


def call_backward(slots, stacked, grads, chan):
    blocks = slots.shape[0]
    share = 128 // chan
    return pl.pallas_call(
        functools.partial(backward_kernel, blocks),
        out_shape=[shape(chan, blocks, share, 512, dtype=F32), shape(2, chan, share, 512)],
        in_specs=[SMEM, VMEM, VMEM],
        out_specs=[VMEM] * 2,
        scratch_shapes=[
            pltpu.VMEM(((blocks + 3) * 512, 128), F32),
            pltpu.VMEM((WIDE, 1152), F32),
        ],
        compiler_params=PARAMS,
    )(slots, stacked, grads)


def add_kernel(copies, pieces, out):
    total = pieces[0].astype(F32)
    for n in range(1, pieces.shape[0]):
        total = total + pieces[n].astype(F32)
    for n in range(copies):
        out[n] = total.astype(BF16)


def call_add(pieces, copies):
    return pl.pallas_call(
        functools.partial(add_kernel, copies),
        out_shape=shape(copies, *pieces.shape[1:]),
        in_specs=[VMEM],
        out_specs=VMEM,
        compiler_params=PARAMS,
    )(pieces)


def stages_of(count):
    return {128: (4, 16, 2), 4: (2, 1, 2), 8: (2, 2, 2), 16: (2, 4, 2)}[count]


def exchange(pieces, groups):
    return lax.all_to_all(pieces, "space", 0, 0, axis_index_groups=groups)


def on_device(features, occupancy, weight, cotangent, neighbours):
    blocks = features.shape[0]
    out = weight.shape[0]
    space = lax.axis_size("space")
    chan = lax.axis_size("chan")
    columns, rows, cores = stages_of(space)
    place = lax.axis_index("space")
    even = place % 2 == 0

    partner = [(i, i ^ 1) for i in range(space)]
    across = [(i, i - 1 if i % 2 == 0 else i + 1) for i in range(1, space - 1)]
    masked = features * occupancy.astype(BF16)[:, None, :]
    first, last = masked[0], masked[blocks - 1]
    from_partner = lax.ppermute(jnp.where(even, last, first), "space", partner)
    from_across = lax.ppermute(jnp.where(even, first, last), "space", across)
    held = jnp.concatenate([masked, from_partner[None], from_across[None]])
    gathered = lax.all_gather(held, "chan", axis=0)

    ids = jnp.concatenate(
        [
            neighbours[:, :13],
            (place * blocks + jnp.arange(blocks, dtype=jnp.int32))[:, None],
            neighbours[:, 13:],
        ],
        axis=1,
    )
    slots = ids - place * blocks
    below = jnp.where(even, blocks + 1, blocks)
    above = jnp.where(even, blocks, blocks + 1)
    slots = jnp.where(slots == -1, below, jnp.where(slots == blocks, above, slots))
    slots = jnp.where(ids < 0, blocks + 2, slots)

    activation, stacked, grads, tiles = call_forward(
        slots, gathered, jnp.transpose(weight, (1, 0, 2)), cotangent, occupancy
    )

    own, rims = call_backward(slots, stacked, grads, chan)
    to_partner = lax.ppermute(rims[0], "space", partner).astype(F32)
    to_across = lax.ppermute(rims[1], "space", across).astype(F32)
    first = jnp.where(even, to_across, to_partner)
    last = jnp.where(even, to_partner, to_across)
    middle = jnp.zeros((chan, blocks - 2) + first.shape[1:], F32)
    own = own + jnp.concatenate([first[:, None], middle, last[:, None]], axis=1)
    own, tiles = lax.optimization_barrier((own, tiles))
    reduced = lax.psum_scatter(own, "chan", scatter_dimension=0)
    input_grad = (reduced * occupancy.astype(F32)[:, None, :]).astype(BF16)

    near = [
        [(y * rows + z) * cores + c for y in range(columns) for c in range(cores)]
        for z in range(rows)
    ]
    far = [
        [(y * rows + z) * cores + c for z in range(rows)]
        for y in range(columns)
        for c in range(cores)
    ]
    parts = exchange(tiles.reshape(columns * cores, -1, 16, 128), near)
    parts = exchange(call_add(parts, 1).reshape(rows, -1, 16, 128), far)
    total = exchange(call_add(parts, rows), far).reshape(-1, 16, 128)
    total = exchange(jnp.broadcast_to(total, (columns * cores,) + total.shape), near)
    total = total.reshape(128, 16, 128)[:108].astype(F32).reshape(27, out, 128)
    weight_grad = jnp.transpose(total * lax.rsqrt(F32(space * blocks * 512)), (1, 0, 2))
    return (activation, input_grad, weight_grad)


def solution(mesh):
    placed = (
        P("space", "chan", None),
        P("space", None),
        P("chan", None, None),
        P("space", "chan", None),
        P("space", None),
    )
    return jax.shard_map(
        on_device,
        mesh=mesh,
        in_specs=placed,
        out_specs=(P("space", "chan", None), P("space", "chan", None), P("chan", None, None)),
        check_vma=False,
    )
```

time: 644 us -> 130 us (0.20)
  waiting for transfers between devices: 340 us -> 3.7 us
  local copies, waits for them, and re-layouts: 109 us -> 1.59 us
  other arithmetic: 111 us -> 4.9 us
  blocking collectives: 11.1 us -> 79.3 us
  matrix products: 27.6 us -> 0 us
  Pallas kernels: 0 us -> 8.92 us
  loops' own time: 8.5 us -> 0 us
    psum x1 -> x0, waiting for transfers between devices: 329 us -> none  [on_device(): lax.psum(weight_running_sum.reshape(cout_local, 27, cin), 'space')]
    scatter-add x4 -> x0, other arithmetic: 68.7 us -> none  [visit(): grad_cubes = grad_cubes.at[slots].add(pieces)]
    all_to_all x0 -> x4, blocking collectives: none -> 68 us  [exchange(): return lax.all_to_all(pieces, 'space', 0, 0, axis_index_groups=groups)]
    gather x8 -> x0, local copies, waits for them, and re-layouts: 33.3 us -> none  [visit(): blocks = enlarged_block[slots] * present.astype(jnp.bfloat16)[:, None, None]]
    mul x4 -> x0, local copies, waits for them, and re-layouts: 32 us -> none  [visit(): fold_back(grad_patches, cin) * present.astype(jnp.float32)[:, None, None]]
    dot_general x12 -> x0, matrix products: 27.6 us -> none  [the longest x4 10.6 us: visit(): pre_act = jnp.dot(weight_flat, patches, preferred_element_type=jnp.float32)]
    another operation x8 -> x0, local copies, waits for them, and re-layouts: 16.4 us -> none  [build_patches(): return jnp.stack(pieces).reshape(27 * channels, 512)]
    mul x6 -> x2, other arithmetic: 17.2 us -> 1.89 us  [the longest x1 0.97 us: on_device(): total * lax.rsqrt(F32(space * blocks * 512))]
  transfers between devices with their start and end apart: 6 -> 5, of which waited for: 5 -> 3; matrix products, arithmetic and copies ran while one was open for 1% -> 1% of each run, Pallas kernels for 0% -> 0%
where the time goes in v1:
time: 130 us
  blocking collectives  79.3 us (61%)
  starting transfers between devices  17 us (13%)
  between operations  14.2 us (11%)
  Pallas kernels  8.92 us (7%)
  other arithmetic  4.9 us (4%)
  waiting for transfers between devices  3.7 us (3%)
  local copies, waits for them, and re-layouts  1.59 us (1%)
    all_to_all x4, blocking collectives, exchange(): return lax.all_to_all(pieces, 'space', 0, 0, axis_index_groups=groups)  68 us
    all_gather x1, blocking collectives, on_device(): gathered = lax.all_gather(held, 'chan', axis=0)  11.3 us
    ppermute x1, starting transfers between devices, on_device(): from_partner = lax.ppermute(jnp.where(even, last, first), 'space', partner)  8.79 us
    pallas_call x1, Pallas kernels, call_forward(): pl.pallas_call(functools.partial(forward_kernel, blocks), out_shape=[shap...  4.94 us
    ppermute x1, starting transfers between devices, on_device(): to_across = lax.ppermute(rims[1], 'space', across).astype(F32)  4.38 us
    pallas_call x1, Pallas kernels, call_backward(): pl.pallas_call(functools.partial(backward_kernel, blocks), out_shape=[sha...  3.89 us
  transfers between devices with their start and end apart: 5, of which 3 were waited for; matrix products, arithmetic and copies ran while one was open for 1% of the time, Pallas kernels for 0%

profile of v1, /device:TPU:1, one launch (start us, length us, event | category | flops | bytes accessed | tf_op | source)
XLA Modules:
  0.0 129.6 jit_solution(13896358387656933911)
XLA Ops:
  7.2 0.0 reduce-scatter.2.cloned.1.call-start
  7.2 0.0 copy-start.2
  7.2 0.7 copy-done.2
  7.9 0.9 broadcast_multiply_fusion
  8.9 8.8 %collective-permute-start = (bf16[32,512]{1,0:T(8,128)(2,1)S(1)}, bf16[32,512]{1,0:T(8,128)(2,1)S(1)}, u32[]{:S(2)}, u32[]{:S(2)}) collective-permute-start(bf16[32,512]{1,0:T(8,128)(2,1)S(1)} %get-tuple-element.23), channel_id=1, source_target_pairs={{0,4},{4,0},{8,12},{12,8},{16,20},{20,16},{24,28},{28,24},{32,36},... | collective-permute-start | bytes 98312 | tf_op jit(solution)/shard_map/ppermute | solution.py:253
  17.7 1.9 %collective-permute-start.1 = (bf16[32,512]{1,0:T(8,128)(2,1)S(1)}, bf16[32,512]{1,0:T(8,128)(2,1)S(1)}, u32[]{:S(2)}, u32[]{:S(2)}) collective-permute-start(bf16[32,512]{1,0:T(8,128)(2,1)S(1)} %get-tuple-element.24), channel_id=1, source_target_pairs={{4,8},{8,4},{12,16},{16,12},{20,24},{24,20},{28,32},{32,28},{36,40... | collective-permute-start | bytes 98312 | tf_op jit(solution)/shard_map/ppermute | solution.py:254
  19.6 0.0 copy-start.3
  19.6 0.7 copy-done.3
  20.3 0.1 fusion.6
  20.3 0.1 fusion.4.slots
  20.4 0.0 collective-permute-done
  20.4 2.5 %collective-permute-done.1 = bf16[32,512]{1,0:T(8,128)(2,1)S(1)} collective-permute-done((bf16[32,512]{1,0:T(8,128)(2,1)S(1)}, bf16[32,512]{1,0:T(8,128)(2,1)S(1)}, u32[]{:S(2)}, u32[]{:S(2)}) %collective-permute-start.1) | collective-permute-done | bytes 32800 | tf_op jit(solution)/shard_map/ppermute | solution.py:254
  22.9 0.0 copy-start
  22.9 0.0 copy-start.1
  22.9 11.3 %all-gather = bf16[24,32,512]{2,1,0:T(8,128)(2,1)S(1)} all-gather(bf16[6,32,512]{2,1,0:T(8,128)(2,1)S(1)} %pad_maximum_fusion), channel_id=2, replica_groups=mesh['space'=128,'chan'=4] {'chan'}, dimensions={0}, use_global_device_ids=true | all-gather | bytes 983040 | tf_op jit(solution)/shard_map/all_gather | solution.py:256
  34.2 0.0 copy-done
  34.2 0.0 copy-done.1
  34.3 4.9 %shard_map.76 = (bf16[4,64,512]{2,1,0:T(8,128)(2,1)}, bf16[192,1152]{1,0:T(8,128)(2,1)S(1)}, bf16[192,2560]{1,0:T(8,128)(2,1)S(1)}, bf16[128,16,128]{2,1,0:T(8,128)(2,1)S(1)}) custom-call(s32[4,27]{1,0:T(4,128)S(1)} %fusion.4.slots, bf16[4,6,32,512]{3,2,1,0:T(8,128)(2,1)S(1)} %bitcast.31, bf16[27,64,128]{2,1,0:T(8,128)(2,1)S(1)} %bitcast.33, ...), custom_call_target="tpu_custom_call" | custom-call | tf_op jit(solution)/shard_map/pallas_call | solution.py:179
  39.2 3.9 %shard_map.77 = (f32[4,4,32,512]{3,2,1,0:T(8,128)S(1)}, bf16[2,4,32,512]{3,2,1,0:T(8,128)(2,1)S(1)}) custom-call(s32[4,27]{1,0:T(4,128)S(1)} %fusion.4.slots, bf16[192,1152]{1,0:T(8,128)(2,1)S(1)} %get-tuple-element.12.stacked, bf16[192,2560]{1,0:T(8,128)(2,1)S(1)} %get-tuple-element.13.grads), custom_call_target="tpu_custom_call" | custom-call | tf_op jit(solution)/shard_map/pallas_call | solution.py:201
  43.1 4.4 %collective-permute-start.2 = (bf16[4,32,512]{2,1,0:T(8,128)(2,1)S(1)}, bf16[4,32,512]{2,1,0:T(8,128)(2,1)S(1)}, u32[]{:S(2)}, u32[]{:S(2)}) collective-permute-start(bf16[4,32,512]{2,1,0:T(8,128)(2,1)S(1)} %get-tuple-element.22), channel_id=1, source_target_pairs={{4,8},{8,4},{12,16},{16,12},{20,24},{24,20},{28,32},{32,28},{36,40... | collective-permute-start | bytes 393224 | tf_op jit(solution)/shard_map/ppermute | solution.py:278
  47.5 1.9 %collective-permute-start.3 = (bf16[4,32,512]{2,1,0:T(8,128)(2,1)S(1)}, bf16[4,32,512]{2,1,0:T(8,128)(2,1)S(1)}, u32[]{:S(2)}, u32[]{:S(2)}) collective-permute-start(bf16[4,32,512]{2,1,0:T(8,128)(2,1)S(1)} %get-tuple-element.21), channel_id=1, source_target_pairs={{0,4},{4,0},{8,12},{12,8},{16,20},{20,16},{24,28},{28,24},{32,36},... | collective-permute-start | bytes 393224 | tf_op jit(solution)/shard_map/ppermute | solution.py:277
  49.5 0.1 pad.1.clone
  49.5 0.6 collective-permute-done.2
  50.2 0.6 collective-permute-done.3
  50.8 0.1 fusion
  50.8 1.2 maximum_add_fusion
  52.0 0.0 reduce-scatter.2.cloned.1.call-update
  52.0 19.3 %all_to_all.20.pieces = bf16[8,16,16,128]{3,2,1,0:T(8,128)(2,1)S(1)} all-to-all(bf16[8,16,16,128]{3,2,1,0:T(8,128)(2,1)S(1)} %bitcast.32), channel_id=1, replica_groups={{0,4,128,132,256,260,384,388},{8,12,136,140,264,268,392,396},{16,20,144..., dimensions={0} | all-to-all | bytes 1048576 | tf_op jit(solution)/shard_map/all_to_all | solution.py:237
  71.4 0.1 shard_map.78
  71.4 18.8 %all_to_all.21.pieces = bf16[16,1,16,128]{3,2,1,0:T(8,128)(2,1)S(1)} all-to-all(bf16[16,1,16,128]{3,2,1,0:T(8,128)(2,1)S(1)} %bitcast.34), channel_id=1, replica_groups={{0,8,16,24,32,40,48,56,64,72,80,88,96,104,112,120},{4,12,20,28,36,44,52..., dimensions={0} | all-to-all | bytes 131072 | tf_op jit(solution)/shard_map/all_to_all | solution.py:237
  90.3 14.5 %all_to_all.22 = bf16[16,1,16,128]{3,2,1,0:T(8,128)(2,1)S(1)} all-to-all(bf16[16,1,16,128]{3,2,1,0:T(8,128)(2,1)S(1)} %shard_map.79), channel_id=1, replica_groups={{0,8,16,24,32,40,48,56,64,72,80,88,96,104,112,120},{4,12,20,28,36,44,52..., dimensions={0} | all-to-all | bytes 131072 | tf_op jit(solution)/shard_map/all_to_all | solution.py:237
  104.7 0.1 broadcast_in_dim.40
  104.8 15.4 %all_to_all.23 = bf16[8,16,16,128]{3,2,1,0:T(8,128)(2,1)S(1)} all-to-all(bf16[8,16,16,128]{3,2,1,0:T(8,128)(2,1)S(1)} %broadcast_in_dim.40), channel_id=1, replica_groups={{0,4,128,132,256,260,384,388},{8,12,136,140,264,268,392,396},{16,20,144..., dimensions={0} | all-to-all | bytes 1048576 | tf_op jit(solution)/shard_map/all_to_all | solution.py:237
  120.2 1.0 convert_multiply_fusion
  121.2 0.0 reduce-scatter.2.cloned.1.call-done
  121.2 1.6 %fusion.2 = bf16[4,32,512]{2,1,0:T(8,128)(2,1)} fusion(f32[1,4,32,512]{3,2,1,0:T(8,128)} %reduce-scatter.2.cloned.1.call-done, f32[4,512]{1,0:T(4,128)S(1)} %get-tuple-element.25), kind=kLoop, calls=%fused_computation.7 | loop fusion | flops 131072 | bytes 401408 | tf_op jit(solution)/shard_map/convert_element_type | solution.py:285
  (7 shorter events, 0.1 us)
Async XLA Ops:
  7.2 114.0 %reduce-scatter.2.cloned.1.call-start = ((), (), s32[]{:S(2)}) async-start(), calls=%async_computation.5 | async-start | bytes 1310720 | tf_op jit(solution)/shard_map/reduce_scatter | solution.py:284
  7.2 0.7 copy-start.2
  8.9 11.6 %collective-permute-start = (bf16[32,512]{1,0:T(8,128)(2,1)S(1)}, bf16[32,512]{1,0:T(8,128)(2,1)S(1)}, u32[]{:S(2)}, u32[]{:S(2)}) collective-permute-start(bf16[32,512]{1,0:T(8,128)(2,1)S(1)} %get-tuple-element.23), channel_id=1, source_target_pairs={{0,4},{4,0},{8,12},{12,8},{16,20},{20,16},{24,28},{28,24},{32,36},... | collective-permute-start | bytes 98312 | tf_op jit(solution)/shard_map/ppermute | solution.py:253
  17.7 5.2 %collective-permute-start.1 = (bf16[32,512]{1,0:T(8,128)(2,1)S(1)}, bf16[32,512]{1,0:T(8,128)(2,1)S(1)}, u32[]{:S(2)}, u32[]{:S(2)}) collective-permute-start(bf16[32,512]{1,0:T(8,128)(2,1)S(1)} %get-tuple-element.24), channel_id=1, source_target_pairs={{4,8},{8,4},{12,16},{16,12},{20,24},{24,20},{28,32},{32,28},{36,40... | collective-permute-start | bytes 98312 | tf_op jit(solution)/shard_map/ppermute | solution.py:254
  19.6 0.7 copy-start.3
  22.9 11.3 %copy-start = (bf16[64,27,128]{2,0,1:T(8,128)(2,1)S(1)}, bf16[64,27,128]{2,0,1:T(8,128)(2,1)}, u32[]{:S(2)}) copy-start(bf16[64,27,128]{2,0,1:T(8,128)(2,1)} %param.7) | copy-start | bytes 1327108
  22.9 11.3 %copy-start.1 = (bf16[4,64,512]{2,1,0:T(8,128)(2,1)S(1)}, bf16[4,64,512]{2,1,0:T(8,128)(2,1)}, u32[]{:S(2)}) copy-start(bf16[4,64,512]{2,1,0:T(8,128)(2,1)} %cotangent.1) | copy-start | bytes 786436
  43.1 7.0 %collective-permute-start.2 = (bf16[4,32,512]{2,1,0:T(8,128)(2,1)S(1)}, bf16[4,32,512]{2,1,0:T(8,128)(2,1)S(1)}, u32[]{:S(2)}, u32[]{:S(2)}) collective-permute-start(bf16[4,32,512]{2,1,0:T(8,128)(2,1)S(1)} %get-tuple-element.22), channel_id=1, source_target_pairs={{4,8},{8,4},{12,16},{16,12},{20,24},{24,20},{28,32},{32,28},{36,40... | collective-permute-start | bytes 393224 | tf_op jit(solution)/shard_map/ppermute | solution.py:278
  47.5 3.2 %collective-permute-start.3 = (bf16[4,32,512]{2,1,0:T(8,128)(2,1)S(1)}, bf16[4,32,512]{2,1,0:T(8,128)(2,1)S(1)}, u32[]{:S(2)}, u32[]{:S(2)}) collective-permute-start(bf16[4,32,512]{2,1,0:T(8,128)(2,1)S(1)} %get-tuple-element.21), channel_id=1, source_target_pairs={{0,4},{4,0},{8,12},{12,8},{16,20},{20,16},{24,28},{28,24},{32,36},... | collective-permute-start | bytes 393224 | tf_op jit(solution)/shard_map/ppermute | solution.py:277
Sparse Core Ops, SparseCore 0:
  52.2 32.1 reduce-scatter.1

commit v2 on v1

--- a/solution.py
+++ b/solution.py
@@ -112,12 +112,12 @@
             for r in range(12):
                 corner = part[r * 16 : (r + 1) * 16, t * 128 : (t + 1) * 128]
                 tiles[(r // 4 * 9 + first + t) * 4 + r % 4] = corner.astype(BF16)
-    for t in range(108, 128):
+    for t in range(108, tiles.shape[0]):
         tiles[t] = jnp.zeros((16, 128), BF16)
 
 
 def backward_kernel(
-    blocks, slots, stacked, grads, own, rims, sums, wide
+    blocks, slots, stacked, grads, pieces, sums, wide
 ):
     sums[...] = jnp.zeros_like(sums)
     row_index = lax.broadcasted_iota(jnp.int32, (64, 128), 0) % 8
@@ -158,23 +158,18 @@
                     first = pl.multiple_of(slots[p, number] * 512, 512)
                     rows = pl.ds(first + i_to * 64 + j_to * 8, 8 * len(js))
                     sums[rows, :] = sums[rows, :] + part
-    share = own.shape[2]
-    for slot in range(blocks):
-        turned = sums[slot * 512 : (slot + 1) * 512, :].T
-        for c in range(own.shape[0]):
-            own[c, slot] = turned[c * share : (c + 1) * share, :]
-    for rim in range(2):
-        slot = blocks + rim
+    share = pieces.shape[2]
+    for slot in range(blocks + 2):
         turned = sums[slot * 512 : (slot + 1) * 512, :].T.astype(BF16)
-        for c in range(own.shape[0]):
-            rims[rim, c] = turned[c * share : (c + 1) * share, :]
+        for c in range(pieces.shape[0]):
+            pieces[c, slot] = turned[c * share : (c + 1) * share, :]
 
 
 def shape(*dims, dtype=BF16):
     return jax.ShapeDtypeStruct(dims, dtype)
 
 
-def call_forward(slots, gathered, weight, cotangent, occupancy):
+def call_forward(slots, gathered, weight, cotangent, occupancy, tiles):
     blocks, out = cotangent.shape[:2]
     return pl.pallas_call(
         functools.partial(forward_kernel, blocks),
@@ -182,7 +177,7 @@
             shape(blocks, out, 512),
             shape(3 * out, 1152),
             shape(3 * out, blocks * WIDE),
-            shape(128, 16, 128),
+            shape(tiles, 16, 128),
         ],
         in_specs=[SMEM] + [VMEM] * 4,
         out_specs=[VMEM] * 4,
@@ -200,9 +195,9 @@
     share = 128 // chan
     return pl.pallas_call(
         functools.partial(backward_kernel, blocks),
-        out_shape=[shape(chan, blocks, share, 512, dtype=F32), shape(2, chan, share, 512)],
+        out_shape=shape(chan, blocks + 2, share, 512),
         in_specs=[SMEM, VMEM, VMEM],
-        out_specs=[VMEM] * 2,
+        out_specs=VMEM,
         scratch_shapes=[
             pltpu.VMEM(((blocks + 3) * 512, 128), F32),
             pltpu.VMEM((WIDE, 1152), F32),
@@ -229,12 +224,67 @@
     )(pieces)
 
 
+def sum_kernel(blocks, pieces, own, to_partner, to_across):
+    for slot in range(blocks + 2):
+        total = pieces[0, slot].astype(F32)
+        for c in range(1, pieces.shape[0]):
+            total = total + pieces[c, slot].astype(F32)
+        if slot < blocks:
+            own[slot] = total
+        else:
+            (to_partner if slot == blocks else to_across)[...] = total.astype(BF16)
+
+
+def call_sum(pieces):
+    blocks, rim = pieces.shape[1] - 2, pieces.shape[2:]
+    return pl.pallas_call(
+        functools.partial(sum_kernel, blocks),
+        out_shape=[shape(blocks, *rim, dtype=F32), shape(*rim), shape(*rim)],
+        in_specs=[VMEM],
+        out_specs=[VMEM] * 3,
+        compiler_params=PARAMS,
+    )(pieces)
+
+
+def final_kernel(even, own, from_partner, from_across, occupancy, out):
+    blocks = own.shape[0]
+    is_even = even[0] == 1
+    partner, across = from_partner[...].astype(F32), from_across[...].astype(F32)
+    for slot in range(blocks):
+        total = own[slot]
+        if slot == 0:
+            total = total + jnp.where(is_even, across, partner)
+        if slot == blocks - 1:
+            total = total + jnp.where(is_even, partner, across)
+        out[slot] = (total * occupancy[slot : slot + 1, :].astype(F32)).astype(BF16)
+
+
+def call_final(even, own, from_partner, from_across, occupancy):
+    return pl.pallas_call(
+        final_kernel,
+        out_shape=shape(*own.shape),
+        in_specs=[SMEM] + [VMEM] * 4,
+        out_specs=VMEM,
+        compiler_params=PARAMS,
+    )(even.astype(jnp.int32).reshape(1), own, from_partner, from_across, occupancy)
+
+
 def stages_of(count):
     return {128: (4, 16, 2), 4: (2, 1, 2), 8: (2, 2, 2), 16: (2, 4, 2)}[count]
 
 
 def exchange(pieces, groups):
     return lax.all_to_all(pieces, "space", 0, 0, axis_index_groups=groups)
+
+
+def groups_of(space):
+    columns, rows, cores = stages_of(space)
+    near, far = {}, {}
+    for index in range(space):
+        y, z, core = index // (rows * cores), index // cores % rows, index % cores
+        near.setdefault(z // 2, []).append(index)
+        far.setdefault((y, core, z % 2), []).append(index)
+    return list(near.values()), list(far.values())
 
 
 def on_device(features, occupancy, weight, cotangent, neighbours):
@@ -242,7 +292,8 @@
     out = weight.shape[0]
     space = lax.axis_size("space")
     chan = lax.axis_size("chan")
-    columns, rows, cores = stages_of(space)
+    near, far = groups_of(space)
+    share = -(-108 // len(near[0]))
     place = lax.axis_index("space")
     even = place % 2 == 0
 
@@ -270,35 +321,24 @@
     slots = jnp.where(ids < 0, blocks + 2, slots)
 
     activation, stacked, grads, tiles = call_forward(
-        slots, gathered, jnp.transpose(weight, (1, 0, 2)), cotangent, occupancy
+        slots, gathered, jnp.transpose(weight, (1, 0, 2)), cotangent, occupancy,
+        len(near[0]) * share,
     )
 
-    own, rims = call_backward(slots, stacked, grads, chan)
-    to_partner = lax.ppermute(rims[0], "space", partner).astype(F32)
-    to_across = lax.ppermute(rims[1], "space", across).astype(F32)
-    first = jnp.where(even, to_across, to_partner)
-    last = jnp.where(even, to_partner, to_across)
-    middle = jnp.zeros((chan, blocks - 2) + first.shape[1:], F32)
-    own = own + jnp.concatenate([first[:, None], middle, last[:, None]], axis=1)
-    own, tiles = lax.optimization_barrier((own, tiles))
-    reduced = lax.psum_scatter(own, "chan", scatter_dimension=0)
-    input_grad = (reduced * occupancy.astype(F32)[:, None, :]).astype(BF16)
-
-    near = [
-        [(y * rows + z) * cores + c for y in range(columns) for c in range(cores)]
-        for z in range(rows)
-    ]
-    far = [
-        [(y * rows + z) * cores + c for z in range(rows)]
-        for y in range(columns)
-        for c in range(cores)
-    ]
-    parts = exchange(tiles.reshape(columns * cores, -1, 16, 128), near)
-    parts = exchange(call_add(parts, 1).reshape(rows, -1, 16, 128), far)
-    total = exchange(call_add(parts, rows), far).reshape(-1, 16, 128)
-    total = exchange(jnp.broadcast_to(total, (columns * cores,) + total.shape), near)
-    total = total.reshape(128, 16, 128)[:108].astype(F32).reshape(27, out, 128)
+    pieces = call_backward(slots, stacked, grads, chan)
+    own, rim_partner, rim_across = call_sum(lax.all_to_all(pieces, "chan", 0, 0))
+    rim_partner, rim_across, tiles = lax.optimization_barrier((rim_partner, rim_across, tiles))
+    to_partner = lax.ppermute(rim_partner, "space", partner)
+    to_across = lax.ppermute(rim_across, "space", across)
+
+    parts = exchange(tiles.reshape(len(near[0]), share, 16, 128), near)
+    to_partner, to_across, parts = lax.optimization_barrier((to_partner, to_across, parts))
+    parts = exchange(call_add(parts, len(far[0])), far)
+    total = exchange(call_add(parts, len(near[0])), near)
+    total = total.reshape(-1, 16, 128)[:108].astype(F32).reshape(27, out, 128)
     weight_grad = jnp.transpose(total * lax.rsqrt(F32(space * blocks * 512)), (1, 0, 2))
+
+    input_grad = call_final(even, own, to_partner, to_across, occupancy)
     return (activation, input_grad, weight_grad)
 
 

time: 130 us -> 116 us (0.89)
  blocking collectives: 79.3 us -> 52.3 us
  starting transfers between devices: 17 us -> 33.1 us
  between operations: 14.2 us -> 0.77 us
  waiting for transfers between devices: 3.7 us -> 14.4 us
  other arithmetic: 4.9 us -> 2.01 us
  Pallas kernels: 8.92 us -> 11 us
    all_to_all x4 -> x1, blocking collectives: 68 us -> 26.9 us  [exchange(): return lax.all_to_all(pieces, 'space', 0, 0, axis_index_groups=groups)]
    all_to_all x0 -> x2, starting transfers between devices: none -> 16.8 us  [exchange(): return lax.all_to_all(pieces, 'space', 0, 0, axis_index_groups=groups)]
    all_to_all x0 -> x1, blocking collectives: none -> 14.1 us  [on_device(): lax.all_to_all(pieces, 'chan', 0, 0)]
    all_to_all x0 -> x2, waiting for transfers between devices: none -> 9.74 us  [exchange(): return lax.all_to_all(pieces, 'space', 0, 0, axis_index_groups=groups)]
    convert_element_type x2 -> x1, other arithmetic: 1.63 us -> 0.01 us  [on_device(): masked = features * occupancy.astype(BF16)[:, None, :]]
    pallas_call x1 -> x3, Pallas kernels: 3.89 us -> 4.45 us  [the longest x1 3.67 us: call_backward(): pl.pallas_call(functools.partial(backward_kernel, blocks), out_shape=shap...]
  transfers between devices with their start and end apart: 5 -> 6, of which waited for: 3 -> 4; matrix products, arithmetic and copies ran while one was open for 1% -> 0% of each run, Pallas kernels for 0% -> 1%
where the time goes in v2:
time: 116 us; the launch traced here: 115 us
  blocking collectives  52.3 us (45%)
  starting transfers between devices  33.1 us (29%)
  waiting for transfers between devices  14.4 us (12%)
  Pallas kernels  11 us (9%)
  other arithmetic  2.01 us (2%)
  local copies, waits for them, and re-layouts  1.43 us (1%)
    all_to_all x1, blocking collectives, exchange(): return lax.all_to_all(pieces, 'space', 0, 0, axis_index_groups=groups)  26.9 us
    all_to_all x2, starting transfers between devices, exchange(): return lax.all_to_all(pieces, 'space', 0, 0, axis_index_groups=groups)  16.8 us
    all_to_all x1, blocking collectives, on_device(): lax.all_to_all(pieces, 'chan', 0, 0)  14.1 us
    all_gather x1, blocking collectives, on_device(): gathered = lax.all_gather(held, 'chan', axis=0)  11.3 us
    all_to_all x2, waiting for transfers between devices, exchange(): return lax.all_to_all(pieces, 'space', 0, 0, axis_index_groups=groups)  9.74 us
    ppermute x1, starting transfers between devices, on_device(): from_partner = lax.ppermute(jnp.where(even, last, first), 'space', partner)  8.79 us
    pallas_call x1, Pallas kernels, call_forward(): pl.pallas_call(functools.partial(forward_kernel, blocks), out_shape=[shap...  5.71 us
    pallas_call x1, Pallas kernels, call_backward(): pl.pallas_call(functools.partial(backward_kernel, blocks), out_shape=shap...  3.67 us
  transfers between devices with their start and end apart: 6, of which 4 were waited for; matrix products, arithmetic and copies ran while one was open for 0% of the time, Pallas kernels for 1%

profile of v2, /device:TPU:1, one launch (start us, length us, event | category | flops | bytes accessed | tf_op | source)
XLA Modules:
  0.0 115.1 jit_solution(9684490390073668987)
XLA Ops:
  0.6 0.0 copy-start.2
  0.7 0.7 copy-done.2
  1.3 0.9 broadcast_multiply_fusion
  2.3 8.8 %collective-permute-start = (bf16[32,512]{1,0:T(8,128)(2,1)S(1)}, bf16[32,512]{1,0:T(8,128)(2,1)S(1)}, u32[]{:S(2)}, u32[]{:S(2)}) collective-permute-start(bf16[32,512]{1,0:T(8,128)(2,1)S(1)} %get-tuple-element.29), channel_id=1, source_target_pairs={{0,4},{4,0},{8,12},{12,8},{16,20},{20,16},{24,28},{28,24},{32,36},... | collective-permute-start | bytes 98312 | tf_op jit(solution)/shard_map/ppermute | solution.py:304
  11.1 1.9 %collective-permute-start.1 = (bf16[32,512]{1,0:T(8,128)(2,1)S(1)}, bf16[32,512]{1,0:T(8,128)(2,1)S(1)}, u32[]{:S(2)}, u32[]{:S(2)}) collective-permute-start(bf16[32,512]{1,0:T(8,128)(2,1)S(1)} %get-tuple-element.30), channel_id=1, source_target_pairs={{4,8},{8,4},{12,16},{16,12},{20,24},{24,20},{28,32},{32,28},{36,40... | collective-permute-start | bytes 98312 | tf_op jit(solution)/shard_map/ppermute | solution.py:305
  13.0 0.0 copy-start.3
  13.0 0.7 copy-done.3
  13.7 0.1 fusion.2
  13.8 0.1 fusion.1.slots
  13.8 0.0 collective-permute-done
  13.8 2.5 %collective-permute-done.1 = bf16[32,512]{1,0:T(8,128)(2,1)S(1)} collective-permute-done((bf16[32,512]{1,0:T(8,128)(2,1)S(1)}, bf16[32,512]{1,0:T(8,128)(2,1)S(1)}, u32[]{:S(2)}, u32[]{:S(2)}) %collective-permute-start.1) | collective-permute-done | bytes 32800 | tf_op jit(solution)/shard_map/ppermute | solution.py:305
  16.3 0.0 copy-start
  16.3 0.0 copy-start.1
  16.4 11.3 %all-gather = bf16[24,32,512]{2,1,0:T(8,128)(2,1)S(1)} all-gather(bf16[6,32,512]{2,1,0:T(8,128)(2,1)S(1)} %pad_maximum_fusion), channel_id=2, replica_groups=mesh['space'=128,'chan'=4] {'chan'}, dimensions={0}, use_global_device_ids=true | all-gather | bytes 983040 | tf_op jit(solution)/shard_map/all_gather | solution.py:307
  27.7 0.0 copy-done
  27.7 0.0 copy-done.1
  27.7 5.7 %shard_map.76 = (bf16[4,64,512]{2,1,0:T(8,128)(2,1)}, bf16[192,1152]{1,0:T(8,128)(2,1)S(1)}, bf16[192,2560]{1,0:T(8,128)(2,1)S(1)}, bf16[112,16,128]{2,1,0:T(8,128)(2,1)}) custom-call(s32[4,27]{1,0:T(4,128)S(1)} %fusion.1.slots, bf16[4,6,32,512]{3,2,1,0:T(8,128)(2,1)S(1)} %bitcast.14, bf16[27,64,128]{2,1,0:T(8,128)(2,1)S(1)} %bitcast.15, ...), custom_call_target="tpu_custom_call" | custom-call | tf_op jit(solution)/shard_map/pallas_call | solution.py:174
  33.4 3.7 %shard_map.77 = bf16[4,6,32,512]{3,2,1,0:T(8,128)(2,1)S(1)} custom-call(s32[4,27]{1,0:T(4,128)S(1)} %fusion.1.slots, bf16[192,1152]{1,0:T(8,128)(2,1)S(1)} %get-tuple-element.17.stacked, bf16[192,2560]{1,0:T(8,128)(2,1)S(1)} %get-tuple-element.18.grads), custom_call_target="tpu_custom_call" | custom-call | tf_op jit(solution)/shard_map/pallas_call | solution.py:196
  37.1 14.1 %all_to_all.20.pieces = bf16[4,6,32,512]{3,2,1,0:T(8,128)(2,1)S(1)} all-to-all(bf16[4,6,32,512]{3,2,1,0:T(8,128)(2,1)S(1)} %shard_map.77), channel_id=1, replica_groups=mesh['space'=128,'chan'=4] {'chan'}, dimensions={0} | all-to-all | bytes 1572864 | tf_op jit(solution)/shard_map/all_to_all | solution.py:329
  51.1 0.1 shard_map.78
  51.2 8.4 %all-to-all-start.1 = ((bf16[16,7,16,128]{3,2,1,0:T(8,128)(2,1)}), bf16[16,7,16,128]{3,2,1,0:T(8,128)(2,1)S(1)}, u32[]{:S(2)}, u32[]{:S(2)}) async-start(bf16[16,7,16,128]{3,2,1,0:T(8,128)(2,1)} %bitcast.7), calls=%async_computation.1 | async-start | bytes 917504 | tf_op jit(solution)/shard_map/all_to_all | solution.py:277
  59.6 2.0 %collective-permute-start.2 = (bf16[32,512]{1,0:T(8,128)(2,1)S(1)}, bf16[32,512]{1,0:T(8,128)(2,1)S(1)}, u32[]{:S(2)}, u32[]{:S(2)}) collective-permute-start(bf16[32,512]{1,0:T(8,128)(2,1)S(1)} %get-tuple-element.23), channel_id=1, source_target_pairs={{0,4},{4,0},{8,12},{12,8},{16,20},{20,16},{24,28},{28,24},{32,36},... | collective-permute-start | bytes 98312 | tf_op jit(solution)/shard_map/ppermute | solution.py:331
  61.6 3.6 %collective-permute-start.3 = (bf16[32,512]{1,0:T(8,128)(2,1)S(1)}, bf16[32,512]{1,0:T(8,128)(2,1)S(1)}, u32[]{:S(2)}, u32[]{:S(2)}) collective-permute-start(bf16[32,512]{1,0:T(8,128)(2,1)S(1)} %get-tuple-element.24), channel_id=1, source_target_pairs={{4,8},{8,4},{12,16},{16,12},{20,24},{24,20},{28,32},{32,28},{36,40... | collective-permute-start | bytes 98312 | tf_op jit(solution)/shard_map/ppermute | solution.py:332
  65.2 0.0 collective-permute-done.2.from_partner
  65.2 2.2 %collective-permute-done.3.from_across = bf16[32,512]{1,0:T(8,128)(2,1)S(1)} collective-permute-done((bf16[32,512]{1,0:T(8,128)(2,1)S(1)}, bf16[32,512]{1,0:T(8,128)(2,1)S(1)}, u32[]{:S(2)}, u32[]{:S(2)}) %collective-permute-start.3) | collective-permute-done | bytes 32800 | tf_op jit(solution)/shard_map/ppermute | solution.py:332
  67.4 1.3 %all-to-all-done.1.pieces = bf16[16,7,16,128]{3,2,1,0:T(8,128)(2,1)S(1)} async-done(((bf16[16,7,16,128]{3,2,1,0:T(8,128)(2,1)}), bf16[16,7,16,128]{3,2,1,0:T(8,128)(2,1)S(1)}, u32[]{:S(2)}, u32[]{:S(2)}) %all-to-all-start.1) | async-done | bytes 458784 | tf_op jit(solution)/shard_map/all_to_all | solution.py:277
  68.7 0.1 shard_map.80
  68.8 26.9 %all_to_all.21.pieces = bf16[8,7,16,128]{3,2,1,0:T(8,128)(2,1)S(1)} all-to-all(bf16[8,7,16,128]{3,2,1,0:T(8,128)(2,1)S(1)} %shard_map.80), channel_id=1, replica_groups={{0,16,32,48,64,80,96,112},{4,20,36,52,68,84,100,116},{8,24,40,56,72,88,..., dimensions={0} | all-to-all | bytes 458752 | tf_op jit(solution)/shard_map/all_to_all | solution.py:277
  95.7 0.8 shard_map.81
  96.5 8.4 %all-to-all-start.3 = ((bf16[16,7,16,128]{3,2,1,0:T(8,128)(2,1)}), bf16[16,7,16,128]{3,2,1,0:T(8,128)(2,1)S(1)}, u32[]{:S(2)}, u32[]{:S(2)}) async-start(bf16[16,7,16,128]{3,2,1,0:T(8,128)(2,1)} %shard_map.81), calls=%async_computation.3 | async-start | bytes 917504 | tf_op jit(solution)/shard_map/all_to_all | solution.py:277
  104.9 0.7 shard_map.79
  105.6 8.5 %all-to-all-done.3 = bf16[16,7,16,128]{3,2,1,0:T(8,128)(2,1)S(1)} async-done(((bf16[16,7,16,128]{3,2,1,0:T(8,128)(2,1)}), bf16[16,7,16,128]{3,2,1,0:T(8,128)(2,1)S(1)}, u32[]{:S(2)}, u32[]{:S(2)}) %all-to-all-start.3) | async-done | bytes 458784 | tf_op jit(solution)/shard_map/all_to_all | solution.py:277
  114.1 1.0 convert_multiply_fusion
  (4 shorter events, 0.0 us)
Async XLA Ops:
  0.6 0.7 copy-start.2
  2.3 11.6 %collective-permute-start = (bf16[32,512]{1,0:T(8,128)(2,1)S(1)}, bf16[32,512]{1,0:T(8,128)(2,1)S(1)}, u32[]{:S(2)}, u32[]{:S(2)}) collective-permute-start(bf16[32,512]{1,0:T(8,128)(2,1)S(1)} %get-tuple-element.29), channel_id=1, source_target_pairs={{0,4},{4,0},{8,12},{12,8},{16,20},{20,16},{24,28},{28,24},{32,36},... | collective-permute-start | bytes 98312 | tf_op jit(solution)/shard_map/ppermute | solution.py:304
  11.1 5.2 %collective-permute-start.1 = (bf16[32,512]{1,0:T(8,128)(2,1)S(1)}, bf16[32,512]{1,0:T(8,128)(2,1)S(1)}, u32[]{:S(2)}, u32[]{:S(2)}) collective-permute-start(bf16[32,512]{1,0:T(8,128)(2,1)S(1)} %get-tuple-element.30), channel_id=1, source_target_pairs={{4,8},{8,4},{12,16},{16,12},{20,24},{24,20},{28,32},{32,28},{36,40... | collective-permute-start | bytes 98312 | tf_op jit(solution)/shard_map/ppermute | solution.py:305
  13.0 0.7 copy-start.3
  16.3 11.3 %copy-start = (bf16[64,27,128]{2,0,1:T(8,128)(2,1)S(1)}, bf16[64,27,128]{2,0,1:T(8,128)(2,1)}, u32[]{:S(2)}) copy-start(bf16[64,27,128]{2,0,1:T(8,128)(2,1)} %param.7) | copy-start | bytes 1327108
  16.3 11.3 %copy-start.1 = (bf16[4,64,512]{2,1,0:T(8,128)(2,1)S(1)}, bf16[4,64,512]{2,1,0:T(8,128)(2,1)}, u32[]{:S(2)}) copy-start(bf16[4,64,512]{2,1,0:T(8,128)(2,1)} %cotangent.1) | copy-start | bytes 786436
  51.2 17.5 %all-to-all-start.1 = ((bf16[16,7,16,128]{3,2,1,0:T(8,128)(2,1)}), bf16[16,7,16,128]{3,2,1,0:T(8,128)(2,1)S(1)}, u32[]{:S(2)}, u32[]{:S(2)}) async-start(bf16[16,7,16,128]{3,2,1,0:T(8,128)(2,1)} %bitcast.7), calls=%async_computation.1 | async-start | bytes 917504 | tf_op jit(solution)/shard_map/all_to_all | solution.py:277
  59.6 5.6 %collective-permute-start.2 = (bf16[32,512]{1,0:T(8,128)(2,1)S(1)}, bf16[32,512]{1,0:T(8,128)(2,1)S(1)}, u32[]{:S(2)}, u32[]{:S(2)}) collective-permute-start(bf16[32,512]{1,0:T(8,128)(2,1)S(1)} %get-tuple-element.23), channel_id=1, source_target_pairs={{0,4},{4,0},{8,12},{12,8},{16,20},{20,16},{24,28},{28,24},{32,36},... | collective-permute-start | bytes 98312 | tf_op jit(solution)/shard_map/ppermute | solution.py:331
  61.6 5.8 %collective-permute-start.3 = (bf16[32,512]{1,0:T(8,128)(2,1)S(1)}, bf16[32,512]{1,0:T(8,128)(2,1)S(1)}, u32[]{:S(2)}, u32[]{:S(2)}) collective-permute-start(bf16[32,512]{1,0:T(8,128)(2,1)S(1)} %get-tuple-element.24), channel_id=1, source_target_pairs={{4,8},{8,4},{12,16},{16,12},{20,24},{24,20},{28,32},{32,28},{36,40... | collective-permute-start | bytes 98312 | tf_op jit(solution)/shard_map/ppermute | solution.py:332
  96.5 17.6 %all-to-all-start.3 = ((bf16[16,7,16,128]{3,2,1,0:T(8,128)(2,1)}), bf16[16,7,16,128]{3,2,1,0:T(8,128)(2,1)S(1)}, u32[]{:S(2)}, u32[]{:S(2)}) async-start(bf16[16,7,16,128]{3,2,1,0:T(8,128)(2,1)} %shard_map.81), calls=%async_computation.3 | async-start | bytes 917504 | tf_op jit(solution)/shard_map/all_to_all | solution.py:277

commit v3 on v2

--- a/solution.py
+++ b/solution.py
@@ -117,10 +117,10 @@
 
 
 def backward_kernel(
-    blocks, slots, stacked, grads, pieces, sums, wide
+    blocks, slots, place, stacked, grads, mine, *rest
 ):
+    sends, (sums, wide, turned) = rest[:-3], rest[-3:]
     sums[...] = jnp.zeros_like(sums)
-    row_index = lax.broadcasted_iota(jnp.int32, (64, 128), 0) % 8
     edge = lax.broadcasted_iota(jnp.int32, (8, 128), 0)
     for p in range(blocks):
         turn = grads[:, p * WIDE : (p + 1) * WIDE].astype(F32).T.astype(BF16)
@@ -158,11 +158,17 @@
                     first = pl.multiple_of(slots[p, number] * 512, 512)
                     rows = pl.ds(first + i_to * 64 + j_to * 8, 8 * len(js))
                     sums[rows, :] = sums[rows, :] + part
-    share = pieces.shape[2]
+    count, share = len(sends) + 1, mine.shape[1]
     for slot in range(blocks + 2):
-        turned = sums[slot * 512 : (slot + 1) * 512, :].T.astype(BF16)
-        for c in range(pieces.shape[0]):
-            pieces[c, slot] = turned[c * share : (c + 1) * share, :]
+        turned[slot * 128 : (slot + 1) * 128, :] = sums[slot * 512 : (slot + 1) * 512, :].T
+    for shift in range(count):
+        row = pl.multiple_of(lax.rem(place[0] + shift, count) * share, share)
+        for slot in range(blocks + 2):
+            piece = turned[pl.ds(slot * 128 + row, share), :]
+            if shift == 0:
+                mine[slot] = piece
+            else:
+                sends[shift - 1][slot] = piece.astype(BF16)
 
 
 def shape(*dims, dtype=BF16):
@@ -187,23 +193,26 @@
             pltpu.VMEM((blocks * WIDE, 1152), BF16),
         ],
         compiler_params=PARAMS,
+        cost_estimate=pl.CostEstimate(flops=3 * 10**9, bytes_accessed=4 * 10**6, transcendentals=10**6),
     )(slots, gathered, weight, cotangent, occupancy)
 
 
-def call_backward(slots, stacked, grads, chan):
+def call_backward(slots, place, stacked, grads, chan):
     blocks = slots.shape[0]
-    share = 128 // chan
+    piece = (blocks + 2, 128 // chan, 512)
     return pl.pallas_call(
         functools.partial(backward_kernel, blocks),
-        out_shape=shape(chan, blocks + 2, share, 512),
-        in_specs=[SMEM, VMEM, VMEM],
-        out_specs=VMEM,
+        out_shape=[shape(*piece, dtype=F32)] + [shape(*piece)] * (chan - 1),
+        in_specs=[SMEM, SMEM, VMEM, VMEM],
+        out_specs=[VMEM] * chan,
         scratch_shapes=[
             pltpu.VMEM(((blocks + 3) * 512, 128), F32),
             pltpu.VMEM((WIDE, 1152), F32),
+            pltpu.VMEM(((blocks + 2) * 128, 512), F32),
         ],
         compiler_params=PARAMS,
-    )(slots, stacked, grads)
+        cost_estimate=pl.CostEstimate(flops=2 * 10**9, bytes_accessed=8 * 10**6, transcendentals=0),
+    )(slots, place, stacked, grads)
 
 
 def add_kernel(copies, pieces, out):
@@ -224,26 +233,27 @@
     )(pieces)
 
 
-def sum_kernel(blocks, pieces, own, to_partner, to_across):
+def sum_kernel(blocks, mine, *refs):
+    arrived, (own, to_partner, to_across) = refs[:-3], refs[-3:]
     for slot in range(blocks + 2):
-        total = pieces[0, slot].astype(F32)
-        for c in range(1, pieces.shape[0]):
-            total = total + pieces[c, slot].astype(F32)
+        total = mine[slot]
+        for ref in arrived:
+            total = total + ref[slot].astype(F32)
         if slot < blocks:
             own[slot] = total
         else:
             (to_partner if slot == blocks else to_across)[...] = total.astype(BF16)
 
 
-def call_sum(pieces):
-    blocks, rim = pieces.shape[1] - 2, pieces.shape[2:]
+def call_sum(mine, arrived):
+    blocks, rim = mine.shape[0] - 2, mine.shape[1:]
     return pl.pallas_call(
         functools.partial(sum_kernel, blocks),
         out_shape=[shape(blocks, *rim, dtype=F32), shape(*rim), shape(*rim)],
-        in_specs=[VMEM],
+        in_specs=[VMEM] * (1 + len(arrived)),
         out_specs=[VMEM] * 3,
         compiler_params=PARAMS,
-    )(pieces)
+    )(mine, *arrived)
 
 
 def final_kernel(even, own, from_partner, from_across, occupancy, out):
@@ -325,16 +335,21 @@
         len(near[0]) * share,
     )
 
-    pieces = call_backward(slots, stacked, grads, chan)
-    own, rim_partner, rim_across = call_sum(lax.all_to_all(pieces, "chan", 0, 0))
-    rim_partner, rim_across, tiles = lax.optimization_barrier((rim_partner, rim_across, tiles))
+    parts = exchange(tiles.reshape(len(near[0]), share, 16, 128), near)
+    mine, *sends = call_backward(
+        slots, lax.axis_index("chan").astype(jnp.int32).reshape(1), stacked, grads, chan
+    )
+    parts, mine, sends = lax.optimization_barrier((parts, mine, sends))
+    parts = exchange(call_add(parts, len(far[0])), far)
+    arrived = [
+        lax.ppermute(piece, "chan", [(c, (c + shift + 1) % chan) for c in range(chan)])
+        for shift, piece in enumerate(sends)
+    ]
+    parts, arrived = lax.optimization_barrier((parts, arrived))
+    total = exchange(call_add(parts, len(near[0])), near)
+    own, rim_partner, rim_across = call_sum(mine, arrived)
     to_partner = lax.ppermute(rim_partner, "space", partner)
     to_across = lax.ppermute(rim_across, "space", across)
-
-    parts = exchange(tiles.reshape(len(near[0]), share, 16, 128), near)
-    to_partner, to_across, parts = lax.optimization_barrier((to_partner, to_across, parts))
-    parts = exchange(call_add(parts, len(far[0])), far)
-    total = exchange(call_add(parts, len(near[0])), near)
     total = total.reshape(-1, 16, 128)[:108].astype(F32).reshape(27, out, 128)
     weight_grad = jnp.transpose(total * lax.rsqrt(F32(space * blocks * 512)), (1, 0, 2))
 

time: 116 us -> 98 us (0.84)
  blocking collectives: 52.3 us -> 11.3 us
  starting transfers between devices: 33.1 us -> 52.4 us
  waiting for transfers between devices: 14.4 us -> 16.7 us
    all_to_all x2 -> x0, blocking collectives: 41 us -> none  [the longest x1 26.9 us: exchange(): return lax.all_to_all(pieces, 'space', 0, 0, axis_index_groups=groups)]
    ppermute x0 -> x3, starting transfers between devices: none -> 10.1 us  [on_device(): lax.ppermute(piece, 'chan', [(c, (c + shift + 1) % chan) for c in range(c...]
    all_to_all x2 -> x3, starting transfers between devices: 16.8 us -> 26.1 us  [exchange(): return lax.all_to_all(pieces, 'space', 0, 0, axis_index_groups=groups)]
    ppermute x0 -> x3, waiting for transfers between devices: none -> 5.25 us  [on_device(): lax.ppermute(piece, 'chan', [(c, (c + shift + 1) % chan) for c in range(c...]
    all_to_all x2 -> x3, waiting for transfers between devices: 9.74 us -> 6.84 us  [exchange(): return lax.all_to_all(pieces, 'space', 0, 0, axis_index_groups=groups)]
  transfers between devices with their start and end apart: 6 -> 10, of which waited for: 4 -> 7; matrix products, arithmetic and copies ran while one was open for 0% -> 0% of each run, Pallas kernels for 1% -> 5%
where the time goes in v3:
time: 98 us; the launch traced here: 96.6 us
  starting transfers between devices  52.4 us (53%)
  waiting for transfers between devices  16.7 us (17%)
  Pallas kernels  11.9 us (12%)
  blocking collectives  11.3 us (12%)
  other arithmetic  2.01 us (2%)
  local copies, waits for them, and re-layouts  1.43 us (1%)
    all_to_all x3, starting transfers between devices, exchange(): return lax.all_to_all(pieces, 'space', 0, 0, axis_index_groups=groups)  26.1 us
    all_gather x1, blocking collectives, on_device(): gathered = lax.all_gather(held, 'chan', axis=0)  11.3 us
    ppermute x3, starting transfers between devices, on_device(): lax.ppermute(piece, 'chan', [(c, (c + shift + 1) % chan) for c in range(c...  10.1 us
    ppermute x1, starting transfers between devices, on_device(): from_partner = lax.ppermute(jnp.where(even, last, first), 'space', partner)  8.79 us
    all_to_all x3, waiting for transfers between devices, exchange(): return lax.all_to_all(pieces, 'space', 0, 0, axis_index_groups=groups)  6.84 us
    pallas_call x1, Pallas kernels, call_forward(): pl.pallas_call(functools.partial(forward_kernel, blocks), out_shape=[shap...  5.62 us
    ppermute x3, waiting for transfers between devices, on_device(): lax.ppermute(piece, 'chan', [(c, (c + shift + 1) % chan) for c in range(c...  5.25 us
    pallas_call x1, Pallas kernels, call_backward(): pl.pallas_call(functools.partial(backward_kernel, blocks), out_shape=[sha...  3.93 us
  transfers between devices with their start and end apart: 10, of which 7 were waited for; matrix products, arithmetic and copies ran while one was open for 0% of the time, Pallas kernels for 5%

profile of v3, /device:TPU:1, one launch (start us, length us, event | category | flops | bytes accessed | tf_op | source)
XLA Modules:
  0.0 96.6 jit_solution(4264116850865560754)
XLA Ops:
  0.6 0.0 copy-start
  0.7 0.7 copy-done
  1.3 0.9 broadcast_multiply_fusion
  2.3 8.8 %collective-permute-start = (bf16[32,512]{1,0:T(8,128)(2,1)S(1)}, bf16[32,512]{1,0:T(8,128)(2,1)S(1)}, u32[]{:S(2)}, u32[]{:S(2)}) collective-permute-start(bf16[32,512]{1,0:T(8,128)(2,1)S(1)} %get-tuple-element.43), channel_id=1, source_target_pairs={{0,4},{4,0},{8,12},{12,8},{16,20},{20,16},{24,28},{28,24},{32,36},... | collective-permute-start | bytes 98312 | tf_op jit(solution)/shard_map/ppermute | solution.py:314
  11.1 1.9 %collective-permute-start.1 = (bf16[32,512]{1,0:T(8,128)(2,1)S(1)}, bf16[32,512]{1,0:T(8,128)(2,1)S(1)}, u32[]{:S(2)}, u32[]{:S(2)}) collective-permute-start(bf16[32,512]{1,0:T(8,128)(2,1)S(1)} %get-tuple-element.44), channel_id=1, source_target_pairs={{4,8},{8,4},{12,16},{16,12},{20,24},{24,20},{28,32},{32,28},{36,40... | collective-permute-start | bytes 98312 | tf_op jit(solution)/shard_map/ppermute | solution.py:315
  13.0 0.0 copy-start.3
  13.0 0.7 copy-done.3
  13.7 0.1 fusion.2
  13.8 0.1 fusion.1.slots
  13.8 0.0 collective-permute-done
  13.8 2.5 %collective-permute-done.1 = bf16[32,512]{1,0:T(8,128)(2,1)S(1)} collective-permute-done((bf16[32,512]{1,0:T(8,128)(2,1)S(1)}, bf16[32,512]{1,0:T(8,128)(2,1)S(1)}, u32[]{:S(2)}, u32[]{:S(2)}) %collective-permute-start.1) | collective-permute-done | bytes 32800 | tf_op jit(solution)/shard_map/ppermute | solution.py:315
  16.3 0.0 copy-start.1
  16.3 0.0 copy-start.2
  16.4 11.3 %all-gather = bf16[24,32,512]{2,1,0:T(8,128)(2,1)S(1)} all-gather(bf16[6,32,512]{2,1,0:T(8,128)(2,1)S(1)} %pad_maximum_fusion), channel_id=2, replica_groups=mesh['space'=128,'chan'=4] {'chan'}, dimensions={0}, use_global_device_ids=true | all-gather | bytes 983040 | tf_op jit(solution)/shard_map/all_gather | solution.py:317
  27.7 0.0 copy-done.1
  27.7 0.0 copy-done.2
  27.7 5.6 %shard_map.76 = (bf16[4,64,512]{2,1,0:T(8,128)(2,1)}, bf16[192,1152]{1,0:T(8,128)(2,1)S(1)}, bf16[192,2560]{1,0:T(8,128)(2,1)S(1)}, bf16[112,16,128]{2,1,0:T(8,128)(2,1)}) custom-call(s32[4,27]{1,0:T(4,128)S(1)} %fusion.1.slots, bf16[4,6,32,512]{3,2,1,0:T(8,128)(2,1)S(1)} %bitcast.15, bf16[27,64,128]{2,1,0:T(8,128)(2,1)S(1)} %bitcast.16, ...), custom_call_target="tpu_custom_call" | custom-call | flops 3000000000 | bytes 4000000 | tf_op jit(solution)/shard_map/pallas_call | solution.py:180
  33.3 9.5 %all-to-all-start = ((bf16[16,7,16,128]{3,2,1,0:T(8,128)(2,1)}), bf16[16,7,16,128]{3,2,1,0:T(8,128)(2,1)S(1)}, u32[]{:S(2)}, u32[]{:S(2)}) async-start(bf16[16,7,16,128]{3,2,1,0:T(8,128)(2,1)} %bitcast.7), calls=%async_computation | async-start | bytes 917504 | tf_op jit(solution)/shard_map/all_to_all | solution.py:287
  42.8 3.9 %shard_map.77 = (f32[6,32,512]{2,1,0:T(8,128)S(1)}, bf16[6,32,512]{2,1,0:T(8,128)(2,1)S(1)}, bf16[6,32,512]{2,1,0:T(8,128)(2,1)S(1)}, bf16[6,32,512]{2,1,0:T(8,128)(2,1)S(1)}) custom-call(s32[4,27]{1,0:T(4,128)S(1)} %fusion.1.slots, s32[1]{0:T(128)} %bitcast.8.place, bf16[192,1152]{1,0:T(8,128)(2,1)S(1)} %get-tuple-element.25.stacked, ...), custom_call_target="tpu_custom_call" | custom-call | flops 2000000000 | bytes 8000000 | tf_op jit(solution)/shard_map/pallas_call | solution.py:203
  46.7 5.2 %all-to-all-done.pieces = bf16[16,7,16,128]{3,2,1,0:T(8,128)(2,1)S(1)} async-done(((bf16[16,7,16,128]{3,2,1,0:T(8,128)(2,1)}), bf16[16,7,16,128]{3,2,1,0:T(8,128)(2,1)S(1)}, u32[]{:S(2)}, u32[]{:S(2)}) %all-to-all-start) | async-done | bytes 458784 | tf_op jit(solution)/shard_map/all_to_all | solution.py:287
  51.9 0.8 shard_map.78
  52.6 8.2 %all-to-all-start.1 = ((bf16[8,7,16,128]{3,2,1,0:T(8,128)(2,1)}), bf16[8,7,16,128]{3,2,1,0:T(8,128)(2,1)S(1)}, u32[]{:S(2)}, u32[]{:S(2)}) async-start(bf16[8,7,16,128]{3,2,1,0:T(8,128)(2,1)} %shard_map.78), calls=%async_computation.1 | async-start | bytes 458752 | tf_op jit(solution)/shard_map/all_to_all | solution.py:287
  60.8 3.8 %collective-permute-start.2 = (bf16[6,32,512]{2,1,0:T(8,128)(2,1)S(1)}, bf16[6,32,512]{2,1,0:T(8,128)(2,1)S(1)}, u32[]{:S(2)}, u32[]{:S(2)}) collective-permute-start(bf16[6,32,512]{2,1,0:T(8,128)(2,1)S(1)} %get-tuple-element.33), channel_id=1, source_target_pairs={{0,1},{1,2},{2,3},{3,0},{4,5},{5,6},{6,7},{7,4},{8,9},{9,10},{10,1... | collective-permute-start | bytes 589832 | tf_op jit(solution)/shard_map/ppermute | solution.py:345
  64.6 4.3 %collective-permute-start.3 = (bf16[6,32,512]{2,1,0:T(8,128)(2,1)S(1)}, bf16[6,32,512]{2,1,0:T(8,128)(2,1)S(1)}, u32[]{:S(2)}, u32[]{:S(2)}) collective-permute-start(bf16[6,32,512]{2,1,0:T(8,128)(2,1)S(1)} %get-tuple-element.34), channel_id=1, source_target_pairs={{0,2},{1,3},{2,0},{3,1},{4,6},{5,7},{6,4},{7,5},{8,10},{9,11},{10,... | collective-permute-start | bytes 589832 | tf_op jit(solution)/shard_map/ppermute | solution.py:345
  68.9 1.9 %collective-permute-start.4 = (bf16[6,32,512]{2,1,0:T(8,128)(2,1)S(1)}, bf16[6,32,512]{2,1,0:T(8,128)(2,1)S(1)}, u32[]{:S(2)}, u32[]{:S(2)}) collective-permute-start(bf16[6,32,512]{2,1,0:T(8,128)(2,1)S(1)} %get-tuple-element.35), channel_id=1, source_target_pairs={{0,3},{1,0},{2,1},{3,2},{4,7},{5,4},{6,5},{7,6},{8,11},{9,8},{10,9... | collective-permute-start | bytes 589832 | tf_op jit(solution)/shard_map/ppermute | solution.py:345
  70.9 0.0 collective-permute-done.2.refs_0_
  70.9 4.0 %collective-permute-done.3.refs_1_ = bf16[6,32,512]{2,1,0:T(8,128)(2,1)S(1)} collective-permute-done((bf16[6,32,512]{2,1,0:T(8,128)(2,1)S(1)}, bf16[6,32,512]{2,1,0:T(8,128)(2,1)S(1)}, u32[]{:S(2)}, u32[]{:S(2)}) %collective-permute-start.3) | collective-permute-done | bytes 196640 | tf_op jit(solution)/shard_map/ppermute | solution.py:345
  74.9 1.2 %collective-permute-done.4.refs_2_ = bf16[6,32,512]{2,1,0:T(8,128)(2,1)S(1)} collective-permute-done((bf16[6,32,512]{2,1,0:T(8,128)(2,1)S(1)}, bf16[6,32,512]{2,1,0:T(8,128)(2,1)S(1)}, u32[]{:S(2)}, u32[]{:S(2)}) %collective-permute-start.4) | collective-permute-done | bytes 196640 | tf_op jit(solution)/shard_map/ppermute | solution.py:345
  76.1 1.1 %all-to-all-done.1.pieces = bf16[8,7,16,128]{3,2,1,0:T(8,128)(2,1)S(1)} async-done(((bf16[8,7,16,128]{3,2,1,0:T(8,128)(2,1)}), bf16[8,7,16,128]{3,2,1,0:T(8,128)(2,1)S(1)}, u32[]{:S(2)}, u32[]{:S(2)}) %all-to-all-start.1) | async-done | bytes 229408 | tf_op jit(solution)/shard_map/all_to_all | solution.py:287
  77.2 0.8 shard_map.81
  78.0 8.4 %all-to-all-start.2 = ((bf16[16,7,16,128]{3,2,1,0:T(8,128)(2,1)}), bf16[16,7,16,128]{3,2,1,0:T(8,128)(2,1)S(1)}, u32[]{:S(2)}, u32[]{:S(2)}) async-start(bf16[16,7,16,128]{3,2,1,0:T(8,128)(2,1)} %shard_map.81), calls=%async_computation.2 | async-start | bytes 917504 | tf_op jit(solution)/shard_map/all_to_all | solution.py:287
  86.5 0.1 shard_map.79
  86.6 2.1 %collective-permute-start.5 = (bf16[32,512]{1,0:T(8,128)(2,1)S(1)}, bf16[32,512]{1,0:T(8,128)(2,1)S(1)}, u32[]{:S(2)}, u32[]{:S(2)}) collective-permute-start(bf16[32,512]{1,0:T(8,128)(2,1)S(1)} %get-tuple-element.40), channel_id=1, source_target_pairs={{0,4},{4,0},{8,12},{12,8},{16,20},{20,16},{24,28},{28,24},{32,36},... | collective-permute-start | bytes 98312 | tf_op jit(solution)/shard_map/ppermute | solution.py:351
  88.7 3.5 %collective-permute-start.6 = (bf16[32,512]{1,0:T(8,128)(2,1)S(1)}, bf16[32,512]{1,0:T(8,128)(2,1)S(1)}, u32[]{:S(2)}, u32[]{:S(2)}) collective-permute-start(bf16[32,512]{1,0:T(8,128)(2,1)S(1)} %get-tuple-element.41), channel_id=1, source_target_pairs={{4,8},{8,4},{12,16},{16,12},{20,24},{24,20},{28,32},{32,28},{36,40... | collective-permute-start | bytes 98312 | tf_op jit(solution)/shard_map/ppermute | solution.py:352
  92.2 0.0 collective-permute-done.5.from_partner
  92.2 2.2 %collective-permute-done.6.from_across = bf16[32,512]{1,0:T(8,128)(2,1)S(1)} collective-permute-done((bf16[32,512]{1,0:T(8,128)(2,1)S(1)}, bf16[32,512]{1,0:T(8,128)(2,1)S(1)}, u32[]{:S(2)}, u32[]{:S(2)}) %collective-permute-start.6) | collective-permute-done | bytes 32800 | tf_op jit(solution)/shard_map/ppermute | solution.py:352
  94.4 0.7 shard_map.80
  95.0 0.6 all-to-all-done.2
  95.6 1.0 %convert_multiply_fusion = f32[108,16,128]{2,1,0:T(8,128)} fusion(bf16[112,16,128]{2,1,0:T(8,128)(2,1)S(1)} %bitcast.17), kind=kLoop, calls=%fused_computation | loop fusion | flops 442368 | bytes 1327104 | tf_op jit(solution)/shard_map/mul | solution.py:354
  (4 shorter events, 0.0 us)
Async XLA Ops:
  0.6 0.7 copy-start
  2.3 11.6 %collective-permute-start = (bf16[32,512]{1,0:T(8,128)(2,1)S(1)}, bf16[32,512]{1,0:T(8,128)(2,1)S(1)}, u32[]{:S(2)}, u32[]{:S(2)}) collective-permute-start(bf16[32,512]{1,0:T(8,128)(2,1)S(1)} %get-tuple-element.43), channel_id=1, source_target_pairs={{0,4},{4,0},{8,12},{12,8},{16,20},{20,16},{24,28},{28,24},{32,36},... | collective-permute-start | bytes 98312 | tf_op jit(solution)/shard_map/ppermute | solution.py:314
  11.1 5.2 %collective-permute-start.1 = (bf16[32,512]{1,0:T(8,128)(2,1)S(1)}, bf16[32,512]{1,0:T(8,128)(2,1)S(1)}, u32[]{:S(2)}, u32[]{:S(2)}) collective-permute-start(bf16[32,512]{1,0:T(8,128)(2,1)S(1)} %get-tuple-element.44), channel_id=1, source_target_pairs={{4,8},{8,4},{12,16},{16,12},{20,24},{24,20},{28,32},{32,28},{36,40... | collective-permute-start | bytes 98312 | tf_op jit(solution)/shard_map/ppermute | solution.py:315
  13.0 0.7 copy-start.3
  16.3 11.3 %copy-start.1 = (bf16[64,27,128]{2,0,1:T(8,128)(2,1)S(1)}, bf16[64,27,128]{2,0,1:T(8,128)(2,1)}, u32[]{:S(2)}) copy-start(bf16[64,27,128]{2,0,1:T(8,128)(2,1)} %param.7) | copy-start | bytes 1327108
  16.3 11.3 %copy-start.2 = (bf16[4,64,512]{2,1,0:T(8,128)(2,1)S(1)}, bf16[4,64,512]{2,1,0:T(8,128)(2,1)}, u32[]{:S(2)}) copy-start(bf16[4,64,512]{2,1,0:T(8,128)(2,1)} %cotangent.1) | copy-start | bytes 786436
  33.3 18.6 %all-to-all-start = ((bf16[16,7,16,128]{3,2,1,0:T(8,128)(2,1)}), bf16[16,7,16,128]{3,2,1,0:T(8,128)(2,1)S(1)}, u32[]{:S(2)}, u32[]{:S(2)}) async-start(bf16[16,7,16,128]{3,2,1,0:T(8,128)(2,1)} %bitcast.7), calls=%async_computation | async-start | bytes 917504 | tf_op jit(solution)/shard_map/all_to_all | solution.py:287
  52.6 24.6 %all-to-all-start.1 = ((bf16[8,7,16,128]{3,2,1,0:T(8,128)(2,1)}), bf16[8,7,16,128]{3,2,1,0:T(8,128)(2,1)S(1)}, u32[]{:S(2)}, u32[]{:S(2)}) async-start(bf16[8,7,16,128]{3,2,1,0:T(8,128)(2,1)} %shard_map.78), calls=%async_computation.1 | async-start | bytes 458752 | tf_op jit(solution)/shard_map/all_to_all | solution.py:287
  60.8 10.1 %collective-permute-start.2 = (bf16[6,32,512]{2,1,0:T(8,128)(2,1)S(1)}, bf16[6,32,512]{2,1,0:T(8,128)(2,1)S(1)}, u32[]{:S(2)}, u32[]{:S(2)}) collective-permute-start(bf16[6,32,512]{2,1,0:T(8,128)(2,1)S(1)} %get-tuple-element.33), channel_id=1, source_target_pairs={{0,1},{1,2},{2,3},{3,0},{4,5},{5,6},{6,7},{7,4},{8,9},{9,10},{10,1... | collective-permute-start | bytes 589832 | tf_op jit(solution)/shard_map/ppermute | solution.py:345
  64.6 10.3 %collective-permute-start.3 = (bf16[6,32,512]{2,1,0:T(8,128)(2,1)S(1)}, bf16[6,32,512]{2,1,0:T(8,128)(2,1)S(1)}, u32[]{:S(2)}, u32[]{:S(2)}) collective-permute-start(bf16[6,32,512]{2,1,0:T(8,128)(2,1)S(1)} %get-tuple-element.34), channel_id=1, source_target_pairs={{0,2},{1,3},{2,0},{3,1},{4,6},{5,7},{6,4},{7,5},{8,10},{9,11},{10,... | collective-permute-start | bytes 589832 | tf_op jit(solution)/shard_map/ppermute | solution.py:345
  68.9 7.2 %collective-permute-start.4 = (bf16[6,32,512]{2,1,0:T(8,128)(2,1)S(1)}, bf16[6,32,512]{2,1,0:T(8,128)(2,1)S(1)}, u32[]{:S(2)}, u32[]{:S(2)}) collective-permute-start(bf16[6,32,512]{2,1,0:T(8,128)(2,1)S(1)} %get-tuple-element.35), channel_id=1, source_target_pairs={{0,3},{1,0},{2,1},{3,2},{4,7},{5,4},{6,5},{7,6},{8,11},{9,8},{10,9... | collective-permute-start | bytes 589832 | tf_op jit(solution)/shard_map/ppermute | solution.py:345
  78.0 17.6 %all-to-all-start.2 = ((bf16[16,7,16,128]{3,2,1,0:T(8,128)(2,1)}), bf16[16,7,16,128]{3,2,1,0:T(8,128)(2,1)S(1)}, u32[]{:S(2)}, u32[]{:S(2)}) async-start(bf16[16,7,16,128]{3,2,1,0:T(8,128)(2,1)} %shard_map.81), calls=%async_computation.2 | async-start | bytes 917504 | tf_op jit(solution)/shard_map/all_to_all | solution.py:287
  86.6 5.6 %collective-permute-start.5 = (bf16[32,512]{1,0:T(8,128)(2,1)S(1)}, bf16[32,512]{1,0:T(8,128)(2,1)S(1)}, u32[]{:S(2)}, u32[]{:S(2)}) collective-permute-start(bf16[32,512]{1,0:T(8,128)(2,1)S(1)} %get-tuple-element.40), channel_id=1, source_target_pairs={{0,4},{4,0},{8,12},{12,8},{16,20},{20,16},{24,28},{28,24},{32,36},... | collective-permute-start | bytes 98312 | tf_op jit(solution)/shard_map/ppermute | solution.py:351
  88.7 5.7 %collective-permute-start.6 = (bf16[32,512]{1,0:T(8,128)(2,1)S(1)}, bf16[32,512]{1,0:T(8,128)(2,1)S(1)}, u32[]{:S(2)}, u32[]{:S(2)}) collective-permute-start(bf16[32,512]{1,0:T(8,128)(2,1)S(1)} %get-tuple-element.41), channel_id=1, source_target_pairs={{4,8},{8,4},{12,16},{16,12},{20,24},{24,20},{28,32},{32,28},{36,40... | collective-permute-start | bytes 98312 | tf_op jit(solution)/shard_map/ppermute | solution.py:352

commit v4 on v3

--- a/solution.py
+++ b/solution.py
@@ -63,50 +63,92 @@
                     patches[row : row + 16, lanes : lanes + 128] = pairs[2 * t + b]
 
 
-def stack_weight(weight, stacked):
+def load_block(gathered, occupancy, slot):
+    block = jnp.concatenate([gathered[c, slot] for c in range(gathered.shape[0])], axis=0)
+    return block.astype(F32) * occupancy[slot : slot + 1, :].astype(F32)
+
+
+def rim_kernel(even, gathered, occupancy, to_partner, to_across):
+    first = load_block(gathered, occupancy, 0).astype(BF16)
+    last = load_block(gathered, occupancy, gathered.shape[1] - 1).astype(BF16)
+    is_even = even[0] == 1
+    to_partner[...] = jnp.where(is_even, last, first)
+    to_across[...] = jnp.where(is_even, first, last)
+
+
+def forward_block(
+    slots, block, stacked, cotangent, occupancy, voxels, cube, patches, grads, place
+):
+    base, top = place * CUBE, place * WIDE
+    fill_cube(slots, block, voxels, cube, base)
+    pack_patches(cube, base, patches, top)
+    wide = lax.dot_general(
+        stacked[...], patches[top : top + WIDE, :], NT, preferred_element_type=F32
+    )
+    pre = (
+        wide[0:64, 0:512]
+        + pltpu.roll(wide[64:128], WIDE - 64, 1)[:, 0:512]
+        + wide[128:192, 128:640]
+    )
+    live = occupancy[block : block + 1, :].astype(F32)
+    sigma = jax.nn.sigmoid(pre)
+    slope = sigma * (1.0 + pre * (1.0 - sigma))
+    grad = (cotangent[block].astype(F32) * slope * live).astype(BF16).astype(F32)
+    grad = jnp.concatenate([grad, jnp.zeros((64, 128), F32)], axis=1)
+    lanes = slice(top, top + WIDE)
+    grads[0:64, lanes] = grad.astype(BF16)
+    grads[64:128, lanes] = pltpu.roll(grad, 64, 1).astype(BF16)
+    grads[128:192, lanes] = pltpu.roll(grad, 128, 1).astype(BF16)
+    return (pre * sigma * live).astype(BF16)
+
+
+def own_voxels(gathered, occupancy, voxels):
+    blocks = gathered.shape[1]
+    for slot in range(blocks):
+        block = load_block(gathered, occupancy, slot)
+        voxels[slot * 512 : (slot + 1) * 512, :] = block.T
+    voxels[(blocks + 2) * 512 : (blocks + 3) * 512, :] = jnp.zeros((512, 128), F32)
+
+
+def inner_kernel(
+    slots, gathered, weight, cotangent, occupancy,
+    activation, stacked, grads, product,
+    voxels, cube, patches,
+):
+    blocks = cotangent.shape[0]
     out = weight.shape[1]
     for number in range(27):
         a, lanes = number // 9, number % 9 * 128
         stacked[a * out : (a + 1) * out, lanes : lanes + 128] = weight[number]
-
-
-def forward_kernel(
-    blocks, slots, gathered, weight, cotangent, occupancy,
-    activation, stacked, grads, tiles,
+    own_voxels(gathered, occupancy, voxels)
+    for block in range(1, blocks - 1):
+        activation[block - 1] = forward_block(
+            slots, block, stacked, cotangent, occupancy, voxels, cube, patches, grads, block - 1
+        )
+    for first in range(0, 9, 2):
+        lanes = slice(first * 128, min(first + 2, 9) * 128)
+        product[:, lanes] = jnp.dot(grads[...], patches[:, lanes], preferred_element_type=F32)
+
+
+def outer_kernel(
+    slots, gathered, from_partner, from_across, cotangent, occupancy, inner, stacked, product,
+    activation, grads, tiles,
     voxels, cube, patches,
 ):
-    stack_weight(weight, stacked)
-    for slot in range(blocks + 2):
-        block = jnp.concatenate([gathered[c, slot] for c in range(gathered.shape[0])], axis=0)
-        voxels[slot * 512 : (slot + 1) * 512, :] = block.astype(F32).T
-    voxels[(blocks + 2) * 512 : (blocks + 3) * 512, :] = jnp.zeros((512, 128), F32)
-    for p in range(blocks):
-        fill_cube(slots, p, voxels, cube, p * CUBE)
-        pack_patches(cube, p * CUBE, patches, p * WIDE)
-        wide = lax.dot_general(
-            stacked[...], patches[p * WIDE : (p + 1) * WIDE, :], NT, preferred_element_type=F32
+    blocks = cotangent.shape[0]
+    own_voxels(gathered, occupancy, voxels)
+    for slot, rim in ((blocks, from_partner), (blocks + 1, from_across)):
+        voxels[slot * 512 : (slot + 1) * 512, :] = rim[...].astype(F32).T
+    activation[1 : blocks - 1] = inner[...]
+    for place, block in enumerate((0, blocks - 1)):
+        activation[block] = forward_block(
+            slots, block, stacked, cotangent, occupancy, voxels, cube, patches, grads, place
         )
-        pre = (
-            wide[0:64, 0:512]
-            + pltpu.roll(wide[64:128], WIDE - 64, 1)[:, 0:512]
-            + wide[128:192, 128:640]
-        )
-        live = occupancy[p : p + 1, :].astype(F32)
-        sigma = jax.nn.sigmoid(pre)
-        activation[p] = (pre * sigma * live).astype(BF16)
-        slope = sigma * (1.0 + pre * (1.0 - sigma))
-        grad = (cotangent[p].astype(F32) * slope * live).astype(BF16).astype(F32)
-        grad = jnp.concatenate([grad, jnp.zeros((64, 128), F32)], axis=1)
-        lanes = slice(p * WIDE, (p + 1) * WIDE)
-        grads[0:64, lanes] = grad.astype(BF16)
-        grads[64:128, lanes] = pltpu.roll(grad, 64, 1).astype(BF16)
-        grads[128:192, lanes] = pltpu.roll(grad, 128, 1).astype(BF16)
     for first in range(0, 9, 2):
         count = min(2, 9 - first)
-        part = jnp.dot(
-            grads[...],
-            patches[:, first * 128 : (first + count) * 128],
-            preferred_element_type=F32,
+        lanes = slice(first * 128, (first + count) * 128)
+        part = product[:, lanes] + jnp.dot(
+            grads[...], patches[:, lanes], preferred_element_type=F32
         )
         for t in range(count):
             for r in range(12):
@@ -117,13 +159,14 @@
 
 
 def backward_kernel(
-    blocks, slots, place, stacked, grads, mine, *rest
+    blocks, slots, place, stacked, inner, outer, mine, *rest
 ):
     sends, (sums, wide, turned) = rest[:-3], rest[-3:]
     sums[...] = jnp.zeros_like(sums)
     edge = lax.broadcasted_iota(jnp.int32, (8, 128), 0)
     for p in range(blocks):
-        turn = grads[:, p * WIDE : (p + 1) * WIDE].astype(F32).T.astype(BF16)
+        grads, at = (inner, p - 1) if 0 < p < blocks - 1 else (outer, min(p, 1))
+        turn = grads[:, at * WIDE : (at + 1) * WIDE].astype(F32).T.astype(BF16)
         wide[...] = jnp.dot(turn, stacked[...], preferred_element_type=F32)
         for i in range(10):
             a, i_to = (-1, 7) if i == 0 else ((1, 0) if i == 9 else (0, i - 1))
@@ -175,35 +218,68 @@
     return jax.ShapeDtypeStruct(dims, dtype)
 
 
-def call_forward(slots, gathered, weight, cotangent, occupancy, tiles):
+def call_rims(even, gathered, occupancy):
+    rim = shape(128, 512)
+    return pl.pallas_call(
+        rim_kernel,
+        out_shape=[rim, rim],
+        in_specs=[SMEM, VMEM, VMEM],
+        out_specs=[VMEM] * 2,
+        compiler_params=PARAMS,
+        cost_estimate=pl.CostEstimate(flops=10**6, bytes_accessed=10**6, transcendentals=0),
+    )(even, gathered, occupancy)
+
+
+def scratch_of(blocks, count):
+    return [
+        pltpu.VMEM(((blocks + 3) * 512, 128), F32),
+        pltpu.VMEM((count * CUBE, 128), F32),
+        pltpu.VMEM((count * WIDE, 1152), BF16),
+    ]
+
+
+def call_inner(slots, gathered, weight, cotangent, occupancy):
     blocks, out = cotangent.shape[:2]
     return pl.pallas_call(
-        functools.partial(forward_kernel, blocks),
+        inner_kernel,
         out_shape=[
-            shape(blocks, out, 512),
+            shape(blocks - 2, out, 512),
             shape(3 * out, 1152),
-            shape(3 * out, blocks * WIDE),
-            shape(tiles, 16, 128),
+            shape(3 * out, (blocks - 2) * WIDE),
+            shape(3 * out, 1152, dtype=F32),
         ],
         in_specs=[SMEM] + [VMEM] * 4,
         out_specs=[VMEM] * 4,
-        scratch_shapes=[
-            pltpu.VMEM(((blocks + 3) * 512, 128), F32),
-            pltpu.VMEM((blocks * CUBE, 128), F32),
-            pltpu.VMEM((blocks * WIDE, 1152), BF16),
+        scratch_shapes=scratch_of(blocks, blocks - 2),
+        compiler_params=PARAMS,
+        cost_estimate=pl.CostEstimate(flops=10**9, bytes_accessed=4 * 10**6, transcendentals=10**5),
+    )(slots, gathered, weight, cotangent, occupancy)
+
+
+def call_outer(slots, gathered, rims, cotangent, occupancy, inner, stacked, product, tiles):
+    blocks, out = cotangent.shape[:2]
+    return pl.pallas_call(
+        outer_kernel,
+        out_shape=[
+            shape(blocks, out, 512),
+            shape(3 * out, 2 * WIDE),
+            shape(tiles, 16, 128),
         ],
-        compiler_params=PARAMS,
-        cost_estimate=pl.CostEstimate(flops=3 * 10**9, bytes_accessed=4 * 10**6, transcendentals=10**6),
-    )(slots, gathered, weight, cotangent, occupancy)
-
-
-def call_backward(slots, place, stacked, grads, chan):
+        in_specs=[SMEM] + [VMEM] * 8,
+        out_specs=[VMEM] * 3,
+        scratch_shapes=scratch_of(blocks, 2),
+        compiler_params=PARAMS,
+        cost_estimate=pl.CostEstimate(flops=10**9, bytes_accessed=4 * 10**6, transcendentals=10**5),
+    )(slots, gathered, *rims, cotangent, occupancy, inner, stacked, product)
+
+
+def call_backward(slots, place, stacked, inner, outer, chan):
     blocks = slots.shape[0]
     piece = (blocks + 2, 128 // chan, 512)
     return pl.pallas_call(
         functools.partial(backward_kernel, blocks),
         out_shape=[shape(*piece, dtype=F32)] + [shape(*piece)] * (chan - 1),
-        in_specs=[SMEM, SMEM, VMEM, VMEM],
+        in_specs=[SMEM, SMEM, VMEM, VMEM, VMEM],
         out_specs=[VMEM] * chan,
         scratch_shapes=[
             pltpu.VMEM(((blocks + 3) * 512, 128), F32),
@@ -212,7 +288,7 @@
         ],
         compiler_params=PARAMS,
         cost_estimate=pl.CostEstimate(flops=2 * 10**9, bytes_accessed=8 * 10**6, transcendentals=0),
-    )(slots, place, stacked, grads)
+    )(slots, place, stacked, inner, outer)
 
 
 def add_kernel(copies, pieces, out):
@@ -276,7 +352,7 @@
         in_specs=[SMEM] + [VMEM] * 4,
         out_specs=VMEM,
         compiler_params=PARAMS,
-    )(even.astype(jnp.int32).reshape(1), own, from_partner, from_across, occupancy)
+    )(even, own, from_partner, from_across, occupancy)
 
 
 def stages_of(count):
@@ -309,12 +385,12 @@
 
     partner = [(i, i ^ 1) for i in range(space)]
     across = [(i, i - 1 if i % 2 == 0 else i + 1) for i in range(1, space - 1)]
-    masked = features * occupancy.astype(BF16)[:, None, :]
-    first, last = masked[0], masked[blocks - 1]
-    from_partner = lax.ppermute(jnp.where(even, last, first), "space", partner)
-    from_across = lax.ppermute(jnp.where(even, first, last), "space", across)
-    held = jnp.concatenate([masked, from_partner[None], from_across[None]])
-    gathered = lax.all_gather(held, "chan", axis=0)
+    even_flag = even.astype(jnp.int32).reshape(1)
+    gathered = lax.all_gather(features, "chan", axis=0)
+    rims = [
+        lax.ppermute(rim, "space", pairs)
+        for rim, pairs in zip(call_rims(even_flag, gathered, occupancy), (partner, across))
+    ]
 
     ids = jnp.concatenate(
         [
@@ -330,21 +406,23 @@
     slots = jnp.where(slots == -1, below, jnp.where(slots == blocks, above, slots))
     slots = jnp.where(ids < 0, blocks + 2, slots)
 
-    activation, stacked, grads, tiles = call_forward(
-        slots, gathered, jnp.transpose(weight, (1, 0, 2)), cotangent, occupancy,
-        len(near[0]) * share,
+    inner, stacked, inner_grads, product = call_inner(
+        slots, gathered, jnp.transpose(weight, (1, 0, 2)), cotangent, occupancy
+    )
+    activation, outer_grads, tiles = call_outer(
+        slots, gathered, rims, cotangent, occupancy, inner, stacked, product, len(near[0]) * share
     )
 
     parts = exchange(tiles.reshape(len(near[0]), share, 16, 128), near)
     mine, *sends = call_backward(
-        slots, lax.axis_index("chan").astype(jnp.int32).reshape(1), stacked, grads, chan
-    )
-    parts, mine, sends = lax.optimization_barrier((parts, mine, sends))
+        slots, lax.axis_index("chan").astype(jnp.int32).reshape(1), stacked,
+        inner_grads, outer_grads, chan,
+    )
+    rings = [[(c, (c + shift) % chan) for c in range(chan)] for shift in range(1, chan)]
+    arrived = [lax.ppermute(sends[0], "chan", rings[0])]
+    parts, mine, arrived, sends = lax.optimization_barrier((parts, mine, arrived, sends))
     parts = exchange(call_add(parts, len(far[0])), far)
-    arrived = [
-        lax.ppermute(piece, "chan", [(c, (c + shift + 1) % chan) for c in range(chan)])
-        for shift, piece in enumerate(sends)
-    ]
+    arrived += [lax.ppermute(piece, "chan", ring) for piece, ring in zip(sends[1:], rings[1:])]
     parts, arrived = lax.optimization_barrier((parts, arrived))
     total = exchange(call_add(parts, len(near[0])), near)
     own, rim_partner, rim_across = call_sum(mine, arrived)
@@ -353,7 +431,7 @@
     total = total.reshape(-1, 16, 128)[:108].astype(F32).reshape(27, out, 128)
     weight_grad = jnp.transpose(total * lax.rsqrt(F32(space * blocks * 512)), (1, 0, 2))
 
-    input_grad = call_final(even, own, to_partner, to_across, occupancy)
+    input_grad = call_final(even_flag, own, to_partner, to_across, occupancy)
     return (activation, input_grad, weight_grad)
 
 

time: 98 us -> 100 us (1.020); the launches traced: 96.6 us -> 99.8 us
  waiting for transfers between devices: 16.7 us -> 19.2 us
  Pallas kernels: 11.9 us -> 13.7 us
    ppermute x5, waiting for transfers between devices: 7.71 us -> 11.9 us  [the longest x1 6.26 us: on_device(): arrived = [lax.ppermute(sends[0], 'chan', rings[0])]]
    pallas_call x1 -> x3, Pallas kernels: 5.62 us -> 7.36 us  [the longest x1 4.09 us: call_outer(): pl.pallas_call(outer_kernel, out_shape=[shape(blocks, out, 512), shape(3...]
    all_to_all x3, waiting for transfers between devices: 6.84 us -> 5.16 us  [exchange(): return lax.all_to_all(pieces, 'space', 0, 0, axis_index_groups=groups)]
    ppermute x5, starting transfers between devices: 20.8 us -> 22.3 us  [the longest x2 12.6 us: on_device(): lax.ppermute(rim, 'space', pairs)]
    all_to_all x3, starting transfers between devices: 26.1 us -> 24.9 us  [exchange(): return lax.all_to_all(pieces, 'space', 0, 0, axis_index_groups=groups)]
  transfers between devices with their start and end apart: 10 -> 10, of which waited for: 7 -> 7; matrix products, arithmetic and copies ran while one was open for 0% -> 0% of each run, Pallas kernels for 5% -> 8%
where the time goes in v4:
time: 100 us; the launch traced here: 99.8 us
  starting transfers between devices  52.9 us (53%)
  waiting for transfers between devices  19.2 us (19%)
  Pallas kernels  13.7 us (14%)
  blocking collectives  11.4 us (11%)
  other arithmetic  1.06 us (1%)
    all_to_all x3, starting transfers between devices, exchange(): return lax.all_to_all(pieces, 'space', 0, 0, axis_index_groups=groups)  24.9 us
    ppermute x2, starting transfers between devices, on_device(): lax.ppermute(rim, 'space', pairs)  12.6 us
    all_gather x1, blocking collectives, on_device(): gathered = lax.all_gather(features, 'chan', axis=0)  11.4 us
    ppermute x2, starting transfers between devices, on_device(): lax.ppermute(piece, 'chan', ring)  6.3 us
    ppermute x1, waiting for transfers between devices, on_device(): arrived = [lax.ppermute(sends[0], 'chan', rings[0])]  6.26 us
    ppermute x2, waiting for transfers between devices, on_device(): lax.ppermute(piece, 'chan', ring)  5.38 us
    all_to_all x3, waiting for transfers between devices, exchange(): return lax.all_to_all(pieces, 'space', 0, 0, axis_index_groups=groups)  5.16 us
    pallas_call x1, Pallas kernels, call_outer(): pl.pallas_call(outer_kernel, out_shape=[shape(blocks, out, 512), shape(3...  4.09 us
  transfers between devices with their start and end apart: 10, of which 7 were waited for; matrix products, arithmetic and copies ran while one was open for 0% of the time, Pallas kernels for 8%

profile of v4, /device:TPU:1, one launch (start us, length us, event | category | flops | bytes accessed | tf_op | source)
XLA Modules:
  0.0 99.8 jit_solution(4979292841228909081)
XLA Ops:
  0.6 0.0 copy-start
  0.7 0.0 copy-start.2
  0.7 11.4 %all-gather = bf16[16,32,512]{2,1,0:T(8,128)(2,1)S(1)} all-gather(bf16[4,32,512]{2,1,0:T(8,128)(2,1)} %param.5), channel_id=2, replica_groups=mesh['space'=128,'chan'=4] {'chan'}, dimensions={0}, use_global_device_ids=true | all-gather | bytes 655360 | tf_op jit(solution)/shard_map/all_gather | solution.py:389
  12.1 0.0 copy-start.1
  12.1 0.0 copy-done
  12.1 0.1 shard_map.76
  12.2 10.6 %collective-permute-start = (bf16[128,512]{1,0:T(8,128)(2,1)S(1)}, bf16[128,512]{1,0:T(8,128)(2,1)S(1)}, u32[]{:S(2)}, u32[]{:S(2)}) collective-permute-start(bf16[128,512]{1,0:T(8,128)(2,1)S(1)} %get-tuple-element.28), channel_id=1, source_target_pairs={{0,4},{4,0},{8,12},{12,8},{16,20},{20,16},{24,28},{28,24},{32,36},... | collective-permute-start | bytes 393224 | tf_op jit(solution)/shard_map/ppermute | solution.py:391
  22.8 1.9 %collective-permute-start.1 = (bf16[128,512]{1,0:T(8,128)(2,1)S(1)}, bf16[128,512]{1,0:T(8,128)(2,1)S(1)}, u32[]{:S(2)}, u32[]{:S(2)}) collective-permute-start(bf16[128,512]{1,0:T(8,128)(2,1)S(1)} %get-tuple-element.29), channel_id=1, source_target_pairs={{4,8},{8,4},{12,16},{16,12},{20,24},{24,20},{28,32},{32,28},{36,40... | collective-permute-start | bytes 393224 | tf_op jit(solution)/shard_map/ppermute | solution.py:391
  24.7 0.0 copy-start.3
  24.8 0.7 copy-done.3
  25.4 0.1 fusion.2
  25.5 0.1 fusion.1.slots
  25.6 0.0 copy-done.2
  25.6 0.0 copy-done.1
  25.6 3.2 %shard_map.77 = (bf16[2,64,512]{2,1,0:T(8,128)(2,1)S(1)}, bf16[192,1152]{1,0:T(8,128)(2,1)S(1)}, bf16[192,1280]{1,0:T(8,128)(2,1)S(1)}, f32[192,1152]{1,0:T(8,128)S(1)}) custom-call(s32[4,27]{1,0:T(4,128)S(1)} %fusion.1.slots, bf16[4,4,32,512]{3,2,1,0:T(8,128)(2,1)S(1)} %bitcast.10, bf16[27,64,128]{2,1,0:T(8,128)(2,1)S(1)} %bitcast.12, ...), custom_call_target="tpu_custom_call" | custom-call | flops 1000000000 | bytes 4000000 | tf_op jit(solution)/shard_map/pallas_call | solution.py:243
  28.8 0.0 collective-permute-done.from_partner
  28.8 0.3 collective-permute-done.1.from_across
  29.1 4.1 %shard_map.78 = (bf16[4,64,512]{2,1,0:T(8,128)(2,1)}, bf16[192,1280]{1,0:T(8,128)(2,1)S(1)}, bf16[112,16,128]{2,1,0:T(8,128)(2,1)}) custom-call(s32[4,27]{1,0:T(4,128)S(1)} %fusion.1.slots, bf16[4,4,32,512]{3,2,1,0:T(8,128)(2,1)S(1)} %bitcast.11, bf16[128,512]{1,0:T(8,128)(2,1)S(1)} %collective-permute-done.from_partner, ...), custom_call_target="tpu_custom_call" | custom-call | flops 1000000000 | bytes 4000000 | tf_op jit(solution)/shard_map/pallas_call | solution.py:261
  33.2 8.8 %all-to-all-start = ((bf16[16,7,16,128]{3,2,1,0:T(8,128)(2,1)}), bf16[16,7,16,128]{3,2,1,0:T(8,128)(2,1)S(1)}, u32[]{:S(2)}, u32[]{:S(2)}) async-start(bf16[16,7,16,128]{3,2,1,0:T(8,128)(2,1)} %bitcast.3), calls=%async_computation | async-start | bytes 917504 | tf_op jit(solution)/shard_map/all_to_all | solution.py:363
  42.0 4.0 %shard_map.79 = (f32[6,32,512]{2,1,0:T(8,128)S(1)}, bf16[6,32,512]{2,1,0:T(8,128)(2,1)S(1)}, bf16[6,32,512]{2,1,0:T(8,128)(2,1)S(1)}, bf16[6,32,512]{2,1,0:T(8,128)(2,1)S(1)}) custom-call(s32[4,27]{1,0:T(4,128)S(1)} %fusion.1.slots, s32[1]{0:T(128)} %bitcast.4.place, bf16[192,1152]{1,0:T(8,128)(2,1)S(1)} %get-tuple-element.31.stacked, ...), custom_call_target="tpu_custom_call" | custom-call | flops 2000000000 | bytes 8000000 | tf_op jit(solution)/shard_map/pallas_call | solution.py:279
  46.0 3.5 %collective-permute-start.2 = (bf16[6,32,512]{2,1,0:T(8,128)(2,1)S(1)}, bf16[6,32,512]{2,1,0:T(8,128)(2,1)S(1)}, u32[]{:S(2)}, u32[]{:S(2)}) collective-permute-start(bf16[6,32,512]{2,1,0:T(8,128)(2,1)S(1)} %get-tuple-element.38), channel_id=1, source_target_pairs={{0,1},{1,2},{2,3},{3,0},{4,5},{5,6},{6,7},{7,4},{8,9},{9,10},{10,1... | collective-permute-start | bytes 589832 | tf_op jit(solution)/shard_map/ppermute | solution.py:422
  49.5 6.3 %collective-permute-done.2.refs_0_ = bf16[6,32,512]{2,1,0:T(8,128)(2,1)S(1)} collective-permute-done((bf16[6,32,512]{2,1,0:T(8,128)(2,1)S(1)}, bf16[6,32,512]{2,1,0:T(8,128)(2,1)S(1)}, u32[]{:S(2)}, u32[]{:S(2)}) %collective-permute-start.2) | collective-permute-done | bytes 196640 | tf_op jit(solution)/shard_map/ppermute | solution.py:422
  55.7 0.0 all-to-all-done.pieces
  55.8 0.8 shard_map.80
  56.5 6.6 %all-to-all-start.1 = ((bf16[8,7,16,128]{3,2,1,0:T(8,128)(2,1)}), bf16[8,7,16,128]{3,2,1,0:T(8,128)(2,1)S(1)}, u32[]{:S(2)}, u32[]{:S(2)}) async-start(bf16[8,7,16,128]{3,2,1,0:T(8,128)(2,1)} %shard_map.80), calls=%async_computation.1 | async-start | bytes 458752 | tf_op jit(solution)/shard_map/all_to_all | solution.py:363
  63.1 2.6 %collective-permute-start.3 = (bf16[6,32,512]{2,1,0:T(8,128)(2,1)S(1)}, bf16[6,32,512]{2,1,0:T(8,128)(2,1)S(1)}, u32[]{:S(2)}, u32[]{:S(2)}) collective-permute-start(bf16[6,32,512]{2,1,0:T(8,128)(2,1)S(1)} %get-tuple-element.44), channel_id=1, source_target_pairs={{0,2},{1,3},{2,0},{3,1},{4,6},{5,7},{6,4},{7,5},{8,10},{9,11},{10,... | collective-permute-start | bytes 589832 | tf_op jit(solution)/shard_map/ppermute | solution.py:425
  65.7 3.7 %collective-permute-start.4 = (bf16[6,32,512]{2,1,0:T(8,128)(2,1)S(1)}, bf16[6,32,512]{2,1,0:T(8,128)(2,1)S(1)}, u32[]{:S(2)}, u32[]{:S(2)}) collective-permute-start(bf16[6,32,512]{2,1,0:T(8,128)(2,1)S(1)} %get-tuple-element.45), channel_id=1, source_target_pairs={{0,3},{1,0},{2,1},{3,2},{4,7},{5,4},{6,5},{7,6},{8,11},{9,8},{10,9... | collective-permute-start | bytes 589832 | tf_op jit(solution)/shard_map/ppermute | solution.py:425
  69.5 2.4 %collective-permute-done.3.refs_1_ = bf16[6,32,512]{2,1,0:T(8,128)(2,1)S(1)} collective-permute-done((bf16[6,32,512]{2,1,0:T(8,128)(2,1)S(1)}, bf16[6,32,512]{2,1,0:T(8,128)(2,1)S(1)}, u32[]{:S(2)}, u32[]{:S(2)}) %collective-permute-start.3) | collective-permute-done | bytes 196640 | tf_op jit(solution)/shard_map/ppermute | solution.py:425
  71.8 3.0 %collective-permute-done.4.refs_2_ = bf16[6,32,512]{2,1,0:T(8,128)(2,1)S(1)} collective-permute-done((bf16[6,32,512]{2,1,0:T(8,128)(2,1)S(1)}, bf16[6,32,512]{2,1,0:T(8,128)(2,1)S(1)}, u32[]{:S(2)}, u32[]{:S(2)}) %collective-permute-start.4) | collective-permute-done | bytes 196640 | tf_op jit(solution)/shard_map/ppermute | solution.py:425
  74.8 4.6 %all-to-all-done.1.pieces = bf16[8,7,16,128]{3,2,1,0:T(8,128)(2,1)S(1)} async-done(((bf16[8,7,16,128]{3,2,1,0:T(8,128)(2,1)}), bf16[8,7,16,128]{3,2,1,0:T(8,128)(2,1)S(1)}, u32[]{:S(2)}, u32[]{:S(2)}) %all-to-all-start.1) | async-done | bytes 229408 | tf_op jit(solution)/shard_map/all_to_all | solution.py:363
  79.4 0.8 shard_map.83
  80.2 9.5 %all-to-all-start.2 = ((bf16[16,7,16,128]{3,2,1,0:T(8,128)(2,1)}), bf16[16,7,16,128]{3,2,1,0:T(8,128)(2,1)S(1)}, u32[]{:S(2)}, u32[]{:S(2)}) async-start(bf16[16,7,16,128]{3,2,1,0:T(8,128)(2,1)} %shard_map.83), calls=%async_computation.2 | async-start | bytes 917504 | tf_op jit(solution)/shard_map/all_to_all | solution.py:363
  89.8 0.1 shard_map.81
  89.9 2.0 %collective-permute-start.5 = (bf16[32,512]{1,0:T(8,128)(2,1)S(1)}, bf16[32,512]{1,0:T(8,128)(2,1)S(1)}, u32[]{:S(2)}, u32[]{:S(2)}) collective-permute-start(bf16[32,512]{1,0:T(8,128)(2,1)S(1)} %get-tuple-element.50), channel_id=1, source_target_pairs={{0,4},{4,0},{8,12},{12,8},{16,20},{20,16},{24,28},{28,24},{32,36},... | collective-permute-start | bytes 98312 | tf_op jit(solution)/shard_map/ppermute | solution.py:429
  91.9 3.6 %collective-permute-start.6 = (bf16[32,512]{1,0:T(8,128)(2,1)S(1)}, bf16[32,512]{1,0:T(8,128)(2,1)S(1)}, u32[]{:S(2)}, u32[]{:S(2)}) collective-permute-start(bf16[32,512]{1,0:T(8,128)(2,1)S(1)} %get-tuple-element.51), channel_id=1, source_target_pairs={{4,8},{8,4},{12,16},{16,12},{20,24},{24,20},{28,32},{32,28},{36,40... | collective-permute-start | bytes 98312 | tf_op jit(solution)/shard_map/ppermute | solution.py:430
  95.5 0.0 collective-permute-done.5.from_partner
  95.5 2.1 %collective-permute-done.6.from_across = bf16[32,512]{1,0:T(8,128)(2,1)S(1)} collective-permute-done((bf16[32,512]{1,0:T(8,128)(2,1)S(1)}, bf16[32,512]{1,0:T(8,128)(2,1)S(1)}, u32[]{:S(2)}, u32[]{:S(2)}) %collective-permute-start.6) | collective-permute-done | bytes 32800 | tf_op jit(solution)/shard_map/ppermute | solution.py:430
  97.6 0.7 shard_map.82
  98.3 0.6 all-to-all-done.2
  98.9 1.0 convert_multiply_fusion
  (1 shorter events, 0.0 us)
Async XLA Ops:
  0.6 11.4 %copy-start = (s32[4,512]{1,0:T(4,128)S(1)}, s32[4,512]{1,0:T(4,128)}, u32[]{:S(2)}) copy-start(s32[4,512]{1,0:T(4,128)} %occupancy.7) | copy-start | bytes 24580
  0.7 24.9 %copy-start.2 = (bf16[4,64,512]{2,1,0:T(8,128)(2,1)S(1)}, bf16[4,64,512]{2,1,0:T(8,128)(2,1)}, u32[]{:S(2)}) copy-start(bf16[4,64,512]{2,1,0:T(8,128)(2,1)} %cotangent.3) | copy-start | bytes 786436
  12.1 13.5 %copy-start.1 = (bf16[64,27,128]{2,0,1:T(8,128)(2,1)S(1)}, bf16[64,27,128]{2,0,1:T(8,128)(2,1)}, u32[]{:S(2)}) copy-start(bf16[64,27,128]{2,0,1:T(8,128)(2,1)} %param.7) | copy-start | bytes 1327108
  12.2 16.6 %collective-permute-start = (bf16[128,512]{1,0:T(8,128)(2,1)S(1)}, bf16[128,512]{1,0:T(8,128)(2,1)S(1)}, u32[]{:S(2)}, u32[]{:S(2)}) collective-permute-start(bf16[128,512]{1,0:T(8,128)(2,1)S(1)} %get-tuple-element.28), channel_id=1, source_target_pairs={{0,4},{4,0},{8,12},{12,8},{16,20},{20,16},{24,28},{28,24},{32,36},... | collective-permute-start | bytes 393224 | tf_op jit(solution)/shard_map/ppermute | solution.py:391
  22.8 6.3 %collective-permute-start.1 = (bf16[128,512]{1,0:T(8,128)(2,1)S(1)}, bf16[128,512]{1,0:T(8,128)(2,1)S(1)}, u32[]{:S(2)}, u32[]{:S(2)}) collective-permute-start(bf16[128,512]{1,0:T(8,128)(2,1)S(1)} %get-tuple-element.29), channel_id=1, source_target_pairs={{4,8},{8,4},{12,16},{16,12},{20,24},{24,20},{28,32},{32,28},{36,40... | collective-permute-start | bytes 393224 | tf_op jit(solution)/shard_map/ppermute | solution.py:391
  24.7 0.7 copy-start.3
  33.2 22.6 %all-to-all-start = ((bf16[16,7,16,128]{3,2,1,0:T(8,128)(2,1)}), bf16[16,7,16,128]{3,2,1,0:T(8,128)(2,1)S(1)}, u32[]{:S(2)}, u32[]{:S(2)}) async-start(bf16[16,7,16,128]{3,2,1,0:T(8,128)(2,1)} %bitcast.3), calls=%async_computation | async-start | bytes 917504 | tf_op jit(solution)/shard_map/all_to_all | solution.py:363
  46.0 9.7 %collective-permute-start.2 = (bf16[6,32,512]{2,1,0:T(8,128)(2,1)S(1)}, bf16[6,32,512]{2,1,0:T(8,128)(2,1)S(1)}, u32[]{:S(2)}, u32[]{:S(2)}) collective-permute-start(bf16[6,32,512]{2,1,0:T(8,128)(2,1)S(1)} %get-tuple-element.38), channel_id=1, source_target_pairs={{0,1},{1,2},{2,3},{3,0},{4,5},{5,6},{6,7},{7,4},{8,9},{9,10},{10,1... | collective-permute-start | bytes 589832 | tf_op jit(solution)/shard_map/ppermute | solution.py:422
  56.5 22.9 %all-to-all-start.1 = ((bf16[8,7,16,128]{3,2,1,0:T(8,128)(2,1)}), bf16[8,7,16,128]{3,2,1,0:T(8,128)(2,1)S(1)}, u32[]{:S(2)}, u32[]{:S(2)}) async-start(bf16[8,7,16,128]{3,2,1,0:T(8,128)(2,1)} %shard_map.80), calls=%async_computation.1 | async-start | bytes 458752 | tf_op jit(solution)/shard_map/all_to_all | solution.py:363
  63.1 8.7 %collective-permute-start.3 = (bf16[6,32,512]{2,1,0:T(8,128)(2,1)S(1)}, bf16[6,32,512]{2,1,0:T(8,128)(2,1)S(1)}, u32[]{:S(2)}, u32[]{:S(2)}) collective-permute-start(bf16[6,32,512]{2,1,0:T(8,128)(2,1)S(1)} %get-tuple-element.44), channel_id=1, source_target_pairs={{0,2},{1,3},{2,0},{3,1},{4,6},{5,7},{6,4},{7,5},{8,10},{9,11},{10,... | collective-permute-start | bytes 589832 | tf_op jit(solution)/shard_map/ppermute | solution.py:425
  65.7 9.1 %collective-permute-start.4 = (bf16[6,32,512]{2,1,0:T(8,128)(2,1)S(1)}, bf16[6,32,512]{2,1,0:T(8,128)(2,1)S(1)}, u32[]{:S(2)}, u32[]{:S(2)}) collective-permute-start(bf16[6,32,512]{2,1,0:T(8,128)(2,1)S(1)} %get-tuple-element.45), channel_id=1, source_target_pairs={{0,3},{1,0},{2,1},{3,2},{4,7},{5,4},{6,5},{7,6},{8,11},{9,8},{10,9... | collective-permute-start | bytes 589832 | tf_op jit(solution)/shard_map/ppermute | solution.py:425
  80.2 18.6 %all-to-all-start.2 = ((bf16[16,7,16,128]{3,2,1,0:T(8,128)(2,1)}), bf16[16,7,16,128]{3,2,1,0:T(8,128)(2,1)S(1)}, u32[]{:S(2)}, u32[]{:S(2)}) async-start(bf16[16,7,16,128]{3,2,1,0:T(8,128)(2,1)} %shard_map.83), calls=%async_computation.2 | async-start | bytes 917504 | tf_op jit(solution)/shard_map/all_to_all | solution.py:363
  89.9 5.6 %collective-permute-start.5 = (bf16[32,512]{1,0:T(8,128)(2,1)S(1)}, bf16[32,512]{1,0:T(8,128)(2,1)S(1)}, u32[]{:S(2)}, u32[]{:S(2)}) collective-permute-start(bf16[32,512]{1,0:T(8,128)(2,1)S(1)} %get-tuple-element.50), channel_id=1, source_target_pairs={{0,4},{4,0},{8,12},{12,8},{16,20},{20,16},{24,28},{28,24},{32,36},... | collective-permute-start | bytes 98312 | tf_op jit(solution)/shard_map/ppermute | solution.py:429
  91.9 5.7 %collective-permute-start.6 = (bf16[32,512]{1,0:T(8,128)(2,1)S(1)}, bf16[32,512]{1,0:T(8,128)(2,1)S(1)}, u32[]{:S(2)}, u32[]{:S(2)}) collective-permute-start(bf16[32,512]{1,0:T(8,128)(2,1)S(1)} %get-tuple-element.51), channel_id=1, source_target_pairs={{4,8},{8,4},{12,16},{16,12},{20,24},{24,20},{28,32},{32,28},{36,40... | collective-permute-start | bytes 98312 | tf_op jit(solution)/shard_map/ppermute | solution.py:430

commit v5 on v4

--- a/solution.py
+++ b/solution.py
@@ -26,9 +26,21 @@
     return [(1 + i, i) for i in range(8)]
 
 
-def fill_cube(slots, block, voxels, cube, base):
+def slot_of(spot, listed, block, number, blocks):
+    if number == 13:
+        return block
+    name = listed[block, number if number < 13 else number - 1]
+    local = name - spot[0] * blocks
+    is_even = spot[1] == 1
+    below = jnp.where(is_even, blocks + 1, blocks)
+    above = jnp.where(is_even, blocks, blocks + 1)
+    local = jnp.where(local == -1, below, jnp.where(local == blocks, above, local))
+    return jnp.where(name < 0, blocks + 2, local)
+
+
+def fill_cube(spot, listed, block, blocks, voxels, cube, base):
     for number, (a, b, c) in enumerate(OFFSETS):
-        first = pl.multiple_of(slots[block, number] * 512, 512)
+        first = pl.multiple_of(slot_of(spot, listed, block, number, blocks) * 512, 512)
         for i_to, i_from in spans(a):
             if c == 0:
                 for j_to, j_from in spans(b):
@@ -68,19 +80,19 @@
     return block.astype(F32) * occupancy[slot : slot + 1, :].astype(F32)
 
 
-def rim_kernel(even, gathered, occupancy, to_partner, to_across):
+def rim_kernel(spot, gathered, occupancy, to_partner, to_across):
     first = load_block(gathered, occupancy, 0).astype(BF16)
     last = load_block(gathered, occupancy, gathered.shape[1] - 1).astype(BF16)
-    is_even = even[0] == 1
+    is_even = spot[1] == 1
     to_partner[...] = jnp.where(is_even, last, first)
     to_across[...] = jnp.where(is_even, first, last)
 
 
 def forward_block(
-    slots, block, stacked, cotangent, occupancy, voxels, cube, patches, grads, place
+    spot, listed, block, stacked, cotangent, occupancy, voxels, cube, patches, grads, place
 ):
     base, top = place * CUBE, place * WIDE
-    fill_cube(slots, block, voxels, cube, base)
+    fill_cube(spot, listed, block, cotangent.shape[0], voxels, cube, base)
     pack_patches(cube, base, patches, top)
     wide = lax.dot_general(
         stacked[...], patches[top : top + WIDE, :], NT, preferred_element_type=F32
@@ -111,7 +123,7 @@
 
 
 def inner_kernel(
-    slots, gathered, weight, cotangent, occupancy,
+    spot, listed, gathered, weight, cotangent, occupancy,
     activation, stacked, grads, product,
     voxels, cube, patches,
 ):
@@ -123,7 +135,8 @@
     own_voxels(gathered, occupancy, voxels)
     for block in range(1, blocks - 1):
         activation[block - 1] = forward_block(
-            slots, block, stacked, cotangent, occupancy, voxels, cube, patches, grads, block - 1
+            spot, listed, block, stacked, cotangent, occupancy, voxels, cube, patches, grads,
+            block - 1,
         )
     for first in range(0, 9, 2):
         lanes = slice(first * 128, min(first + 2, 9) * 128)
@@ -131,7 +144,7 @@
 
 
 def outer_kernel(
-    slots, gathered, from_partner, from_across, cotangent, occupancy, inner, stacked, product,
+    spot, listed, gathered, from_partner, from_across, cotangent, occupancy, inner, stacked, product,
     activation, grads, tiles,
     voxels, cube, patches,
 ):
@@ -142,7 +155,7 @@
     activation[1 : blocks - 1] = inner[...]
     for place, block in enumerate((0, blocks - 1)):
         activation[block] = forward_block(
-            slots, block, stacked, cotangent, occupancy, voxels, cube, patches, grads, place
+            spot, listed, block, stacked, cotangent, occupancy, voxels, cube, patches, grads, place
         )
     for first in range(0, 9, 2):
         count = min(2, 9 - first)
@@ -158,14 +171,9 @@
         tiles[t] = jnp.zeros((16, 128), BF16)
 
 
-def backward_kernel(
-    blocks, slots, place, stacked, inner, outer, mine, *rest
-):
-    sends, (sums, wide, turned) = rest[:-3], rest[-3:]
-    sums[...] = jnp.zeros_like(sums)
+def add_gradients(spot, listed, picked, blocks, stacked, grads, sums, wide):
     edge = lax.broadcasted_iota(jnp.int32, (8, 128), 0)
-    for p in range(blocks):
-        grads, at = (inner, p - 1) if 0 < p < blocks - 1 else (outer, min(p, 1))
+    for at, p in enumerate(picked):
         turn = grads[:, at * WIDE : (at + 1) * WIDE].astype(F32).T.astype(BF16)
         wide[...] = jnp.dot(turn, stacked[...], preferred_element_type=F32)
         for i in range(10):
@@ -198,27 +206,49 @@
                         ]
                     part = parts[0] if len(parts) == 1 else jnp.concatenate(parts, axis=0)
                     number = 9 * (a + 1) + 3 * (b + 1) + c + 1
-                    first = pl.multiple_of(slots[p, number] * 512, 512)
+                    slot = slot_of(spot, listed, p, number, blocks)
+                    first = pl.multiple_of(slot * 512, 512)
                     rows = pl.ds(first + i_to * 64 + j_to * 8, 8 * len(js))
                     sums[rows, :] = sums[rows, :] + part
-    count, share = len(sends) + 1, mine.shape[1]
-    for slot in range(blocks + 2):
-        turned[slot * 128 : (slot + 1) * 128, :] = sums[slot * 512 : (slot + 1) * 512, :].T
+
+
+def outer_gradient_kernel(blocks, spot, listed, stacked, grads, own, to_partner, to_across, sums, wide):
+    sums[...] = jnp.zeros_like(sums)
+    add_gradients(spot, listed, (0, blocks - 1), blocks, stacked, grads, sums, wide)
+    own[...] = sums[0 : blocks * 512, :]
+    for slot, rim in ((blocks, to_partner), (blocks + 1, to_across)):
+        rim[...] = sums[slot * 512 : (slot + 1) * 512, :].T.astype(BF16)
+
+
+def inner_gradient_kernel(blocks, spot, listed, stacked, grads, outer, turned, sums, wide):
+    sums[0 : blocks * 512, :] = outer[...]
+    add_gradients(spot, listed, range(1, blocks - 1), blocks, stacked, grads, sums, wide)
+    for slot in range(blocks):
+        turned[slot] = sums[slot * 512 : (slot + 1) * 512, :].T
+
+
+def share_kernel(spot, turned, from_partner, from_across, mine, *rest):
+    sends, total = rest[:-1], rest[-1]
+    blocks, count, share = turned.shape[0], len(sends) + 1, mine.shape[1]
+    is_even = spot[1] == 1
+    partner, across = from_partner[...].astype(F32), from_across[...].astype(F32)
+    total[...] = turned[...]
+    total[0] += jnp.where(is_even, across, partner)
+    total[blocks - 1] += jnp.where(is_even, partner, across)
     for shift in range(count):
-        row = pl.multiple_of(lax.rem(place[0] + shift, count) * share, share)
-        for slot in range(blocks + 2):
-            piece = turned[pl.ds(slot * 128 + row, share), :]
-            if shift == 0:
-                mine[slot] = piece
-            else:
-                sends[shift - 1][slot] = piece.astype(BF16)
+        row = pl.multiple_of(lax.rem(spot[2] + shift, count) * share, share)
+        piece = total[:, pl.ds(row, share), :]
+        if shift == 0:
+            mine[...] = piece
+        else:
+            sends[shift - 1][...] = piece.astype(BF16)
 
 
 def shape(*dims, dtype=BF16):
     return jax.ShapeDtypeStruct(dims, dtype)
 
 
-def call_rims(even, gathered, occupancy):
+def call_rims(spot, gathered, occupancy):
     rim = shape(128, 512)
     return pl.pallas_call(
         rim_kernel,
@@ -227,7 +257,7 @@
         out_specs=[VMEM] * 2,
         compiler_params=PARAMS,
         cost_estimate=pl.CostEstimate(flops=10**6, bytes_accessed=10**6, transcendentals=0),
-    )(even, gathered, occupancy)
+    )(spot, gathered, occupancy)
 
 
 def scratch_of(blocks, count):
@@ -238,7 +268,7 @@
     ]
 
 
-def call_inner(slots, gathered, weight, cotangent, occupancy):
+def call_inner(spot, listed, gathered, weight, cotangent, occupancy):
     blocks, out = cotangent.shape[:2]
     return pl.pallas_call(
         inner_kernel,
@@ -248,15 +278,15 @@
             shape(3 * out, (blocks - 2) * WIDE),
             shape(3 * out, 1152, dtype=F32),
         ],
-        in_specs=[SMEM] + [VMEM] * 4,
+        in_specs=[SMEM] * 2 + [VMEM] * 4,
         out_specs=[VMEM] * 4,
         scratch_shapes=scratch_of(blocks, blocks - 2),
         compiler_params=PARAMS,
         cost_estimate=pl.CostEstimate(flops=10**9, bytes_accessed=4 * 10**6, transcendentals=10**5),
-    )(slots, gathered, weight, cotangent, occupancy)
-
-
-def call_outer(slots, gathered, rims, cotangent, occupancy, inner, stacked, product, tiles):
+    )(spot, listed, gathered, weight, cotangent, occupancy)
+
+
+def call_outer(spot, listed, gathered, rims, cotangent, occupancy, inner, stacked, product, tiles):
     blocks, out = cotangent.shape[:2]
     return pl.pallas_call(
         outer_kernel,
@@ -265,30 +295,58 @@
             shape(3 * out, 2 * WIDE),
             shape(tiles, 16, 128),
         ],
-        in_specs=[SMEM] + [VMEM] * 8,
+        in_specs=[SMEM] * 2 + [VMEM] * 8,
         out_specs=[VMEM] * 3,
         scratch_shapes=scratch_of(blocks, 2),
         compiler_params=PARAMS,
         cost_estimate=pl.CostEstimate(flops=10**9, bytes_accessed=4 * 10**6, transcendentals=10**5),
-    )(slots, gathered, *rims, cotangent, occupancy, inner, stacked, product)
-
-
-def call_backward(slots, place, stacked, inner, outer, chan):
-    blocks = slots.shape[0]
-    piece = (blocks + 2, 128 // chan, 512)
-    return pl.pallas_call(
-        functools.partial(backward_kernel, blocks),
-        out_shape=[shape(*piece, dtype=F32)] + [shape(*piece)] * (chan - 1),
-        in_specs=[SMEM, SMEM, VMEM, VMEM, VMEM],
-        out_specs=[VMEM] * chan,
+    )(spot, listed, gathered, *rims, cotangent, occupancy, inner, stacked, product)
+
+
+def call_outer_gradient(spot, listed, stacked, grads):
+    blocks = listed.shape[0]
+    rim = shape(128, 512)
+    return pl.pallas_call(
+        functools.partial(outer_gradient_kernel, blocks),
+        out_shape=[shape(blocks * 512, 128, dtype=F32), rim, rim],
+        in_specs=[SMEM, SMEM, VMEM, VMEM],
+        out_specs=[VMEM] * 3,
         scratch_shapes=[
             pltpu.VMEM(((blocks + 3) * 512, 128), F32),
             pltpu.VMEM((WIDE, 1152), F32),
-            pltpu.VMEM(((blocks + 2) * 128, 512), F32),
         ],
         compiler_params=PARAMS,
-        cost_estimate=pl.CostEstimate(flops=2 * 10**9, bytes_accessed=8 * 10**6, transcendentals=0),
-    )(slots, place, stacked, inner, outer)
+        cost_estimate=pl.CostEstimate(flops=10**9, bytes_accessed=8 * 10**6, transcendentals=0),
+    )(spot, listed, stacked, grads)
+
+
+def call_inner_gradient(spot, listed, stacked, grads, outer):
+    blocks = listed.shape[0]
+    return pl.pallas_call(
+        functools.partial(inner_gradient_kernel, blocks),
+        out_shape=shape(blocks, 128, 512, dtype=F32),
+        in_specs=[SMEM, SMEM, VMEM, VMEM, VMEM],
+        out_specs=VMEM,
+        scratch_shapes=[
+            pltpu.VMEM(((blocks + 3) * 512, 128), F32),
+            pltpu.VMEM((WIDE, 1152), F32),
+        ],
+        compiler_params=PARAMS,
+        cost_estimate=pl.CostEstimate(flops=10**9, bytes_accessed=8 * 10**6, transcendentals=0),
+    )(spot, listed, stacked, grads, outer)
+
+
+def call_share(spot, turned, rims, chan):
+    piece = (turned.shape[0], 128 // chan, 512)
+    return pl.pallas_call(
+        share_kernel,
+        out_shape=[shape(*piece, dtype=F32)] + [shape(*piece)] * (chan - 1),
+        in_specs=[SMEM] + [VMEM] * 3,
+        out_specs=[VMEM] * chan,
+        scratch_shapes=[pltpu.VMEM(turned.shape, F32)],
+        compiler_params=PARAMS,
+        cost_estimate=pl.CostEstimate(flops=10**7, bytes_accessed=4 * 10**6, transcendentals=0),
+    )(spot, turned, *rims)
 
 
 def add_kernel(copies, pieces, out):
@@ -309,50 +367,23 @@
     )(pieces)
 
 
-def sum_kernel(blocks, mine, *refs):
-    arrived, (own, to_partner, to_across) = refs[:-3], refs[-3:]
-    for slot in range(blocks + 2):
+def final_kernel(occupancy, mine, *refs):
+    arrived, out = refs[:-1], refs[-1]
+    for slot in range(out.shape[0]):
         total = mine[slot]
         for ref in arrived:
             total = total + ref[slot].astype(F32)
-        if slot < blocks:
-            own[slot] = total
-        else:
-            (to_partner if slot == blocks else to_across)[...] = total.astype(BF16)
-
-
-def call_sum(mine, arrived):
-    blocks, rim = mine.shape[0] - 2, mine.shape[1:]
-    return pl.pallas_call(
-        functools.partial(sum_kernel, blocks),
-        out_shape=[shape(blocks, *rim, dtype=F32), shape(*rim), shape(*rim)],
-        in_specs=[VMEM] * (1 + len(arrived)),
-        out_specs=[VMEM] * 3,
-        compiler_params=PARAMS,
-    )(mine, *arrived)
-
-
-def final_kernel(even, own, from_partner, from_across, occupancy, out):
-    blocks = own.shape[0]
-    is_even = even[0] == 1
-    partner, across = from_partner[...].astype(F32), from_across[...].astype(F32)
-    for slot in range(blocks):
-        total = own[slot]
-        if slot == 0:
-            total = total + jnp.where(is_even, across, partner)
-        if slot == blocks - 1:
-            total = total + jnp.where(is_even, partner, across)
         out[slot] = (total * occupancy[slot : slot + 1, :].astype(F32)).astype(BF16)
 
 
-def call_final(even, own, from_partner, from_across, occupancy):
+def call_final(occupancy, mine, arrived):
     return pl.pallas_call(
         final_kernel,
-        out_shape=shape(*own.shape),
-        in_specs=[SMEM] + [VMEM] * 4,
+        out_shape=shape(*mine.shape),
+        in_specs=[VMEM] * (2 + len(arrived)),
         out_specs=VMEM,
         compiler_params=PARAMS,
-    )(even, own, from_partner, from_across, occupancy)
+    )(occupancy, mine, *arrived)
 
 
 def stages_of(count):
@@ -381,57 +412,41 @@
     near, far = groups_of(space)
     share = -(-108 // len(near[0]))
     place = lax.axis_index("space")
-    even = place % 2 == 0
 
     partner = [(i, i ^ 1) for i in range(space)]
     across = [(i, i - 1 if i % 2 == 0 else i + 1) for i in range(1, space - 1)]
-    even_flag = even.astype(jnp.int32).reshape(1)
+    spot = jnp.stack([place, (place + 1) % 2, lax.axis_index("chan")]).astype(jnp.int32)
     gathered = lax.all_gather(features, "chan", axis=0)
     rims = [
         lax.ppermute(rim, "space", pairs)
-        for rim, pairs in zip(call_rims(even_flag, gathered, occupancy), (partner, across))
+        for rim, pairs in zip(call_rims(spot, gathered, occupancy), (partner, across))
     ]
 
-    ids = jnp.concatenate(
-        [
-            neighbours[:, :13],
-            (place * blocks + jnp.arange(blocks, dtype=jnp.int32))[:, None],
-            neighbours[:, 13:],
-        ],
-        axis=1,
-    )
-    slots = ids - place * blocks
-    below = jnp.where(even, blocks + 1, blocks)
-    above = jnp.where(even, blocks, blocks + 1)
-    slots = jnp.where(slots == -1, below, jnp.where(slots == blocks, above, slots))
-    slots = jnp.where(ids < 0, blocks + 2, slots)
-
     inner, stacked, inner_grads, product = call_inner(
-        slots, gathered, jnp.transpose(weight, (1, 0, 2)), cotangent, occupancy
+        spot, neighbours, gathered, jnp.transpose(weight, (1, 0, 2)), cotangent, occupancy
     )
     activation, outer_grads, tiles = call_outer(
-        slots, gathered, rims, cotangent, occupancy, inner, stacked, product, len(near[0]) * share
+        spot, neighbours, gathered, rims, cotangent, occupancy, inner, stacked, product,
+        len(near[0]) * share,
     )
 
     parts = exchange(tiles.reshape(len(near[0]), share, 16, 128), near)
-    mine, *sends = call_backward(
-        slots, lax.axis_index("chan").astype(jnp.int32).reshape(1), stacked,
-        inner_grads, outer_grads, chan,
-    )
-    rings = [[(c, (c + shift) % chan) for c in range(chan)] for shift in range(1, chan)]
-    arrived = [lax.ppermute(sends[0], "chan", rings[0])]
-    parts, mine, arrived, sends = lax.optimization_barrier((parts, mine, arrived, sends))
+    own, *rims = call_outer_gradient(spot, neighbours, stacked, outer_grads)
+    rims = [lax.ppermute(rim, "space", pairs) for rim, pairs in zip(rims, (partner, across))]
+    turned = call_inner_gradient(spot, neighbours, stacked, inner_grads, own)
+    parts, turned, rims = lax.optimization_barrier((parts, turned, rims))
     parts = exchange(call_add(parts, len(far[0])), far)
-    arrived += [lax.ppermute(piece, "chan", ring) for piece, ring in zip(sends[1:], rings[1:])]
-    parts, arrived = lax.optimization_barrier((parts, arrived))
+    mine, *sends = call_share(spot, turned, rims, chan)
+    arrived = [
+        lax.ppermute(piece, "chan", [(c, (c + shift + 1) % chan) for c in range(chan)])
+        for shift, piece in enumerate(sends)
+    ]
+    parts, arrived[0], arrived[2] = lax.optimization_barrier((parts, arrived[0], arrived[2]))
     total = exchange(call_add(parts, len(near[0])), near)
-    own, rim_partner, rim_across = call_sum(mine, arrived)
-    to_partner = lax.ppermute(rim_partner, "space", partner)
-    to_across = lax.ppermute(rim_across, "space", across)
+    input_grad = call_final(occupancy, mine, arrived)
     total = total.reshape(-1, 16, 128)[:108].astype(F32).reshape(27, out, 128)
     weight_grad = jnp.transpose(total * lax.rsqrt(F32(space * blocks * 512)), (1, 0, 2))
 
-    input_grad = call_final(even_flag, own, to_partner, to_across, occupancy)
     return (activation, input_grad, weight_grad)
 
 

time: 100 us -> 99.2 us (level)
  waiting for transfers between devices: 19.2 us -> 15.1 us
  Pallas kernels: 13.7 us -> 15.4 us
  starting transfers between devices: 52.9 us -> 54.2 us
    ppermute x5 -> x3, starting transfers between devices: 15.4 us -> 9.7 us  [on_device(): lax.ppermute(piece, 'chan', [(c, (c + shift + 1) % chan) for c in range(c...]
    ppermute x5 -> x3, waiting for transfers between devices: 13.8 us -> 8.21 us  [on_device(): lax.ppermute(piece, 'chan', [(c, (c + shift + 1) % chan) for c in range(c...]
    ppermute x2 -> x4, starting transfers between devices: 12.6 us -> 18 us  [on_device(): lax.ppermute(rim, 'space', pairs)]
    all_to_all x3, starting transfers between devices: 24.9 us -> 26.5 us  [exchange(): return lax.all_to_all(pieces, 'space', 0, 0, axis_index_groups=groups)]
    pallas_call x3 -> x4, Pallas kernels: 4.8 us -> 6.24 us  [the longest x1 2.44 us: call_inner_gradient(): pl.pallas_call(functools.partial(inner_gradient_kernel, blocks), out_shap...]
    ppermute x2 -> x4, waiting for transfers between devices: 0.28 us -> 1.45 us  [on_device(): lax.ppermute(rim, 'space', pairs)]
  transfers between devices with their start and end apart: 10 -> 10, of which waited for: 7 -> 6; matrix products, arithmetic and copies ran while one was open for 0% -> 0% of each run, Pallas kernels for 8% -> 9%
where the time goes in v5:
time: 99.2 us; the launch traced here: 98.5 us
  starting transfers between devices  54.2 us (55%)
  Pallas kernels  15.4 us (16%)
  waiting for transfers between devices  15.1 us (15%)
  blocking collectives  11.4 us (11%)
  other arithmetic  1.05 us (1%)
    all_to_all x3, starting transfers between devices, exchange(): return lax.all_to_all(pieces, 'space', 0, 0, axis_index_groups=groups)  26.5 us
    ppermute x4, starting transfers between devices, on_device(): lax.ppermute(rim, 'space', pairs)  18 us
    all_gather x1, blocking collectives, on_device(): gathered = lax.all_gather(features, 'chan', axis=0)  11.4 us
    ppermute x3, starting transfers between devices, on_device(): lax.ppermute(piece, 'chan', [(c, (c + shift + 1) % chan) for c in range(c...  9.7 us
    ppermute x3, waiting for transfers between devices, on_device(): lax.ppermute(piece, 'chan', [(c, (c + shift + 1) % chan) for c in range(c...  8.21 us
    all_to_all x3, waiting for transfers between devices, exchange(): return lax.all_to_all(pieces, 'space', 0, 0, axis_index_groups=groups)  5.4 us
    pallas_call x1, Pallas kernels, call_outer(): pl.pallas_call(outer_kernel, out_shape=[shape(blocks, out, 512), shape(3...  3.92 us
    pallas_call x1, Pallas kernels, call_inner(): pl.pallas_call(inner_kernel, out_shape=[shape(blocks - 2, out, 512), shap...  3.1 us
  transfers between devices with their start and end apart: 10, of which 6 were waited for; matrix products, arithmetic and copies ran while one was open for 0% of the time, Pallas kernels for 9%

profile of v5, /device:TPU:1, one launch (start us, length us, event | category | flops | bytes accessed | tf_op | source)
XLA Modules:
  0.0 98.5 jit_solution(4223716096677845268)
XLA Ops:
  0.6 0.0 copy-start.1
  0.6 11.4 %all-gather = bf16[16,32,512]{2,1,0:T(8,128)(2,1)S(1)} all-gather(bf16[4,32,512]{2,1,0:T(8,128)(2,1)} %param.5), channel_id=2, replica_groups=mesh['space'=128,'chan'=4] {'chan'}, dimensions={0}, use_global_device_ids=true | all-gather | bytes 655360 | tf_op jit(solution)/shard_map/all_gather | solution.py:419
  12.1 0.0 copy-start
  12.1 0.1 pad_add_fusion.spot
  12.1 0.6 copy-done
  12.8 0.0 copy-start.2
  12.8 0.6 shard_map.76
  13.4 0.0 copy-start.3
  13.4 10.5 %collective-permute-start = (bf16[128,512]{1,0:T(8,128)(2,1)S(1)}, bf16[128,512]{1,0:T(8,128)(2,1)S(1)}, u32[]{:S(2)}, u32[]{:S(2)}) collective-permute-start(bf16[128,512]{1,0:T(8,128)(2,1)S(1)} %get-tuple-element.26), channel_id=1, source_target_pairs={{0,4},{4,0},{8,12},{12,8},{16,20},{20,16},{24,28},{28,24},{32,36},... | collective-permute-start | bytes 393224 | tf_op jit(solution)/shard_map/ppermute | solution.py:421
  23.9 1.9 %collective-permute-start.1 = (bf16[128,512]{1,0:T(8,128)(2,1)S(1)}, bf16[128,512]{1,0:T(8,128)(2,1)S(1)}, u32[]{:S(2)}, u32[]{:S(2)}) collective-permute-start(bf16[128,512]{1,0:T(8,128)(2,1)S(1)} %get-tuple-element.27), channel_id=1, source_target_pairs={{4,8},{8,4},{12,16},{16,12},{20,24},{24,20},{28,32},{32,28},{36,40... | collective-permute-start | bytes 393224 | tf_op jit(solution)/shard_map/ppermute | solution.py:421
  25.8 0.0 copy-done.1
  25.8 0.0 copy-done.2
  25.8 0.0 copy-done.3
  25.9 3.1 %shard_map.77 = (bf16[2,64,512]{2,1,0:T(8,128)(2,1)S(1)}, bf16[192,1152]{1,0:T(8,128)(2,1)S(1)}, bf16[192,1280]{1,0:T(8,128)(2,1)S(1)}, f32[192,1152]{1,0:T(8,128)S(1)}) custom-call(s32[3]{0:T(128)S(1)} %pad_add_fusion.spot, s32[4,26]{1,0:T(4,128)S(1)} %copy-done.3, bf16[4,4,32,512]{3,2,1,0:T(8,128)(2,1)S(1)} %bitcast.11, bf16[27,64,128]{2,1,0:T(8,128)(2,1)S(1)} %bitcast.13, ...), custom_call_target="tpu_custom_call" | custom-call | flops 1000000000 | bytes 4000000 | tf_op jit(solution)/shard_map/pallas_call | solution.py:273
  29.0 0.0 collective-permute-done.from_partner
  29.0 1.2 %collective-permute-done.1.from_across = bf16[128,512]{1,0:T(8,128)(2,1)S(1)} collective-permute-done((bf16[128,512]{1,0:T(8,128)(2,1)S(1)}, bf16[128,512]{1,0:T(8,128)(2,1)S(1)}, u32[]{:S(2)}, u32[]{:S(2)}) %collective-permute-start.1) | collective-permute-done | bytes 131104 | tf_op jit(solution)/shard_map/ppermute | solution.py:421
  30.2 3.9 %shard_map.78 = (bf16[4,64,512]{2,1,0:T(8,128)(2,1)}, bf16[192,1280]{1,0:T(8,128)(2,1)S(1)}, bf16[112,16,128]{2,1,0:T(8,128)(2,1)}) custom-call(s32[3]{0:T(128)S(1)} %pad_add_fusion.spot, s32[4,26]{1,0:T(4,128)S(1)} %copy-done.3, bf16[4,4,32,512]{3,2,1,0:T(8,128)(2,1)S(1)} %bitcast.12, bf16[128,512]{1,0:T(8,128)(2,1)S(1)} %collective-permute-done.from_partner, ...), custom_call_target="tpu_custom_call" | custom-call | flops 1000000000 | bytes 4000000 | tf_op jit(solution)/shard_map/pallas_call | solution.py:291
  34.1 7.9 %all-to-all-start = ((bf16[16,7,16,128]{3,2,1,0:T(8,128)(2,1)}), bf16[16,7,16,128]{3,2,1,0:T(8,128)(2,1)S(1)}, u32[]{:S(2)}, u32[]{:S(2)}) async-start(bf16[16,7,16,128]{3,2,1,0:T(8,128)(2,1)} %bitcast.5), calls=%async_computation | async-start | bytes 917504 | tf_op jit(solution)/shard_map/all_to_all | solution.py:394
  42.0 2.4 %shard_map.79 = (f32[2048,128]{1,0:T(8,128)S(1)}, bf16[128,512]{1,0:T(8,128)(2,1)S(1)}, bf16[128,512]{1,0:T(8,128)(2,1)S(1)}) custom-call(s32[3]{0:T(128)S(1)} %pad_add_fusion.spot, s32[4,26]{1,0:T(4,128)S(1)} %copy-done.3, bf16[192,1152]{1,0:T(8,128)(2,1)S(1)} %get-tuple-element.29.stacked, bf16[192,1280]{1,0:T(8,128)(2,1)S(1)} %get-tuple-element.34.grads), custom_call_target="tpu_custom_call" | custom-call | flops 1000000000 | bytes 8000000 | tf_op jit(solution)/shard_map/pallas_call | solution.py:309
  44.3 2.0 %collective-permute-start.2 = (bf16[128,512]{1,0:T(8,128)(2,1)S(1)}, bf16[128,512]{1,0:T(8,128)(2,1)S(1)}, u32[]{:S(2)}, u32[]{:S(2)}) collective-permute-start(bf16[128,512]{1,0:T(8,128)(2,1)S(1)} %get-tuple-element.36), channel_id=1, source_target_pairs={{0,4},{4,0},{8,12},{12,8},{16,20},{20,16},{24,28},{28,24},{32,36},... | collective-permute-start | bytes 393224 | tf_op jit(solution)/shard_map/ppermute | solution.py:435
  46.3 3.6 %collective-permute-start.3 = (bf16[128,512]{1,0:T(8,128)(2,1)S(1)}, bf16[128,512]{1,0:T(8,128)(2,1)S(1)}, u32[]{:S(2)}, u32[]{:S(2)}) collective-permute-start(bf16[128,512]{1,0:T(8,128)(2,1)S(1)} %get-tuple-element.37), channel_id=1, source_target_pairs={{4,8},{8,4},{12,16},{16,12},{20,24},{24,20},{28,32},{32,28},{36,40... | collective-permute-start | bytes 393224 | tf_op jit(solution)/shard_map/ppermute | solution.py:435
  49.9 2.4 %shard_map.80.turned = f32[4,128,512]{2,1,0:T(8,128)S(1)} custom-call(s32[3]{0:T(128)S(1)} %pad_add_fusion.spot, s32[4,26]{1,0:T(4,128)S(1)} %copy-done.3, bf16[192,1152]{1,0:T(8,128)(2,1)S(1)} %get-tuple-element.29.stacked, bf16[192,1280]{1,0:T(8,128)(2,1)S(1)} %get-tuple-element.33.grads, f32[2048,128]{1,0:T(8,128)S(1)} %get-tuple-element.35.outer), custom_call_target="tpu_custom_call" | custom-call | flops 1000000000 | bytes 8000000 | tf_op jit(solution)/shard_map/pallas_call | solution.py:325
  52.4 0.0 collective-permute-done.2.from_partner
  52.4 0.2 collective-permute-done.3.from_across
  52.6 0.0 all-to-all-done.pieces
  52.6 0.8 shard_map.82
  53.4 7.9 %all-to-all-start.1 = ((bf16[8,7,16,128]{3,2,1,0:T(8,128)(2,1)}), bf16[8,7,16,128]{3,2,1,0:T(8,128)(2,1)S(1)}, u32[]{:S(2)}, u32[]{:S(2)}) async-start(bf16[8,7,16,128]{3,2,1,0:T(8,128)(2,1)} %shard_map.82), calls=%async_computation.1 | async-start | bytes 458752 | tf_op jit(solution)/shard_map/all_to_all | solution.py:394
  61.3 0.7 shard_map.81
  62.0 3.5 %collective-permute-start.4 = (bf16[4,32,512]{2,1,0:T(8,128)(2,1)S(1)}, bf16[4,32,512]{2,1,0:T(8,128)(2,1)S(1)}, u32[]{:S(2)}, u32[]{:S(2)}) collective-permute-start(bf16[4,32,512]{2,1,0:T(8,128)(2,1)S(1)} %get-tuple-element.43), channel_id=1, source_target_pairs={{0,1},{1,2},{2,3},{3,0},{4,5},{5,6},{6,7},{7,4},{8,9},{9,10},{10,1... | collective-permute-start | bytes 393224 | tf_op jit(solution)/shard_map/ppermute | solution.py:441
  65.5 3.1 %collective-permute-start.5 = (bf16[4,32,512]{2,1,0:T(8,128)(2,1)S(1)}, bf16[4,32,512]{2,1,0:T(8,128)(2,1)S(1)}, u32[]{:S(2)}, u32[]{:S(2)}) collective-permute-start(bf16[4,32,512]{2,1,0:T(8,128)(2,1)S(1)} %get-tuple-element.44), channel_id=1, source_target_pairs={{0,3},{1,0},{2,1},{3,2},{4,7},{5,4},{6,5},{7,6},{8,11},{9,8},{10,9... | collective-permute-start | bytes 393224 | tf_op jit(solution)/shard_map/ppermute | solution.py:441
  68.6 0.4 collective-permute-done.4.refs_0_
  69.0 2.5 %collective-permute-done.5.refs_2_ = bf16[4,32,512]{2,1,0:T(8,128)(2,1)S(1)} collective-permute-done((bf16[4,32,512]{2,1,0:T(8,128)(2,1)S(1)}, bf16[4,32,512]{2,1,0:T(8,128)(2,1)S(1)}, u32[]{:S(2)}, u32[]{:S(2)}) %collective-permute-start.5) | collective-permute-done | bytes 131104 | tf_op jit(solution)/shard_map/ppermute | solution.py:441
  71.5 5.4 %all-to-all-done.1.pieces = bf16[8,7,16,128]{3,2,1,0:T(8,128)(2,1)S(1)} async-done(((bf16[8,7,16,128]{3,2,1,0:T(8,128)(2,1)}), bf16[8,7,16,128]{3,2,1,0:T(8,128)(2,1)S(1)}, u32[]{:S(2)}, u32[]{:S(2)}) %all-to-all-start.1) | async-done | bytes 229408 | tf_op jit(solution)/shard_map/all_to_all | solution.py:394
  76.9 0.8 shard_map.84
  77.7 10.7 %all-to-all-start.2 = ((bf16[16,7,16,128]{3,2,1,0:T(8,128)(2,1)}), bf16[16,7,16,128]{3,2,1,0:T(8,128)(2,1)S(1)}, u32[]{:S(2)}, u32[]{:S(2)}) async-start(bf16[16,7,16,128]{3,2,1,0:T(8,128)(2,1)} %shard_map.84), calls=%async_computation.2 | async-start | bytes 917504 | tf_op jit(solution)/shard_map/all_to_all | solution.py:394
  88.4 3.1 %collective-permute-start.6 = (bf16[4,32,512]{2,1,0:T(8,128)(2,1)S(1)}, bf16[4,32,512]{2,1,0:T(8,128)(2,1)S(1)}, u32[]{:S(2)}, u32[]{:S(2)}) collective-permute-start(bf16[4,32,512]{2,1,0:T(8,128)(2,1)S(1)} %get-tuple-element.46), channel_id=1, source_target_pairs={{0,2},{1,3},{2,0},{3,1},{4,6},{5,7},{6,4},{7,5},{8,10},{9,11},{10,... | collective-permute-start | bytes 393224 | tf_op jit(solution)/shard_map/ppermute | solution.py:441
  91.5 5.3 %collective-permute-done.6.refs_1_ = bf16[4,32,512]{2,1,0:T(8,128)(2,1)S(1)} collective-permute-done((bf16[4,32,512]{2,1,0:T(8,128)(2,1)S(1)}, bf16[4,32,512]{2,1,0:T(8,128)(2,1)S(1)}, u32[]{:S(2)}, u32[]{:S(2)}) %collective-permute-start.6) | collective-permute-done | bytes 131104 | tf_op jit(solution)/shard_map/ppermute | solution.py:441
  96.8 0.7 shard_map.83
  97.6 0.0 all-to-all-done.2
  97.6 1.0 convert_multiply_fusion
Async XLA Ops:
  0.6 25.2 %copy-start.1 = (bf16[64,27,128]{2,0,1:T(8,128)(2,1)S(1)}, bf16[64,27,128]{2,0,1:T(8,128)(2,1)}, u32[]{:S(2)}) copy-start(bf16[64,27,128]{2,0,1:T(8,128)(2,1)} %param.7) | copy-start | bytes 1327108
  12.1 0.7 copy-start
  12.8 13.1 %copy-start.2 = (bf16[4,64,512]{2,1,0:T(8,128)(2,1)S(1)}, bf16[4,64,512]{2,1,0:T(8,128)(2,1)}, u32[]{:S(2)}) copy-start(bf16[4,64,512]{2,1,0:T(8,128)(2,1)} %cotangent.3) | copy-start | bytes 786436
  13.4 12.5 %copy-start.3 = (s32[4,26]{1,0:T(4,128)S(1)}, s32[4,26]{1,0:T(4,128)}, u32[]{:S(2)}) copy-start(s32[4,26]{1,0:T(4,128)} %listed.7) | copy-start | bytes 1252
  13.4 15.6 %collective-permute-start = (bf16[128,512]{1,0:T(8,128)(2,1)S(1)}, bf16[128,512]{1,0:T(8,128)(2,1)S(1)}, u32[]{:S(2)}, u32[]{:S(2)}) collective-permute-start(bf16[128,512]{1,0:T(8,128)(2,1)S(1)} %get-tuple-element.26), channel_id=1, source_target_pairs={{0,4},{4,0},{8,12},{12,8},{16,20},{20,16},{24,28},{28,24},{32,36},... | collective-permute-start | bytes 393224 | tf_op jit(solution)/shard_map/ppermute | solution.py:421
  23.9 6.3 %collective-permute-start.1 = (bf16[128,512]{1,0:T(8,128)(2,1)S(1)}, bf16[128,512]{1,0:T(8,128)(2,1)S(1)}, u32[]{:S(2)}, u32[]{:S(2)}) collective-permute-start(bf16[128,512]{1,0:T(8,128)(2,1)S(1)} %get-tuple-element.27), channel_id=1, source_target_pairs={{4,8},{8,4},{12,16},{16,12},{20,24},{24,20},{28,32},{32,28},{36,40... | collective-permute-start | bytes 393224 | tf_op jit(solution)/shard_map/ppermute | solution.py:421
  34.1 18.5 %all-to-all-start = ((bf16[16,7,16,128]{3,2,1,0:T(8,128)(2,1)}), bf16[16,7,16,128]{3,2,1,0:T(8,128)(2,1)S(1)}, u32[]{:S(2)}, u32[]{:S(2)}) async-start(bf16[16,7,16,128]{3,2,1,0:T(8,128)(2,1)} %bitcast.5), calls=%async_computation | async-start | bytes 917504 | tf_op jit(solution)/shard_map/all_to_all | solution.py:394
  44.3 8.0 %collective-permute-start.2 = (bf16[128,512]{1,0:T(8,128)(2,1)S(1)}, bf16[128,512]{1,0:T(8,128)(2,1)S(1)}, u32[]{:S(2)}, u32[]{:S(2)}) collective-permute-start(bf16[128,512]{1,0:T(8,128)(2,1)S(1)} %get-tuple-element.36), channel_id=1, source_target_pairs={{0,4},{4,0},{8,12},{12,8},{16,20},{20,16},{24,28},{28,24},{32,36},... | collective-permute-start | bytes 393224 | tf_op jit(solution)/shard_map/ppermute | solution.py:435
  46.3 6.3 %collective-permute-start.3 = (bf16[128,512]{1,0:T(8,128)(2,1)S(1)}, bf16[128,512]{1,0:T(8,128)(2,1)S(1)}, u32[]{:S(2)}, u32[]{:S(2)}) collective-permute-start(bf16[128,512]{1,0:T(8,128)(2,1)S(1)} %get-tuple-element.37), channel_id=1, source_target_pairs={{4,8},{8,4},{12,16},{16,12},{20,24},{24,20},{28,32},{32,28},{36,40... | collective-permute-start | bytes 393224 | tf_op jit(solution)/shard_map/ppermute | solution.py:435
  53.4 23.5 %all-to-all-start.1 = ((bf16[8,7,16,128]{3,2,1,0:T(8,128)(2,1)}), bf16[8,7,16,128]{3,2,1,0:T(8,128)(2,1)S(1)}, u32[]{:S(2)}, u32[]{:S(2)}) async-start(bf16[8,7,16,128]{3,2,1,0:T(8,128)(2,1)} %shard_map.82), calls=%async_computation.1 | async-start | bytes 458752 | tf_op jit(solution)/shard_map/all_to_all | solution.py:394
  62.0 7.0 %collective-permute-start.4 = (bf16[4,32,512]{2,1,0:T(8,128)(2,1)S(1)}, bf16[4,32,512]{2,1,0:T(8,128)(2,1)S(1)}, u32[]{:S(2)}, u32[]{:S(2)}) collective-permute-start(bf16[4,32,512]{2,1,0:T(8,128)(2,1)S(1)} %get-tuple-element.43), channel_id=1, source_target_pairs={{0,1},{1,2},{2,3},{3,0},{4,5},{5,6},{6,7},{7,4},{8,9},{9,10},{10,1... | collective-permute-start | bytes 393224 | tf_op jit(solution)/shard_map/ppermute | solution.py:441
  65.5 6.0 %collective-permute-start.5 = (bf16[4,32,512]{2,1,0:T(8,128)(2,1)S(1)}, bf16[4,32,512]{2,1,0:T(8,128)(2,1)S(1)}, u32[]{:S(2)}, u32[]{:S(2)}) collective-permute-start(bf16[4,32,512]{2,1,0:T(8,128)(2,1)S(1)} %get-tuple-element.44), channel_id=1, source_target_pairs={{0,3},{1,0},{2,1},{3,2},{4,7},{5,4},{6,5},{7,6},{8,11},{9,8},{10,9... | collective-permute-start | bytes 393224 | tf_op jit(solution)/shard_map/ppermute | solution.py:441
  77.7 19.9 %all-to-all-start.2 = ((bf16[16,7,16,128]{3,2,1,0:T(8,128)(2,1)}), bf16[16,7,16,128]{3,2,1,0:T(8,128)(2,1)S(1)}, u32[]{:S(2)}, u32[]{:S(2)}) async-start(bf16[16,7,16,128]{3,2,1,0:T(8,128)(2,1)} %shard_map.84), calls=%async_computation.2 | async-start | bytes 917504 | tf_op jit(solution)/shard_map/all_to_all | solution.py:394
  88.4 8.5 %collective-permute-start.6 = (bf16[4,32,512]{2,1,0:T(8,128)(2,1)S(1)}, bf16[4,32,512]{2,1,0:T(8,128)(2,1)S(1)}, u32[]{:S(2)}, u32[]{:S(2)}) collective-permute-start(bf16[4,32,512]{2,1,0:T(8,128)(2,1)S(1)} %get-tuple-element.46), channel_id=1, source_target_pairs={{0,2},{1,3},{2,0},{3,1},{4,6},{5,7},{6,4},{7,5},{8,10},{9,11},{10,... | collective-permute-start | bytes 393224 | tf_op jit(solution)/shard_map/ppermute | solution.py:441

commit v6 on v4

--- a/solution.py
+++ b/solution.py
@@ -13,9 +13,11 @@
 NT = (((1,), (1,)), ((), ()))
 CUBE = 1616
 WIDE = 640
+FLIPS = (2, 1, 3)
 VMEM = pl.BlockSpec(memory_space=pltpu.VMEM)
 SMEM = pl.BlockSpec(memory_space=pltpu.SMEM)
-PARAMS = pltpu.CompilerParams(vmem_limit_bytes=48 * 1024 * 1024)
+PARAMS = pltpu.CompilerParams(vmem_limit_bytes=24 * 1024 * 1024)
+SMALL = pltpu.CompilerParams(vmem_limit_bytes=8 * 1024 * 1024)
 
 
 def spans(shift):
@@ -26,9 +28,21 @@
     return [(1 + i, i) for i in range(8)]
 
 
-def fill_cube(slots, block, voxels, cube, base):
+def slot_of(spot, listed, block, number, blocks):
+    if number == 13:
+        return block
+    name = listed[block, number if number < 13 else number - 1]
+    local = name - spot[0] * blocks
+    is_even = lax.rem(spot[0], 2) == 0
+    below = jnp.where(is_even, blocks + 1, blocks)
+    above = jnp.where(is_even, blocks, blocks + 1)
+    local = jnp.where(local == -1, below, jnp.where(local == blocks, above, local))
+    return jnp.where(name < 0, blocks + 2, local)
+
+
+def fill_cube(spot, listed, block, blocks, voxels, cube, base):
     for number, (a, b, c) in enumerate(OFFSETS):
-        first = pl.multiple_of(slots[block, number] * 512, 512)
+        first = pl.multiple_of(slot_of(spot, listed, block, number, blocks) * 512, 512)
         for i_to, i_from in spans(a):
             if c == 0:
                 for j_to, j_from in spans(b):
@@ -68,19 +82,19 @@
     return block.astype(F32) * occupancy[slot : slot + 1, :].astype(F32)
 
 
-def rim_kernel(even, gathered, occupancy, to_partner, to_across):
+def rim_kernel(spot, gathered, occupancy, to_partner, to_across):
     first = load_block(gathered, occupancy, 0).astype(BF16)
     last = load_block(gathered, occupancy, gathered.shape[1] - 1).astype(BF16)
-    is_even = even[0] == 1
+    is_even = lax.rem(spot[0], 2) == 0
     to_partner[...] = jnp.where(is_even, last, first)
     to_across[...] = jnp.where(is_even, first, last)
 
 
 def forward_block(
-    slots, block, stacked, cotangent, occupancy, voxels, cube, patches, grads, place
+    spot, listed, block, stacked, cotangent, occupancy, voxels, cube, patches, grads, place
 ):
     base, top = place * CUBE, place * WIDE
-    fill_cube(slots, block, voxels, cube, base)
+    fill_cube(spot, listed, block, cotangent.shape[0], voxels, cube, base)
     pack_patches(cube, base, patches, top)
     wide = lax.dot_general(
         stacked[...], patches[top : top + WIDE, :], NT, preferred_element_type=F32
@@ -111,8 +125,8 @@
 
 
 def inner_kernel(
-    slots, gathered, weight, cotangent, occupancy,
-    activation, stacked, grads, product,
+    spot, listed, gathered, weight, cotangent, occupancy,
+    activation, stacked, grads, product, own,
     voxels, cube, patches,
 ):
     blocks = cotangent.shape[0]
@@ -121,9 +135,11 @@
         a, lanes = number // 9, number % 9 * 128
         stacked[a * out : (a + 1) * out, lanes : lanes + 128] = weight[number]
     own_voxels(gathered, occupancy, voxels)
+    own[...] = voxels[0 : blocks * 512, :]
     for block in range(1, blocks - 1):
         activation[block - 1] = forward_block(
-            slots, block, stacked, cotangent, occupancy, voxels, cube, patches, grads, block - 1
+            spot, listed, block, stacked, cotangent, occupancy, voxels, cube, patches, grads,
+            block - 1,
         )
     for first in range(0, 9, 2):
         lanes = slice(first * 128, min(first + 2, 9) * 128)
@@ -131,18 +147,19 @@
 
 
 def outer_kernel(
-    slots, gathered, from_partner, from_across, cotangent, occupancy, inner, stacked, product,
+    spot, listed, own, from_partner, from_across, cotangent, occupancy, inner, stacked, product,
     activation, grads, tiles,
     voxels, cube, patches,
 ):
     blocks = cotangent.shape[0]
-    own_voxels(gathered, occupancy, voxels)
+    voxels[0 : blocks * 512, :] = own[...]
+    voxels[(blocks + 2) * 512 : (blocks + 3) * 512, :] = jnp.zeros((512, 128), F32)
     for slot, rim in ((blocks, from_partner), (blocks + 1, from_across)):
         voxels[slot * 512 : (slot + 1) * 512, :] = rim[...].astype(F32).T
     activation[1 : blocks - 1] = inner[...]
     for place, block in enumerate((0, blocks - 1)):
         activation[block] = forward_block(
-            slots, block, stacked, cotangent, occupancy, voxels, cube, patches, grads, place
+            spot, listed, block, stacked, cotangent, occupancy, voxels, cube, patches, grads, place
         )
     for first in range(0, 9, 2):
         count = min(2, 9 - first)
@@ -158,14 +175,9 @@
         tiles[t] = jnp.zeros((16, 128), BF16)
 
 
-def backward_kernel(
-    blocks, slots, place, stacked, inner, outer, mine, *rest
-):
-    sends, (sums, wide, turned) = rest[:-3], rest[-3:]
-    sums[...] = jnp.zeros_like(sums)
+def add_gradients(spot, listed, picked, blocks, stacked, grads, sums, wide):
     edge = lax.broadcasted_iota(jnp.int32, (8, 128), 0)
-    for p in range(blocks):
-        grads, at = (inner, p - 1) if 0 < p < blocks - 1 else (outer, min(p, 1))
+    for at, p in enumerate(picked):
         turn = grads[:, at * WIDE : (at + 1) * WIDE].astype(F32).T.astype(BF16)
         wide[...] = jnp.dot(turn, stacked[...], preferred_element_type=F32)
         for i in range(10):
@@ -198,36 +210,42 @@
                         ]
                     part = parts[0] if len(parts) == 1 else jnp.concatenate(parts, axis=0)
                     number = 9 * (a + 1) + 3 * (b + 1) + c + 1
-                    first = pl.multiple_of(slots[p, number] * 512, 512)
+                    slot = slot_of(spot, listed, p, number, blocks)
+                    first = pl.multiple_of(slot * 512, 512)
                     rows = pl.ds(first + i_to * 64 + j_to * 8, 8 * len(js))
                     sums[rows, :] = sums[rows, :] + part
-    count, share = len(sends) + 1, mine.shape[1]
+
+
+def backward_kernel(
+    blocks, spot, ring_spot, listed, stacked, inner, outer, mine, *rest
+):
+    sends, (sums, wide, turned) = rest[:-3], rest[-3:]
+    sums[...] = jnp.zeros_like(sums)
+    add_gradients(spot, listed, (0, blocks - 1), blocks, stacked, outer, sums, wide)
+    add_gradients(spot, listed, range(1, blocks - 1), blocks, stacked, inner, sums, wide)
+    share = mine.shape[1]
     for slot in range(blocks + 2):
         turned[slot * 128 : (slot + 1) * 128, :] = sums[slot * 512 : (slot + 1) * 512, :].T
-    for shift in range(count):
-        row = pl.multiple_of(lax.rem(place[0] + shift, count) * share, share)
+    for flip, ref in zip((0,) + FLIPS, (mine,) + tuple(sends)):
+        row = pl.multiple_of((ring_spot[0] ^ flip) * share, share)
         for slot in range(blocks + 2):
-            piece = turned[pl.ds(slot * 128 + row, share), :]
-            if shift == 0:
-                mine[slot] = piece
-            else:
-                sends[shift - 1][slot] = piece.astype(BF16)
+            ref[slot] = turned[pl.ds(slot * 128 + row, share), :].astype(ref.dtype)
 
 
 def shape(*dims, dtype=BF16):
     return jax.ShapeDtypeStruct(dims, dtype)
 
 
-def call_rims(even, gathered, occupancy):
+def call_rims(spot, gathered, occupancy):
     rim = shape(128, 512)
     return pl.pallas_call(
         rim_kernel,
         out_shape=[rim, rim],
         in_specs=[SMEM, VMEM, VMEM],
         out_specs=[VMEM] * 2,
-        compiler_params=PARAMS,
+        compiler_params=SMALL,
         cost_estimate=pl.CostEstimate(flops=10**6, bytes_accessed=10**6, transcendentals=0),
-    )(even, gathered, occupancy)
+    )(spot, gathered, occupancy)
 
 
 def scratch_of(blocks, count):
@@ -238,7 +256,7 @@
     ]
 
 
-def call_inner(slots, gathered, weight, cotangent, occupancy):
+def call_inner(spot, listed, gathered, weight, cotangent, occupancy):
     blocks, out = cotangent.shape[:2]
     return pl.pallas_call(
         inner_kernel,
@@ -247,16 +265,17 @@
             shape(3 * out, 1152),
             shape(3 * out, (blocks - 2) * WIDE),
             shape(3 * out, 1152, dtype=F32),
+            shape(blocks * 512, 128, dtype=F32),
         ],
-        in_specs=[SMEM] + [VMEM] * 4,
-        out_specs=[VMEM] * 4,
+        in_specs=[SMEM] * 2 + [VMEM] * 4,
+        out_specs=[VMEM] * 5,
         scratch_shapes=scratch_of(blocks, blocks - 2),
         compiler_params=PARAMS,
         cost_estimate=pl.CostEstimate(flops=10**9, bytes_accessed=4 * 10**6, transcendentals=10**5),
-    )(slots, gathered, weight, cotangent, occupancy)
-
-
-def call_outer(slots, gathered, rims, cotangent, occupancy, inner, stacked, product, tiles):
+    )(spot, listed, gathered, weight, cotangent, occupancy)
+
+
+def call_outer(spot, listed, own, rims, cotangent, occupancy, inner, stacked, product, tiles):
     blocks, out = cotangent.shape[:2]
     return pl.pallas_call(
         outer_kernel,
@@ -265,21 +284,21 @@
             shape(3 * out, 2 * WIDE),
             shape(tiles, 16, 128),
         ],
-        in_specs=[SMEM] + [VMEM] * 8,
+        in_specs=[SMEM] * 2 + [VMEM] * 8,
         out_specs=[VMEM] * 3,
         scratch_shapes=scratch_of(blocks, 2),
         compiler_params=PARAMS,
         cost_estimate=pl.CostEstimate(flops=10**9, bytes_accessed=4 * 10**6, transcendentals=10**5),
-    )(slots, gathered, *rims, cotangent, occupancy, inner, stacked, product)
-
-
-def call_backward(slots, place, stacked, inner, outer, chan):
-    blocks = slots.shape[0]
+    )(spot, listed, own, *rims, cotangent, occupancy, inner, stacked, product)
+
+
+def call_backward(spot, ring_spot, listed, stacked, inner, outer, chan):
+    blocks = listed.shape[0]
     piece = (blocks + 2, 128 // chan, 512)
     return pl.pallas_call(
         functools.partial(backward_kernel, blocks),
         out_shape=[shape(*piece, dtype=F32)] + [shape(*piece)] * (chan - 1),
-        in_specs=[SMEM, SMEM, VMEM, VMEM, VMEM],
+        in_specs=[SMEM] * 3 + [VMEM] * 3,
         out_specs=[VMEM] * chan,
         scratch_shapes=[
             pltpu.VMEM(((blocks + 3) * 512, 128), F32),
@@ -288,7 +307,7 @@
         ],
         compiler_params=PARAMS,
         cost_estimate=pl.CostEstimate(flops=2 * 10**9, bytes_accessed=8 * 10**6, transcendentals=0),
-    )(slots, place, stacked, inner, outer)
+    )(spot, ring_spot, listed, stacked, inner, outer)
 
 
 def add_kernel(copies, pieces, out):
@@ -305,7 +324,7 @@
         out_shape=shape(copies, *pieces.shape[1:]),
         in_specs=[VMEM],
         out_specs=VMEM,
-        compiler_params=PARAMS,
+        compiler_params=SMALL,
     )(pieces)
 
 
@@ -328,13 +347,13 @@
         out_shape=[shape(blocks, *rim, dtype=F32), shape(*rim), shape(*rim)],
         in_specs=[VMEM] * (1 + len(arrived)),
         out_specs=[VMEM] * 3,
-        compiler_params=PARAMS,
+        compiler_params=SMALL,
     )(mine, *arrived)
 
 
-def final_kernel(even, own, from_partner, from_across, occupancy, out):
+def final_kernel(spot, own, from_partner, from_across, occupancy, out):
     blocks = own.shape[0]
-    is_even = even[0] == 1
+    is_even = lax.rem(spot[0], 2) == 0
     partner, across = from_partner[...].astype(F32), from_across[...].astype(F32)
     for slot in range(blocks):
         total = own[slot]
@@ -345,14 +364,14 @@
         out[slot] = (total * occupancy[slot : slot + 1, :].astype(F32)).astype(BF16)
 
 
-def call_final(even, own, from_partner, from_across, occupancy):
+def call_final(spot, own, from_partner, from_across, occupancy):
     return pl.pallas_call(
         final_kernel,
         out_shape=shape(*own.shape),
         in_specs=[SMEM] + [VMEM] * 4,
         out_specs=VMEM,
-        compiler_params=PARAMS,
-    )(even, own, from_partner, from_across, occupancy)
+        compiler_params=SMALL,
+    )(spot, own, from_partner, from_across, occupancy)
 
 
 def stages_of(count):
@@ -381,48 +400,37 @@
     near, far = groups_of(space)
     share = -(-108 // len(near[0]))
     place = lax.axis_index("space")
-    even = place % 2 == 0
 
     partner = [(i, i ^ 1) for i in range(space)]
     across = [(i, i - 1 if i % 2 == 0 else i + 1) for i in range(1, space - 1)]
-    even_flag = even.astype(jnp.int32).reshape(1)
-    gathered = lax.all_gather(features, "chan", axis=0)
+    spot = place.astype(jnp.int32).reshape(1)
+    ring_spot = lax.axis_index("chan").astype(jnp.int32).reshape(1)
+    gathered = lax.all_to_all(
+        jnp.broadcast_to(features, (chan,) + features.shape), "chan", 0, 0
+    )
     rims = [
         lax.ppermute(rim, "space", pairs)
-        for rim, pairs in zip(call_rims(even_flag, gathered, occupancy), (partner, across))
+        for rim, pairs in zip(call_rims(spot, gathered, occupancy), (partner, across))
     ]
 
-    ids = jnp.concatenate(
-        [
-            neighbours[:, :13],
-            (place * blocks + jnp.arange(blocks, dtype=jnp.int32))[:, None],
-            neighbours[:, 13:],
-        ],
-        axis=1,
-    )
-    slots = ids - place * blocks
-    below = jnp.where(even, blocks + 1, blocks)
-    above = jnp.where(even, blocks, blocks + 1)
-    slots = jnp.where(slots == -1, below, jnp.where(slots == blocks, above, slots))
-    slots = jnp.where(ids < 0, blocks + 2, slots)
-
-    inner, stacked, inner_grads, product = call_inner(
-        slots, gathered, jnp.transpose(weight, (1, 0, 2)), cotangent, occupancy
+    inner, stacked, inner_grads, product, own = call_inner(
+        spot, neighbours, gathered, jnp.transpose(weight, (1, 0, 2)), cotangent, occupancy
     )
     activation, outer_grads, tiles = call_outer(
-        slots, gathered, rims, cotangent, occupancy, inner, stacked, product, len(near[0]) * share
+        spot, neighbours, own, rims, cotangent, occupancy, inner, stacked, product,
+        len(near[0]) * share,
     )
 
     parts = exchange(tiles.reshape(len(near[0]), share, 16, 128), near)
     mine, *sends = call_backward(
-        slots, lax.axis_index("chan").astype(jnp.int32).reshape(1), stacked,
-        inner_grads, outer_grads, chan,
-    )
-    rings = [[(c, (c + shift) % chan) for c in range(chan)] for shift in range(1, chan)]
-    arrived = [lax.ppermute(sends[0], "chan", rings[0])]
-    parts, mine, arrived, sends = lax.optimization_barrier((parts, mine, arrived, sends))
+        spot, ring_spot, neighbours, stacked, inner_grads, outer_grads, chan
+    )
+    parts, mine, sends = lax.optimization_barrier((parts, mine, sends))
     parts = exchange(call_add(parts, len(far[0])), far)
-    arrived += [lax.ppermute(piece, "chan", ring) for piece, ring in zip(sends[1:], rings[1:])]
+    arrived = [
+        lax.ppermute(piece, "chan", [(c, c ^ flip) for c in range(chan)])
+        for flip, piece in zip(FLIPS, sends)
+    ]
     parts, arrived = lax.optimization_barrier((parts, arrived))
     total = exchange(call_add(parts, len(near[0])), near)
     own, rim_partner, rim_across = call_sum(mine, arrived)
@@ -431,7 +439,7 @@
     total = total.reshape(-1, 16, 128)[:108].astype(F32).reshape(27, out, 128)
     weight_grad = jnp.transpose(total * lax.rsqrt(F32(space * blocks * 512)), (1, 0, 2))
 
-    input_grad = call_final(even_flag, own, to_partner, to_across, occupancy)
+    input_grad = call_final(spot, own, to_partner, to_across, occupancy)
     return (activation, input_grad, weight_grad)
 
 

time: 100 us -> 96.7 us (0.967)
  blocking collectives: 11.4 us -> 0 us
  waiting for transfers between devices: 19.2 us -> 23.3 us
  starting transfers between devices: 52.9 us -> 55.8 us
  local copies, waits for them, and re-layouts: 0.75 us -> 1.77 us
    all_gather x1 -> x0, blocking collectives: 11.4 us -> none  [on_device(): gathered = lax.all_gather(features, 'chan', axis=0)]
    ppermute x3, waiting for transfers between devices: 11.6 us -> 4.52 us  [on_device(): lax.ppermute(piece, 'chan', [(c, c ^ flip) for c in range(chan)])]
    all_to_all x0 -> x1, waiting for transfers between devices: none -> 6.93 us  [on_device(): lax.all_to_all(jnp.broadcast_to(features, (chan,) + features.shape), 'cha...]
    all_to_all x0 -> x1, starting transfers between devices: none -> 4.97 us  [on_device(): lax.all_to_all(jnp.broadcast_to(features, (chan,) + features.shape), 'cha...]
    all_to_all x3, waiting for transfers between devices: 5.16 us -> 8.61 us  [exchange(): return lax.all_to_all(pieces, 'space', 0, 0, axis_index_groups=groups)]
    ppermute x2, starting transfers between devices: 12.6 us -> 10.5 us  [on_device(): lax.ppermute(rim, 'space', pairs)]
    broadcast_in_dim x0 -> x1, local copies, waits for them, and re-layouts: none -> 1.75 us  [on_device(): jnp.broadcast_to(features, (chan,) + features.shape)]
  transfers between devices with their start and end apart: 10 -> 11, of which waited for: 7 -> 8; matrix products, arithmetic and copies ran while one was open for 0% -> 0% of each run, Pallas kernels for 8% -> 8%
where the time goes in v6:
time: 96.7 us; the launch traced here: 96.1 us
  starting transfers between devices  55.8 us (58%)
  waiting for transfers between devices  23.3 us (24%)
  Pallas kernels  13.4 us (14%)
  local copies, waits for them, and re-layouts  1.77 us (2%)
  other arithmetic  0.97 us (1%)
    all_to_all x3, starting transfers between devices, exchange(): return lax.all_to_all(pieces, 'space', 0, 0, axis_index_groups=groups)  25.8 us
    ppermute x2, starting transfers between devices, on_device(): lax.ppermute(rim, 'space', pairs)  10.5 us
    ppermute x3, starting transfers between devices, on_device(): lax.ppermute(piece, 'chan', [(c, c ^ flip) for c in range(chan)])  8.97 us
    all_to_all x3, waiting for transfers between devices, exchange(): return lax.all_to_all(pieces, 'space', 0, 0, axis_index_groups=groups)  8.61 us
    all_to_all x1, waiting for transfers between devices, on_device(): lax.all_to_all(jnp.broadcast_to(features, (chan,) + features.shape), 'cha...  6.93 us
    all_to_all x1, starting transfers between devices, on_device(): lax.all_to_all(jnp.broadcast_to(features, (chan,) + features.shape), 'cha...  4.97 us
    ppermute x3, waiting for transfers between devices, on_device(): lax.ppermute(piece, 'chan', [(c, c ^ flip) for c in range(chan)])  4.52 us
    pallas_call x1, Pallas kernels, call_backward(): pl.pallas_call(functools.partial(backward_kernel, blocks), out_shape=[sha...  3.97 us
  transfers between devices with their start and end apart: 11, of which 8 were waited for; matrix products, arithmetic and copies ran while one was open for 0% of the time, Pallas kernels for 8%

profile of v6, /device:TPU:1, one launch (start us, length us, event | category | flops | bytes accessed | tf_op | source)
XLA Modules:
  0.0 96.1 jit_solution(2301645735000476179)
XLA Ops:
  0.6 1.7 %broadcast_in_dim.3 = bf16[4,4,32,512]{3,2,1,0:T(8,128)(2,1)} broadcast(bf16[4,32,512]{2,1,0:T(8,128)(2,1)} %param.5), dimensions={1,2,3} | broadcast | bytes 655360 | tf_op jit(solution)/shard_map/broadcast_in_dim | solution.py:409
  2.4 0.0 copy-start.2
  2.4 5.0 %all-to-all-start = ((bf16[4,4,32,512]{3,2,1,0:T(8,128)(2,1)}), bf16[4,4,32,512]{3,2,1,0:T(8,128)(2,1)S(1)}, u32[]{:S(2)}, u32[]{:S(2)}) async-start(bf16[4,4,32,512]{3,2,1,0:T(8,128)(2,1)} %broadcast_in_dim.3), calls=%async_computation | async-start | bytes 1048576 | tf_op jit(solution)/shard_map/all_to_all | solution.py:408
  7.4 0.0 copy-start
  7.4 0.0 copy-start.1
  7.4 6.9 %all-to-all-done.gathered = bf16[4,4,32,512]{3,2,1,0:T(8,128)(2,1)S(1)} async-done(((bf16[4,4,32,512]{3,2,1,0:T(8,128)(2,1)}), bf16[4,4,32,512]{3,2,1,0:T(8,128)(2,1)S(1)}, u32[]{:S(2)}, u32[]{:S(2)}) %all-to-all-start) | async-done | bytes 524320 | tf_op jit(solution)/shard_map/all_to_all | solution.py:408
  14.3 0.0 copy-done
  14.3 0.1 shard_map.77
  14.4 0.0 copy-start.3
  14.4 8.5 %collective-permute-start = (bf16[128,512]{1,0:T(8,128)(2,1)S(1)}, bf16[128,512]{1,0:T(8,128)(2,1)S(1)}, u32[]{:S(2)}, u32[]{:S(2)}) collective-permute-start(bf16[128,512]{1,0:T(8,128)(2,1)S(1)} %get-tuple-element.30), channel_id=1, source_target_pairs={{0,4},{4,0},{8,12},{12,8},{16,20},{20,16},{24,28},{28,24},{32,36},... | collective-permute-start | bytes 393224 | tf_op jit(solution)/shard_map/ppermute | solution.py:412
  22.9 1.9 %collective-permute-start.1 = (bf16[128,512]{1,0:T(8,128)(2,1)S(1)}, bf16[128,512]{1,0:T(8,128)(2,1)S(1)}, u32[]{:S(2)}, u32[]{:S(2)}) collective-permute-start(bf16[128,512]{1,0:T(8,128)(2,1)S(1)} %get-tuple-element.31), channel_id=1, source_target_pairs={{4,8},{8,4},{12,16},{16,12},{20,24},{24,20},{28,32},{32,28},{36,40... | collective-permute-start | bytes 393224 | tf_op jit(solution)/shard_map/ppermute | solution.py:412
  24.8 0.0 copy-done.2
  24.9 0.0 copy-done.1
  24.9 0.0 copy-done.3
  24.9 3.2 %shard_map.76 = (bf16[2,64,512]{2,1,0:T(8,128)(2,1)S(1)}, bf16[192,1152]{1,0:T(8,128)(2,1)S(1)}, bf16[192,1280]{1,0:T(8,128)(2,1)S(1)}, f32[192,1152]{1,0:T(8,128)S(1)}, f32[2048,128]{1,0:T(8,128)S(1)}) custom-call(s32[1]{0:T(128)} %bitcast.spot, s32[4,26]{1,0:T(4,128)S(1)} %copy-done.3, bf16[4,4,32,512]{3,2,1,0:T(8,128)(2,1)S(1)} %all-to-all-done.gathered, ...), custom_call_target="tpu_custom_call" | custom-call | flops 1000000000 | bytes 4000000 | tf_op jit(solution)/shard_map/pallas_call | solution.py:261
  28.1 0.0 collective-permute-done.from_partner
  28.1 1.1 %collective-permute-done.1.from_across = bf16[128,512]{1,0:T(8,128)(2,1)S(1)} collective-permute-done((bf16[128,512]{1,0:T(8,128)(2,1)S(1)}, bf16[128,512]{1,0:T(8,128)(2,1)S(1)}, u32[]{:S(2)}, u32[]{:S(2)}) %collective-permute-start.1) | collective-permute-done | bytes 131104 | tf_op jit(solution)/shard_map/ppermute | solution.py:412
  29.2 3.8 %shard_map.78 = (bf16[4,64,512]{2,1,0:T(8,128)(2,1)}, bf16[192,1280]{1,0:T(8,128)(2,1)S(1)}, bf16[112,16,128]{2,1,0:T(8,128)(2,1)}) custom-call(s32[1]{0:T(128)} %bitcast.spot, s32[4,26]{1,0:T(4,128)S(1)} %copy-done.3, f32[2048,128]{1,0:T(8,128)S(1)} %get-tuple-element.29.own, bf16[128,512]{1,0:T(8,128)(2,1)S(1)} %collective-permute-done.from_partner, ...), custom_call_target="tpu_custom_call" | custom-call | flops 1000000000 | bytes 4000000 | tf_op jit(solution)/shard_map/pallas_call | solution.py:280
  33.0 9.9 %all-to-all-start.1 = ((bf16[16,7,16,128]{3,2,1,0:T(8,128)(2,1)}), bf16[16,7,16,128]{3,2,1,0:T(8,128)(2,1)S(1)}, u32[]{:S(2)}, u32[]{:S(2)}) async-start(bf16[16,7,16,128]{3,2,1,0:T(8,128)(2,1)} %bitcast.2), calls=%async_computation.1 | async-start | bytes 917504 | tf_op jit(solution)/shard_map/all_to_all | solution.py:382
  42.9 4.0 %shard_map.79 = (f32[6,32,512]{2,1,0:T(8,128)S(1)}, bf16[6,32,512]{2,1,0:T(8,128)(2,1)S(1)}, bf16[6,32,512]{2,1,0:T(8,128)(2,1)S(1)}, bf16[6,32,512]{2,1,0:T(8,128)(2,1)S(1)}) custom-call(s32[1]{0:T(128)} %bitcast.spot, s32[1]{0:T(128)} %bitcast.3.ring_spot, s32[4,26]{1,0:T(4,128)S(1)} %copy-done.3, bf16[192,1152]{1,0:T(8,128)(2,1)S(1)} %get-tuple-element.33.stacked, ...), custom_call_target="tpu_custom_call" | custom-call | flops 2000000000 | bytes 8000000 | tf_op jit(solution)/shard_map/pallas_call | solution.py:298
  46.9 5.1 %all-to-all-done.1.pieces = bf16[16,7,16,128]{3,2,1,0:T(8,128)(2,1)S(1)} async-done(((bf16[16,7,16,128]{3,2,1,0:T(8,128)(2,1)}), bf16[16,7,16,128]{3,2,1,0:T(8,128)(2,1)S(1)}, u32[]{:S(2)}, u32[]{:S(2)}) %all-to-all-start.1) | async-done | bytes 458784 | tf_op jit(solution)/shard_map/all_to_all | solution.py:382
  52.0 0.8 shard_map.80
  52.7 7.5 %all-to-all-start.2 = ((bf16[8,7,16,128]{3,2,1,0:T(8,128)(2,1)}), bf16[8,7,16,128]{3,2,1,0:T(8,128)(2,1)S(1)}, u32[]{:S(2)}, u32[]{:S(2)}) async-start(bf16[8,7,16,128]{3,2,1,0:T(8,128)(2,1)} %shard_map.80), calls=%async_computation.2 | async-start | bytes 458752 | tf_op jit(solution)/shard_map/all_to_all | solution.py:382
  60.2 2.2 %collective-permute-start.2 = (bf16[6,32,512]{2,1,0:T(8,128)(2,1)S(1)}, bf16[6,32,512]{2,1,0:T(8,128)(2,1)S(1)}, u32[]{:S(2)}, u32[]{:S(2)}) collective-permute-start(bf16[6,32,512]{2,1,0:T(8,128)(2,1)S(1)} %get-tuple-element.45), channel_id=1, source_target_pairs={{0,2},{1,3},{2,0},{3,1},{4,6},{5,7},{6,4},{7,5},{8,10},{9,11},{10,... | collective-permute-start | bytes 589832 | tf_op jit(solution)/shard_map/ppermute | solution.py:431
  62.4 3.1 %collective-permute-start.3 = (bf16[6,32,512]{2,1,0:T(8,128)(2,1)S(1)}, bf16[6,32,512]{2,1,0:T(8,128)(2,1)S(1)}, u32[]{:S(2)}, u32[]{:S(2)}) collective-permute-start(bf16[6,32,512]{2,1,0:T(8,128)(2,1)S(1)} %get-tuple-element.46), channel_id=1, source_target_pairs={{0,1},{1,0},{2,3},{3,2},{4,5},{5,4},{6,7},{7,6},{8,9},{9,8},{10,11... | collective-permute-start | bytes 589832 | tf_op jit(solution)/shard_map/ppermute | solution.py:431
  65.5 3.7 %collective-permute-start.4 = (bf16[6,32,512]{2,1,0:T(8,128)(2,1)S(1)}, bf16[6,32,512]{2,1,0:T(8,128)(2,1)S(1)}, u32[]{:S(2)}, u32[]{:S(2)}) collective-permute-start(bf16[6,32,512]{2,1,0:T(8,128)(2,1)S(1)} %get-tuple-element.47), channel_id=1, source_target_pairs={{0,3},{1,2},{2,1},{3,0},{4,7},{5,6},{6,5},{7,4},{8,11},{9,10},{10,... | collective-permute-start | bytes 589832 | tf_op jit(solution)/shard_map/ppermute | solution.py:431
  69.2 0.0 collective-permute-done.2.refs_0_
  69.2 2.0 %collective-permute-done.3.refs_1_ = bf16[6,32,512]{2,1,0:T(8,128)(2,1)S(1)} collective-permute-done((bf16[6,32,512]{2,1,0:T(8,128)(2,1)S(1)}, bf16[6,32,512]{2,1,0:T(8,128)(2,1)S(1)}, u32[]{:S(2)}, u32[]{:S(2)}) %collective-permute-start.3) | collective-permute-done | bytes 196640 | tf_op jit(solution)/shard_map/ppermute | solution.py:431
  71.3 2.5 %collective-permute-done.4.refs_2_ = bf16[6,32,512]{2,1,0:T(8,128)(2,1)S(1)} collective-permute-done((bf16[6,32,512]{2,1,0:T(8,128)(2,1)S(1)}, bf16[6,32,512]{2,1,0:T(8,128)(2,1)S(1)}, u32[]{:S(2)}, u32[]{:S(2)}) %collective-permute-start.4) | collective-permute-done | bytes 196640 | tf_op jit(solution)/shard_map/ppermute | solution.py:431
  73.8 2.9 %all-to-all-done.2.pieces = bf16[8,7,16,128]{3,2,1,0:T(8,128)(2,1)S(1)} async-done(((bf16[8,7,16,128]{3,2,1,0:T(8,128)(2,1)}), bf16[8,7,16,128]{3,2,1,0:T(8,128)(2,1)S(1)}, u32[]{:S(2)}, u32[]{:S(2)}) %all-to-all-start.2) | async-done | bytes 229408 | tf_op jit(solution)/shard_map/all_to_all | solution.py:382
  76.7 0.8 shard_map.83
  77.5 8.4 %all-to-all-start.3 = ((bf16[16,7,16,128]{3,2,1,0:T(8,128)(2,1)}), bf16[16,7,16,128]{3,2,1,0:T(8,128)(2,1)S(1)}, u32[]{:S(2)}, u32[]{:S(2)}) async-start(bf16[16,7,16,128]{3,2,1,0:T(8,128)(2,1)} %shard_map.83), calls=%async_computation.3 | async-start | bytes 917504 | tf_op jit(solution)/shard_map/all_to_all | solution.py:382
  85.9 0.1 shard_map.81
  86.0 2.1 %collective-permute-start.5 = (bf16[32,512]{1,0:T(8,128)(2,1)S(1)}, bf16[32,512]{1,0:T(8,128)(2,1)S(1)}, u32[]{:S(2)}, u32[]{:S(2)}) collective-permute-start(bf16[32,512]{1,0:T(8,128)(2,1)S(1)} %get-tuple-element.52), channel_id=1, source_target_pairs={{0,4},{4,0},{8,12},{12,8},{16,20},{20,16},{24,28},{28,24},{32,36},... | collective-permute-start | bytes 98312 | tf_op jit(solution)/shard_map/ppermute | solution.py:437
  88.2 3.5 %collective-permute-start.6 = (bf16[32,512]{1,0:T(8,128)(2,1)S(1)}, bf16[32,512]{1,0:T(8,128)(2,1)S(1)}, u32[]{:S(2)}, u32[]{:S(2)}) collective-permute-start(bf16[32,512]{1,0:T(8,128)(2,1)S(1)} %get-tuple-element.53), channel_id=1, source_target_pairs={{4,8},{8,4},{12,16},{16,12},{20,24},{24,20},{28,32},{32,28},{36,40... | collective-permute-start | bytes 98312 | tf_op jit(solution)/shard_map/ppermute | solution.py:438
  91.6 0.0 collective-permute-done.5.from_partner
  91.6 2.2 %collective-permute-done.6.from_across = bf16[32,512]{1,0:T(8,128)(2,1)S(1)} collective-permute-done((bf16[32,512]{1,0:T(8,128)(2,1)S(1)}, bf16[32,512]{1,0:T(8,128)(2,1)S(1)}, u32[]{:S(2)}, u32[]{:S(2)}) %collective-permute-start.6) | collective-permute-done | bytes 32800 | tf_op jit(solution)/shard_map/ppermute | solution.py:438
  93.8 0.7 shard_map.82
  94.5 0.6 all-to-all-done.3
  95.1 1.0 %convert_multiply_fusion = f32[108,16,128]{2,1,0:T(8,128)} fusion(bf16[112,16,128]{2,1,0:T(8,128)(2,1)S(1)} %bitcast.9), kind=kLoop, calls=%fused_computation | loop fusion | flops 442368 | bytes 1327104 | tf_op jit(solution)/shard_map/mul | solution.py:440
Async XLA Ops:
  2.4 22.5 %copy-start.2 = (bf16[4,64,512]{2,1,0:T(8,128)(2,1)S(1)}, bf16[4,64,512]{2,1,0:T(8,128)(2,1)}, u32[]{:S(2)}) copy-start(bf16[4,64,512]{2,1,0:T(8,128)(2,1)} %cotangent.3) | copy-start | bytes 786436
  2.4 11.9 %all-to-all-start = ((bf16[4,4,32,512]{3,2,1,0:T(8,128)(2,1)}), bf16[4,4,32,512]{3,2,1,0:T(8,128)(2,1)S(1)}, u32[]{:S(2)}, u32[]{:S(2)}) async-start(bf16[4,4,32,512]{3,2,1,0:T(8,128)(2,1)} %broadcast_in_dim.3), calls=%async_computation | async-start | bytes 1048576 | tf_op jit(solution)/shard_map/all_to_all | solution.py:408
  7.4 6.9 %copy-start = (s32[4,512]{1,0:T(4,128)S(1)}, s32[4,512]{1,0:T(4,128)}, u32[]{:S(2)}) copy-start(s32[4,512]{1,0:T(4,128)} %occupancy.7) | copy-start | bytes 24580
  7.4 17.5 %copy-start.1 = (bf16[64,27,128]{2,0,1:T(8,128)(2,1)S(1)}, bf16[64,27,128]{2,0,1:T(8,128)(2,1)}, u32[]{:S(2)}) copy-start(bf16[64,27,128]{2,0,1:T(8,128)(2,1)} %param.7) | copy-start | bytes 1327108
  14.4 10.5 %copy-start.3 = (s32[4,26]{1,0:T(4,128)S(1)}, s32[4,26]{1,0:T(4,128)}, u32[]{:S(2)}) copy-start(s32[4,26]{1,0:T(4,128)} %listed.5) | copy-start | bytes 1252
  14.4 13.7 %collective-permute-start = (bf16[128,512]{1,0:T(8,128)(2,1)S(1)}, bf16[128,512]{1,0:T(8,128)(2,1)S(1)}, u32[]{:S(2)}, u32[]{:S(2)}) collective-permute-start(bf16[128,512]{1,0:T(8,128)(2,1)S(1)} %get-tuple-element.30), channel_id=1, source_target_pairs={{0,4},{4,0},{8,12},{12,8},{16,20},{20,16},{24,28},{28,24},{32,36},... | collective-permute-start | bytes 393224 | tf_op jit(solution)/shard_map/ppermute | solution.py:412
  22.9 6.3 %collective-permute-start.1 = (bf16[128,512]{1,0:T(8,128)(2,1)S(1)}, bf16[128,512]{1,0:T(8,128)(2,1)S(1)}, u32[]{:S(2)}, u32[]{:S(2)}) collective-permute-start(bf16[128,512]{1,0:T(8,128)(2,1)S(1)} %get-tuple-element.31), channel_id=1, source_target_pairs={{4,8},{8,4},{12,16},{16,12},{20,24},{24,20},{28,32},{32,28},{36,40... | collective-permute-start | bytes 393224 | tf_op jit(solution)/shard_map/ppermute | solution.py:412
  33.0 19.0 %all-to-all-start.1 = ((bf16[16,7,16,128]{3,2,1,0:T(8,128)(2,1)}), bf16[16,7,16,128]{3,2,1,0:T(8,128)(2,1)S(1)}, u32[]{:S(2)}, u32[]{:S(2)}) async-start(bf16[16,7,16,128]{3,2,1,0:T(8,128)(2,1)} %bitcast.2), calls=%async_computation.1 | async-start | bytes 917504 | tf_op jit(solution)/shard_map/all_to_all | solution.py:382
  52.7 23.9 %all-to-all-start.2 = ((bf16[8,7,16,128]{3,2,1,0:T(8,128)(2,1)}), bf16[8,7,16,128]{3,2,1,0:T(8,128)(2,1)S(1)}, u32[]{:S(2)}, u32[]{:S(2)}) async-start(bf16[8,7,16,128]{3,2,1,0:T(8,128)(2,1)} %shard_map.80), calls=%async_computation.2 | async-start | bytes 458752 | tf_op jit(solution)/shard_map/all_to_all | solution.py:382
  60.2 9.0 %collective-permute-start.2 = (bf16[6,32,512]{2,1,0:T(8,128)(2,1)S(1)}, bf16[6,32,512]{2,1,0:T(8,128)(2,1)S(1)}, u32[]{:S(2)}, u32[]{:S(2)}) collective-permute-start(bf16[6,32,512]{2,1,0:T(8,128)(2,1)S(1)} %get-tuple-element.45), channel_id=1, source_target_pairs={{0,2},{1,3},{2,0},{3,1},{4,6},{5,7},{6,4},{7,5},{8,10},{9,11},{10,... | collective-permute-start | bytes 589832 | tf_op jit(solution)/shard_map/ppermute | solution.py:431
  62.4 8.9 %collective-permute-start.3 = (bf16[6,32,512]{2,1,0:T(8,128)(2,1)S(1)}, bf16[6,32,512]{2,1,0:T(8,128)(2,1)S(1)}, u32[]{:S(2)}, u32[]{:S(2)}) collective-permute-start(bf16[6,32,512]{2,1,0:T(8,128)(2,1)S(1)} %get-tuple-element.46), channel_id=1, source_target_pairs={{0,1},{1,0},{2,3},{3,2},{4,5},{5,4},{6,7},{7,6},{8,9},{9,8},{10,11... | collective-permute-start | bytes 589832 | tf_op jit(solution)/shard_map/ppermute | solution.py:431
  65.5 8.2 %collective-permute-start.4 = (bf16[6,32,512]{2,1,0:T(8,128)(2,1)S(1)}, bf16[6,32,512]{2,1,0:T(8,128)(2,1)S(1)}, u32[]{:S(2)}, u32[]{:S(2)}) collective-permute-start(bf16[6,32,512]{2,1,0:T(8,128)(2,1)S(1)} %get-tuple-element.47), channel_id=1, source_target_pairs={{0,3},{1,2},{2,1},{3,0},{4,7},{5,6},{6,5},{7,4},{8,11},{9,10},{10,... | collective-permute-start | bytes 589832 | tf_op jit(solution)/shard_map/ppermute | solution.py:431
  77.5 17.6 %all-to-all-start.3 = ((bf16[16,7,16,128]{3,2,1,0:T(8,128)(2,1)}), bf16[16,7,16,128]{3,2,1,0:T(8,128)(2,1)S(1)}, u32[]{:S(2)}, u32[]{:S(2)}) async-start(bf16[16,7,16,128]{3,2,1,0:T(8,128)(2,1)} %shard_map.83), calls=%async_computation.3 | async-start | bytes 917504 | tf_op jit(solution)/shard_map/all_to_all | solution.py:382
  86.0 5.6 %collective-permute-start.5 = (bf16[32,512]{1,0:T(8,128)(2,1)S(1)}, bf16[32,512]{1,0:T(8,128)(2,1)S(1)}, u32[]{:S(2)}, u32[]{:S(2)}) collective-permute-start(bf16[32,512]{1,0:T(8,128)(2,1)S(1)} %get-tuple-element.52), channel_id=1, source_target_pairs={{0,4},{4,0},{8,12},{12,8},{16,20},{20,16},{24,28},{28,24},{32,36},... | collective-permute-start | bytes 98312 | tf_op jit(solution)/shard_map/ppermute | solution.py:437
  88.2 5.7 %collective-permute-start.6 = (bf16[32,512]{1,0:T(8,128)(2,1)S(1)}, bf16[32,512]{1,0:T(8,128)(2,1)S(1)}, u32[]{:S(2)}, u32[]{:S(2)}) collective-permute-start(bf16[32,512]{1,0:T(8,128)(2,1)S(1)} %get-tuple-element.53), channel_id=1, source_target_pairs={{4,8},{8,4},{12,16},{16,12},{20,24},{24,20},{28,32},{32,28},{36,40... | collective-permute-start | bytes 98312 | tf_op jit(solution)/shard_map/ppermute | solution.py:438

commit v7 on v6

--- a/solution.py
+++ b/solution.py
@@ -405,9 +405,7 @@
     across = [(i, i - 1 if i % 2 == 0 else i + 1) for i in range(1, space - 1)]
     spot = place.astype(jnp.int32).reshape(1)
     ring_spot = lax.axis_index("chan").astype(jnp.int32).reshape(1)
-    gathered = lax.all_to_all(
-        jnp.broadcast_to(features, (chan,) + features.shape), "chan", 0, 0
-    )
+    gathered = lax.all_gather(features, "chan", axis=0)
     rims = [
         lax.ppermute(rim, "space", pairs)
         for rim, pairs in zip(call_rims(spot, gathered, occupancy), (partner, across))

time: 96.7 us -> 94.8 us (0.980)
  blocking collectives: 0 us -> 11.4 us
  waiting for transfers between devices: 23.3 us -> 15.7 us
  starting transfers between devices: 55.8 us -> 51.6 us
  local copies, waits for them, and re-layouts: 1.77 us -> 0.02 us
    all_gather x0 -> x1, blocking collectives: none -> 11.4 us  [on_device(): gathered = lax.all_gather(features, 'chan', axis=0)]
    all_to_all x1 -> x0, waiting for transfers between devices: 6.93 us -> none  [on_device(): lax.all_to_all(jnp.broadcast_to(features, (chan,) + features.shape), 'cha...]
    all_to_all x1 -> x0, starting transfers between devices: 4.97 us -> none  [on_device(): lax.all_to_all(jnp.broadcast_to(features, (chan,) + features.shape), 'cha...]
    ppermute x2, starting transfers between devices: 10.5 us -> 12.4 us  [on_device(): lax.ppermute(rim, 'space', pairs)]
    all_to_all x3, starting transfers between devices: 25.8 us -> 23.9 us  [exchange(): return lax.all_to_all(pieces, 'space', 0, 0, axis_index_groups=groups)]
    broadcast_in_dim x1 -> x0, local copies, waits for them, and re-layouts: 1.75 us -> none  [on_device(): jnp.broadcast_to(features, (chan,) + features.shape)]
    all_to_all x3, waiting for transfers between devices: 8.61 us -> 7.33 us  [exchange(): return lax.all_to_all(pieces, 'space', 0, 0, axis_index_groups=groups)]
  transfers between devices with their start and end apart: 11 -> 10, of which waited for: 8 -> 7; matrix products, arithmetic and copies ran while one was open for 0% -> 0% of each run, Pallas kernels for 8% -> 9%
where the time goes in v7:
time: 94.8 us; the launch traced here: 93.9 us
  starting transfers between devices  51.6 us (54%)
  waiting for transfers between devices  15.7 us (17%)
  Pallas kernels  13.4 us (14%)
  blocking collectives  11.4 us (12%)
  other arithmetic  0.97 us (1%)
    all_to_all x3, starting transfers between devices, exchange(): return lax.all_to_all(pieces, 'space', 0, 0, axis_index_groups=groups)  23.9 us
    ppermute x2, starting transfers between devices, on_device(): lax.ppermute(rim, 'space', pairs)  12.4 us
    all_gather x1, blocking collectives, on_device(): gathered = lax.all_gather(features, 'chan', axis=0)  11.4 us
    ppermute x3, starting transfers between devices, on_device(): lax.ppermute(piece, 'chan', [(c, c ^ flip) for c in range(chan)])  9.67 us
    all_to_all x3, waiting for transfers between devices, exchange(): return lax.all_to_all(pieces, 'space', 0, 0, axis_index_groups=groups)  7.33 us
    ppermute x3, waiting for transfers between devices, on_device(): lax.ppermute(piece, 'chan', [(c, c ^ flip) for c in range(chan)])  5.08 us
    pallas_call x1, Pallas kernels, call_backward(): pl.pallas_call(functools.partial(backward_kernel, blocks), out_shape=[sha...  4 us
    pallas_call x1, Pallas kernels, call_outer(): pl.pallas_call(outer_kernel, out_shape=[shape(blocks, out, 512), shape(3...  3.79 us
  transfers between devices with their start and end apart: 10, of which 7 were waited for; matrix products, arithmetic and copies ran while one was open for 0% of the time, Pallas kernels for 9%

profile of v7, /device:TPU:1, one launch (start us, length us, event | category | flops | bytes accessed | tf_op | source)
XLA Modules:
  0.0 93.9 jit_solution(3197132577305870693)
XLA Ops:
  0.6 0.0 copy-start
  0.6 0.0 copy-start.1
  0.7 11.4 %all-gather = bf16[16,32,512]{2,1,0:T(8,128)(2,1)S(1)} all-gather(bf16[4,32,512]{2,1,0:T(8,128)(2,1)} %param.5), channel_id=2, replica_groups=mesh['space'=128,'chan'=4] {'chan'}, dimensions={0}, use_global_device_ids=true | all-gather | bytes 655360 | tf_op jit(solution)/shard_map/all_gather | solution.py:408
  12.1 0.0 copy-done
  12.1 0.0 copy-start.2
  12.1 0.1 shard_map.77
  12.2 0.0 copy-start.3
  12.2 10.5 %collective-permute-start = (bf16[128,512]{1,0:T(8,128)(2,1)S(1)}, bf16[128,512]{1,0:T(8,128)(2,1)S(1)}, u32[]{:S(2)}, u32[]{:S(2)}) collective-permute-start(bf16[128,512]{1,0:T(8,128)(2,1)S(1)} %get-tuple-element.30), channel_id=1, source_target_pairs={{0,4},{4,0},{8,12},{12,8},{16,20},{20,16},{24,28},{28,24},{32,36},... | collective-permute-start | bytes 393224 | tf_op jit(solution)/shard_map/ppermute | solution.py:410
  22.7 1.9 %collective-permute-start.1 = (bf16[128,512]{1,0:T(8,128)(2,1)S(1)}, bf16[128,512]{1,0:T(8,128)(2,1)S(1)}, u32[]{:S(2)}, u32[]{:S(2)}) collective-permute-start(bf16[128,512]{1,0:T(8,128)(2,1)S(1)} %get-tuple-element.31), channel_id=1, source_target_pairs={{4,8},{8,4},{12,16},{16,12},{20,24},{24,20},{28,32},{32,28},{36,40... | collective-permute-start | bytes 393224 | tf_op jit(solution)/shard_map/ppermute | solution.py:410
  24.6 0.0 copy-done.1
  24.6 0.0 copy-done.2
  24.6 0.0 copy-done.3
  24.6 3.2 %shard_map.76 = (bf16[2,64,512]{2,1,0:T(8,128)(2,1)S(1)}, bf16[192,1152]{1,0:T(8,128)(2,1)S(1)}, bf16[192,1280]{1,0:T(8,128)(2,1)S(1)}, f32[192,1152]{1,0:T(8,128)S(1)}, f32[2048,128]{1,0:T(8,128)S(1)}) custom-call(s32[1]{0:T(128)} %bitcast.spot, s32[4,26]{1,0:T(4,128)S(1)} %copy-done.3, bf16[4,4,32,512]{3,2,1,0:T(8,128)(2,1)S(1)} %bitcast.10, ...), custom_call_target="tpu_custom_call" | custom-call | flops 1000000000 | bytes 4000000 | tf_op jit(solution)/shard_map/pallas_call | solution.py:261
  27.9 0.0 collective-permute-done.from_partner
  27.9 1.1 %collective-permute-done.1.from_across = bf16[128,512]{1,0:T(8,128)(2,1)S(1)} collective-permute-done((bf16[128,512]{1,0:T(8,128)(2,1)S(1)}, bf16[128,512]{1,0:T(8,128)(2,1)S(1)}, u32[]{:S(2)}, u32[]{:S(2)}) %collective-permute-start.1) | collective-permute-done | bytes 131104 | tf_op jit(solution)/shard_map/ppermute | solution.py:410
  29.0 3.8 %shard_map.78 = (bf16[4,64,512]{2,1,0:T(8,128)(2,1)}, bf16[192,1280]{1,0:T(8,128)(2,1)S(1)}, bf16[112,16,128]{2,1,0:T(8,128)(2,1)}) custom-call(s32[1]{0:T(128)} %bitcast.spot, s32[4,26]{1,0:T(4,128)S(1)} %copy-done.3, f32[2048,128]{1,0:T(8,128)S(1)} %get-tuple-element.29.own, bf16[128,512]{1,0:T(8,128)(2,1)S(1)} %collective-permute-done.from_partner, ...), custom_call_target="tpu_custom_call" | custom-call | flops 1000000000 | bytes 4000000 | tf_op jit(solution)/shard_map/pallas_call | solution.py:280
  32.8 8.0 %all-to-all-start = ((bf16[16,7,16,128]{3,2,1,0:T(8,128)(2,1)}), bf16[16,7,16,128]{3,2,1,0:T(8,128)(2,1)S(1)}, u32[]{:S(2)}, u32[]{:S(2)}) async-start(bf16[16,7,16,128]{3,2,1,0:T(8,128)(2,1)} %bitcast.3), calls=%async_computation | async-start | bytes 917504 | tf_op jit(solution)/shard_map/all_to_all | solution.py:382
  40.8 4.0 %shard_map.79 = (f32[6,32,512]{2,1,0:T(8,128)S(1)}, bf16[6,32,512]{2,1,0:T(8,128)(2,1)S(1)}, bf16[6,32,512]{2,1,0:T(8,128)(2,1)S(1)}, bf16[6,32,512]{2,1,0:T(8,128)(2,1)S(1)}) custom-call(s32[1]{0:T(128)} %bitcast.spot, s32[1]{0:T(128)} %bitcast.4.ring_spot, s32[4,26]{1,0:T(4,128)S(1)} %copy-done.3, bf16[192,1152]{1,0:T(8,128)(2,1)S(1)} %get-tuple-element.33.stacked, ...), custom_call_target="tpu_custom_call" | custom-call | flops 2000000000 | bytes 8000000 | tf_op jit(solution)/shard_map/pallas_call | solution.py:298
  44.8 5.1 %all-to-all-done.pieces = bf16[16,7,16,128]{3,2,1,0:T(8,128)(2,1)S(1)} async-done(((bf16[16,7,16,128]{3,2,1,0:T(8,128)(2,1)}), bf16[16,7,16,128]{3,2,1,0:T(8,128)(2,1)S(1)}, u32[]{:S(2)}, u32[]{:S(2)}) %all-to-all-start) | async-done | bytes 458784 | tf_op jit(solution)/shard_map/all_to_all | solution.py:382
  49.8 0.8 shard_map.80
  50.6 7.5 %all-to-all-start.1 = ((bf16[8,7,16,128]{3,2,1,0:T(8,128)(2,1)}), bf16[8,7,16,128]{3,2,1,0:T(8,128)(2,1)S(1)}, u32[]{:S(2)}, u32[]{:S(2)}) async-start(bf16[8,7,16,128]{3,2,1,0:T(8,128)(2,1)} %shard_map.80), calls=%async_computation.1 | async-start | bytes 458752 | tf_op jit(solution)/shard_map/all_to_all | solution.py:382
  58.1 3.1 %collective-permute-start.2 = (bf16[6,32,512]{2,1,0:T(8,128)(2,1)S(1)}, bf16[6,32,512]{2,1,0:T(8,128)(2,1)S(1)}, u32[]{:S(2)}, u32[]{:S(2)}) collective-permute-start(bf16[6,32,512]{2,1,0:T(8,128)(2,1)S(1)} %get-tuple-element.45), channel_id=1, source_target_pairs={{0,2},{1,3},{2,0},{3,1},{4,6},{5,7},{6,4},{7,5},{8,10},{9,11},{10,... | collective-permute-start | bytes 589832 | tf_op jit(solution)/shard_map/ppermute | solution.py:429
  61.2 4.1 %collective-permute-start.3 = (bf16[6,32,512]{2,1,0:T(8,128)(2,1)S(1)}, bf16[6,32,512]{2,1,0:T(8,128)(2,1)S(1)}, u32[]{:S(2)}, u32[]{:S(2)}) collective-permute-start(bf16[6,32,512]{2,1,0:T(8,128)(2,1)S(1)} %get-tuple-element.46), channel_id=1, source_target_pairs={{0,1},{1,0},{2,3},{3,2},{4,5},{5,4},{6,7},{7,6},{8,9},{9,8},{10,11... | collective-permute-start | bytes 589832 | tf_op jit(solution)/shard_map/ppermute | solution.py:429
  65.2 2.5 %collective-permute-start.4 = (bf16[6,32,512]{2,1,0:T(8,128)(2,1)S(1)}, bf16[6,32,512]{2,1,0:T(8,128)(2,1)S(1)}, u32[]{:S(2)}, u32[]{:S(2)}) collective-permute-start(bf16[6,32,512]{2,1,0:T(8,128)(2,1)S(1)} %get-tuple-element.47), channel_id=1, source_target_pairs={{0,3},{1,2},{2,1},{3,0},{4,7},{5,6},{6,5},{7,4},{8,11},{9,10},{10,... | collective-permute-start | bytes 589832 | tf_op jit(solution)/shard_map/ppermute | solution.py:429
  67.8 0.0 collective-permute-done.2.refs_0_
  67.8 3.2 %collective-permute-done.3.refs_1_ = bf16[6,32,512]{2,1,0:T(8,128)(2,1)S(1)} collective-permute-done((bf16[6,32,512]{2,1,0:T(8,128)(2,1)S(1)}, bf16[6,32,512]{2,1,0:T(8,128)(2,1)S(1)}, u32[]{:S(2)}, u32[]{:S(2)}) %collective-permute-start.3) | collective-permute-done | bytes 196640 | tf_op jit(solution)/shard_map/ppermute | solution.py:429
  71.0 1.9 %collective-permute-done.4.refs_2_ = bf16[6,32,512]{2,1,0:T(8,128)(2,1)S(1)} collective-permute-done((bf16[6,32,512]{2,1,0:T(8,128)(2,1)S(1)}, bf16[6,32,512]{2,1,0:T(8,128)(2,1)S(1)}, u32[]{:S(2)}, u32[]{:S(2)}) %collective-permute-start.4) | collective-permute-done | bytes 196640 | tf_op jit(solution)/shard_map/ppermute | solution.py:429
  72.9 1.7 %all-to-all-done.1.pieces = bf16[8,7,16,128]{3,2,1,0:T(8,128)(2,1)S(1)} async-done(((bf16[8,7,16,128]{3,2,1,0:T(8,128)(2,1)}), bf16[8,7,16,128]{3,2,1,0:T(8,128)(2,1)S(1)}, u32[]{:S(2)}, u32[]{:S(2)}) %all-to-all-start.1) | async-done | bytes 229408 | tf_op jit(solution)/shard_map/all_to_all | solution.py:382
  74.5 0.8 shard_map.83
  75.3 8.4 %all-to-all-start.2 = ((bf16[16,7,16,128]{3,2,1,0:T(8,128)(2,1)}), bf16[16,7,16,128]{3,2,1,0:T(8,128)(2,1)S(1)}, u32[]{:S(2)}, u32[]{:S(2)}) async-start(bf16[16,7,16,128]{3,2,1,0:T(8,128)(2,1)} %shard_map.83), calls=%async_computation.2 | async-start | bytes 917504 | tf_op jit(solution)/shard_map/all_to_all | solution.py:382
  83.8 0.1 shard_map.81
  83.9 2.1 %collective-permute-start.5 = (bf16[32,512]{1,0:T(8,128)(2,1)S(1)}, bf16[32,512]{1,0:T(8,128)(2,1)S(1)}, u32[]{:S(2)}, u32[]{:S(2)}) collective-permute-start(bf16[32,512]{1,0:T(8,128)(2,1)S(1)} %get-tuple-element.52), channel_id=1, source_target_pairs={{0,4},{4,0},{8,12},{12,8},{16,20},{20,16},{24,28},{28,24},{32,36},... | collective-permute-start | bytes 98312 | tf_op jit(solution)/shard_map/ppermute | solution.py:435
  86.0 3.5 %collective-permute-start.6 = (bf16[32,512]{1,0:T(8,128)(2,1)S(1)}, bf16[32,512]{1,0:T(8,128)(2,1)S(1)}, u32[]{:S(2)}, u32[]{:S(2)}) collective-permute-start(bf16[32,512]{1,0:T(8,128)(2,1)S(1)} %get-tuple-element.53), channel_id=1, source_target_pairs={{4,8},{8,4},{12,16},{16,12},{20,24},{24,20},{28,32},{32,28},{36,40... | collective-permute-start | bytes 98312 | tf_op jit(solution)/shard_map/ppermute | solution.py:436
  89.5 0.0 collective-permute-done.5.from_partner
  89.5 2.2 %collective-permute-done.6.from_across = bf16[32,512]{1,0:T(8,128)(2,1)S(1)} collective-permute-done((bf16[32,512]{1,0:T(8,128)(2,1)S(1)}, bf16[32,512]{1,0:T(8,128)(2,1)S(1)}, u32[]{:S(2)}, u32[]{:S(2)}) %collective-permute-start.6) | collective-permute-done | bytes 32800 | tf_op jit(solution)/shard_map/ppermute | solution.py:436
  91.7 0.7 shard_map.82
  92.4 0.6 all-to-all-done.2
  93.0 1.0 %convert_multiply_fusion = f32[108,16,128]{2,1,0:T(8,128)} fusion(bf16[112,16,128]{2,1,0:T(8,128)(2,1)S(1)} %bitcast.12), kind=kLoop, calls=%fused_computation | loop fusion | flops 442368 | bytes 1327104 | tf_op jit(solution)/shard_map/mul | solution.py:438
Async XLA Ops:
  0.6 11.4 %copy-start = (s32[4,512]{1,0:T(4,128)S(1)}, s32[4,512]{1,0:T(4,128)}, u32[]{:S(2)}) copy-start(s32[4,512]{1,0:T(4,128)} %occupancy.7) | copy-start | bytes 24580
  0.6 24.0 %copy-start.1 = (bf16[64,27,128]{2,0,1:T(8,128)(2,1)S(1)}, bf16[64,27,128]{2,0,1:T(8,128)(2,1)}, u32[]{:S(2)}) copy-start(bf16[64,27,128]{2,0,1:T(8,128)(2,1)} %param.7) | copy-start | bytes 1327108
  12.1 12.5 %copy-start.2 = (bf16[4,64,512]{2,1,0:T(8,128)(2,1)S(1)}, bf16[4,64,512]{2,1,0:T(8,128)(2,1)}, u32[]{:S(2)}) copy-start(bf16[4,64,512]{2,1,0:T(8,128)(2,1)} %cotangent.3) | copy-start | bytes 786436
  12.2 12.5 %copy-start.3 = (s32[4,26]{1,0:T(4,128)S(1)}, s32[4,26]{1,0:T(4,128)}, u32[]{:S(2)}) copy-start(s32[4,26]{1,0:T(4,128)} %listed.5) | copy-start | bytes 1252
  12.2 15.7 %collective-permute-start = (bf16[128,512]{1,0:T(8,128)(2,1)S(1)}, bf16[128,512]{1,0:T(8,128)(2,1)S(1)}, u32[]{:S(2)}, u32[]{:S(2)}) collective-permute-start(bf16[128,512]{1,0:T(8,128)(2,1)S(1)} %get-tuple-element.30), channel_id=1, source_target_pairs={{0,4},{4,0},{8,12},{12,8},{16,20},{20,16},{24,28},{28,24},{32,36},... | collective-permute-start | bytes 393224 | tf_op jit(solution)/shard_map/ppermute | solution.py:410
  22.7 6.3 %collective-permute-start.1 = (bf16[128,512]{1,0:T(8,128)(2,1)S(1)}, bf16[128,512]{1,0:T(8,128)(2,1)S(1)}, u32[]{:S(2)}, u32[]{:S(2)}) collective-permute-start(bf16[128,512]{1,0:T(8,128)(2,1)S(1)} %get-tuple-element.31), channel_id=1, source_target_pairs={{4,8},{8,4},{12,16},{16,12},{20,24},{24,20},{28,32},{32,28},{36,40... | collective-permute-start | bytes 393224 | tf_op jit(solution)/shard_map/ppermute | solution.py:410
  32.8 17.1 %all-to-all-start = ((bf16[16,7,16,128]{3,2,1,0:T(8,128)(2,1)}), bf16[16,7,16,128]{3,2,1,0:T(8,128)(2,1)S(1)}, u32[]{:S(2)}, u32[]{:S(2)}) async-start(bf16[16,7,16,128]{3,2,1,0:T(8,128)(2,1)} %bitcast.3), calls=%async_computation | async-start | bytes 917504 | tf_op jit(solution)/shard_map/all_to_all | solution.py:382
  50.6 23.9 %all-to-all-start.1 = ((bf16[8,7,16,128]{3,2,1,0:T(8,128)(2,1)}), bf16[8,7,16,128]{3,2,1,0:T(8,128)(2,1)S(1)}, u32[]{:S(2)}, u32[]{:S(2)}) async-start(bf16[8,7,16,128]{3,2,1,0:T(8,128)(2,1)} %shard_map.80), calls=%async_computation.1 | async-start | bytes 458752 | tf_op jit(solution)/shard_map/all_to_all | solution.py:382
  58.1 9.7 %collective-permute-start.2 = (bf16[6,32,512]{2,1,0:T(8,128)(2,1)S(1)}, bf16[6,32,512]{2,1,0:T(8,128)(2,1)S(1)}, u32[]{:S(2)}, u32[]{:S(2)}) collective-permute-start(bf16[6,32,512]{2,1,0:T(8,128)(2,1)S(1)} %get-tuple-element.45), channel_id=1, source_target_pairs={{0,2},{1,3},{2,0},{3,1},{4,6},{5,7},{6,4},{7,5},{8,10},{9,11},{10,... | collective-permute-start | bytes 589832 | tf_op jit(solution)/shard_map/ppermute | solution.py:429
  61.2 9.8 %collective-permute-start.3 = (bf16[6,32,512]{2,1,0:T(8,128)(2,1)S(1)}, bf16[6,32,512]{2,1,0:T(8,128)(2,1)S(1)}, u32[]{:S(2)}, u32[]{:S(2)}) collective-permute-start(bf16[6,32,512]{2,1,0:T(8,128)(2,1)S(1)} %get-tuple-element.46), channel_id=1, source_target_pairs={{0,1},{1,0},{2,3},{3,2},{4,5},{5,4},{6,7},{7,6},{8,9},{9,8},{10,11... | collective-permute-start | bytes 589832 | tf_op jit(solution)/shard_map/ppermute | solution.py:429
  65.2 7.6 %collective-permute-start.4 = (bf16[6,32,512]{2,1,0:T(8,128)(2,1)S(1)}, bf16[6,32,512]{2,1,0:T(8,128)(2,1)S(1)}, u32[]{:S(2)}, u32[]{:S(2)}) collective-permute-start(bf16[6,32,512]{2,1,0:T(8,128)(2,1)S(1)} %get-tuple-element.47), channel_id=1, source_target_pairs={{0,3},{1,2},{2,1},{3,0},{4,7},{5,6},{6,5},{7,4},{8,11},{9,10},{10,... | collective-permute-start | bytes 589832 | tf_op jit(solution)/shard_map/ppermute | solution.py:429
  75.3 17.6 %all-to-all-start.2 = ((bf16[16,7,16,128]{3,2,1,0:T(8,128)(2,1)}), bf16[16,7,16,128]{3,2,1,0:T(8,128)(2,1)S(1)}, u32[]{:S(2)}, u32[]{:S(2)}) async-start(bf16[16,7,16,128]{3,2,1,0:T(8,128)(2,1)} %shard_map.83), calls=%async_computation.2 | async-start | bytes 917504 | tf_op jit(solution)/shard_map/all_to_all | solution.py:382
  83.9 5.6 %collective-permute-start.5 = (bf16[32,512]{1,0:T(8,128)(2,1)S(1)}, bf16[32,512]{1,0:T(8,128)(2,1)S(1)}, u32[]{:S(2)}, u32[]{:S(2)}) collective-permute-start(bf16[32,512]{1,0:T(8,128)(2,1)S(1)} %get-tuple-element.52), channel_id=1, source_target_pairs={{0,4},{4,0},{8,12},{12,8},{16,20},{20,16},{24,28},{28,24},{32,36},... | collective-permute-start | bytes 98312 | tf_op jit(solution)/shard_map/ppermute | solution.py:435
  86.0 5.7 %collective-permute-start.6 = (bf16[32,512]{1,0:T(8,128)(2,1)S(1)}, bf16[32,512]{1,0:T(8,128)(2,1)S(1)}, u32[]{:S(2)}, u32[]{:S(2)}) collective-permute-start(bf16[32,512]{1,0:T(8,128)(2,1)S(1)} %get-tuple-element.53), channel_id=1, source_target_pairs={{4,8},{8,4},{12,16},{16,12},{20,24},{24,20},{28,32},{32,28},{36,40... | collective-permute-start | bytes 98312 | tf_op jit(solution)/shard_map/ppermute | solution.py:436

commit v8 on v7

--- a/solution.py
+++ b/solution.py
@@ -147,7 +147,7 @@
 
 
 def outer_kernel(
-    spot, listed, own, from_partner, from_across, cotangent, occupancy, inner, stacked, product,
+    spot, listed, own, from_across, from_partner, cotangent, occupancy, inner, stacked, product,
     activation, grads, tiles,
     voxels, cube, patches,
 ):
@@ -351,7 +351,7 @@
     )(mine, *arrived)
 
 
-def final_kernel(spot, own, from_partner, from_across, occupancy, out):
+def final_kernel(spot, own, from_across, from_partner, occupancy, out):
     blocks = own.shape[0]
     is_even = lax.rem(spot[0], 2) == 0
     partner, across = from_partner[...].astype(F32), from_across[...].astype(F32)
@@ -364,14 +364,14 @@
         out[slot] = (total * occupancy[slot : slot + 1, :].astype(F32)).astype(BF16)
 
 
-def call_final(spot, own, from_partner, from_across, occupancy):
+def call_final(spot, own, from_across, from_partner, occupancy):
     return pl.pallas_call(
         final_kernel,
         out_shape=shape(*own.shape),
         in_specs=[SMEM] + [VMEM] * 4,
         out_specs=VMEM,
         compiler_params=SMALL,
-    )(spot, own, from_partner, from_across, occupancy)
+    )(spot, own, from_across, from_partner, occupancy)
 
 
 def stages_of(count):
@@ -406,10 +406,10 @@
     spot = place.astype(jnp.int32).reshape(1)
     ring_spot = lax.axis_index("chan").astype(jnp.int32).reshape(1)
     gathered = lax.all_gather(features, "chan", axis=0)
-    rims = [
-        lax.ppermute(rim, "space", pairs)
-        for rim, pairs in zip(call_rims(spot, gathered, occupancy), (partner, across))
-    ]
+    rim_partner, rim_across = call_rims(spot, gathered, occupancy)
+    from_across = lax.ppermute(rim_across, "space", across)
+    from_partner = lax.ppermute(rim_partner, "space", partner)
+    rims = (from_across, from_partner)
 
     inner, stacked, inner_grads, product, own = call_inner(
         spot, neighbours, gathered, jnp.transpose(weight, (1, 0, 2)), cotangent, occupancy
@@ -432,12 +432,12 @@
     parts, arrived = lax.optimization_barrier((parts, arrived))
     total = exchange(call_add(parts, len(near[0])), near)
     own, rim_partner, rim_across = call_sum(mine, arrived)
+    to_across = lax.ppermute(rim_across, "space", across)
     to_partner = lax.ppermute(rim_partner, "space", partner)
-    to_across = lax.ppermute(rim_across, "space", across)
     total = total.reshape(-1, 16, 128)[:108].astype(F32).reshape(27, out, 128)
     weight_grad = jnp.transpose(total * lax.rsqrt(F32(space * blocks * 512)), (1, 0, 2))
 
-    input_grad = call_final(spot, own, to_partner, to_across, occupancy)
+    input_grad = call_final(spot, own, to_across, to_partner, occupancy)
     return (activation, input_grad, weight_grad)
 
 

time: 94.8 us -> 93.8 us (0.989)
    all_to_all x3, starting transfers between devices: 23.9 us -> 25.5 us  [exchange(): return lax.all_to_all(pieces, 'space', 0, 0, axis_index_groups=groups)]
    ppermute x2, starting transfers between devices: 12.4 us -> 11.2 us  [the longest x1 6.99 us: on_device(): from_across = lax.ppermute(rim_across, 'space', across)]
    ppermute x2, waiting for transfers between devices: 1.09 us -> 0.01 us  [the longest x1 0.01 us: on_device(): from_across = lax.ppermute(rim_across, 'space', across)]
  transfers between devices with their start and end apart: 10 -> 10, of which waited for: 7 -> 6; matrix products, arithmetic and copies ran while one was open for 0% -> 0% of each run, Pallas kernels for 9% -> 9%
where the time goes in v8:
time: 93.8 us; the launch traced here: 93.2 us
  starting transfers between devices  51.8 us (55%)
  waiting for transfers between devices  14.8 us (16%)
  Pallas kernels  13.4 us (14%)
  blocking collectives  11.4 us (12%)
  other arithmetic  0.97 us (1%)
    all_to_all x3, starting transfers between devices, exchange(): return lax.all_to_all(pieces, 'space', 0, 0, axis_index_groups=groups)  25.5 us
    all_gather x1, blocking collectives, on_device(): gathered = lax.all_gather(features, 'chan', axis=0)  11.4 us
    ppermute x3, starting transfers between devices, on_device(): lax.ppermute(piece, 'chan', [(c, c ^ flip) for c in range(chan)])  9.66 us
    all_to_all x3, waiting for transfers between devices, exchange(): return lax.all_to_all(pieces, 'space', 0, 0, axis_index_groups=groups)  7.36 us
    ppermute x1, starting transfers between devices, on_device(): from_across = lax.ppermute(rim_across, 'space', across)  6.99 us
    ppermute x3, waiting for transfers between devices, on_device(): lax.ppermute(piece, 'chan', [(c, c ^ flip) for c in range(chan)])  5.08 us
    ppermute x1, starting transfers between devices, on_device(): from_partner = lax.ppermute(rim_partner, 'space', partner)  4.17 us
    pallas_call x1, Pallas kernels, call_backward(): pl.pallas_call(functools.partial(backward_kernel, blocks), out_shape=[sha...  3.96 us
  transfers between devices with their start and end apart: 10, of which 6 were waited for; matrix products, arithmetic and copies ran while one was open for 0% of the time, Pallas kernels for 9%

profile of v8, /device:TPU:1, one launch (start us, length us, event | category | flops | bytes accessed | tf_op | source)
XLA Modules:
  0.0 93.2 jit_solution(9650216331515829637)
XLA Ops:
  0.6 0.0 copy-start
  0.6 0.0 copy-start.1
  0.7 11.4 %all-gather = bf16[16,32,512]{2,1,0:T(8,128)(2,1)S(1)} all-gather(bf16[4,32,512]{2,1,0:T(8,128)(2,1)} %param.5), channel_id=2, replica_groups=mesh['space'=128,'chan'=4] {'chan'}, dimensions={0}, use_global_device_ids=true | all-gather | bytes 655360 | tf_op jit(solution)/shard_map/all_gather | solution.py:408
  12.1 0.0 copy-done
  12.1 0.0 copy-start.2
  12.1 0.1 shard_map.77
  12.2 0.0 copy-start.3
  12.2 7.0 %collective-permute-start = (bf16[128,512]{1,0:T(8,128)(2,1)S(1)}, bf16[128,512]{1,0:T(8,128)(2,1)S(1)}, u32[]{:S(2)}, u32[]{:S(2)}) collective-permute-start(bf16[128,512]{1,0:T(8,128)(2,1)S(1)} %get-tuple-element.30), channel_id=1, source_target_pairs={{4,8},{8,4},{12,16},{16,12},{20,24},{24,20},{28,32},{32,28},{36,40... | collective-permute-start | bytes 393224 | tf_op jit(solution)/shard_map/ppermute | solution.py:410
  19.2 4.2 %collective-permute-start.1 = (bf16[128,512]{1,0:T(8,128)(2,1)S(1)}, bf16[128,512]{1,0:T(8,128)(2,1)S(1)}, u32[]{:S(2)}, u32[]{:S(2)}) collective-permute-start(bf16[128,512]{1,0:T(8,128)(2,1)S(1)} %get-tuple-element.31), channel_id=1, source_target_pairs={{0,4},{4,0},{8,12},{12,8},{16,20},{20,16},{24,28},{28,24},{32,36},... | collective-permute-start | bytes 393224 | tf_op jit(solution)/shard_map/ppermute | solution.py:411
  23.3 0.0 copy-done.1
  23.4 0.0 copy-done.2
  23.4 0.0 copy-done.3
  23.4 3.2 %shard_map.76 = (bf16[2,64,512]{2,1,0:T(8,128)(2,1)S(1)}, bf16[192,1152]{1,0:T(8,128)(2,1)S(1)}, bf16[192,1280]{1,0:T(8,128)(2,1)S(1)}, f32[192,1152]{1,0:T(8,128)S(1)}, f32[2048,128]{1,0:T(8,128)S(1)}) custom-call(s32[1]{0:T(128)} %bitcast.spot, s32[4,26]{1,0:T(4,128)S(1)} %copy-done.3, bf16[4,4,32,512]{3,2,1,0:T(8,128)(2,1)S(1)} %bitcast.10, ...), custom_call_target="tpu_custom_call" | custom-call | flops 1000000000 | bytes 4000000 | tf_op jit(solution)/shard_map/pallas_call | solution.py:261
  26.6 0.0 collective-permute-done.from_across
  26.6 0.0 collective-permute-done.1.from_partner
  26.6 3.8 %shard_map.78 = (bf16[4,64,512]{2,1,0:T(8,128)(2,1)}, bf16[192,1280]{1,0:T(8,128)(2,1)S(1)}, bf16[112,16,128]{2,1,0:T(8,128)(2,1)}) custom-call(s32[1]{0:T(128)} %bitcast.spot, s32[4,26]{1,0:T(4,128)S(1)} %copy-done.3, f32[2048,128]{1,0:T(8,128)S(1)} %get-tuple-element.29.own, bf16[128,512]{1,0:T(8,128)(2,1)S(1)} %collective-permute-done.from_across, ...), custom_call_target="tpu_custom_call" | custom-call | flops 1000000000 | bytes 4000000 | tf_op jit(solution)/shard_map/pallas_call | solution.py:280
  30.5 8.1 %all-to-all-start = ((bf16[16,7,16,128]{3,2,1,0:T(8,128)(2,1)}), bf16[16,7,16,128]{3,2,1,0:T(8,128)(2,1)S(1)}, u32[]{:S(2)}, u32[]{:S(2)}) async-start(bf16[16,7,16,128]{3,2,1,0:T(8,128)(2,1)} %bitcast.3), calls=%async_computation | async-start | bytes 917504 | tf_op jit(solution)/shard_map/all_to_all | solution.py:382
  38.6 4.0 %shard_map.79 = (f32[6,32,512]{2,1,0:T(8,128)S(1)}, bf16[6,32,512]{2,1,0:T(8,128)(2,1)S(1)}, bf16[6,32,512]{2,1,0:T(8,128)(2,1)S(1)}, bf16[6,32,512]{2,1,0:T(8,128)(2,1)S(1)}) custom-call(s32[1]{0:T(128)} %bitcast.spot, s32[1]{0:T(128)} %bitcast.4.ring_spot, s32[4,26]{1,0:T(4,128)S(1)} %copy-done.3, bf16[192,1152]{1,0:T(8,128)(2,1)S(1)} %get-tuple-element.33.stacked, ...), custom_call_target="tpu_custom_call" | custom-call | flops 2000000000 | bytes 8000000 | tf_op jit(solution)/shard_map/pallas_call | solution.py:298
  42.5 5.1 %all-to-all-done.pieces = bf16[16,7,16,128]{3,2,1,0:T(8,128)(2,1)S(1)} async-done(((bf16[16,7,16,128]{3,2,1,0:T(8,128)(2,1)}), bf16[16,7,16,128]{3,2,1,0:T(8,128)(2,1)S(1)}, u32[]{:S(2)}, u32[]{:S(2)}) %all-to-all-start) | async-done | bytes 458784 | tf_op jit(solution)/shard_map/all_to_all | solution.py:382
  47.7 0.8 shard_map.80
  48.4 9.0 %all-to-all-start.1 = ((bf16[8,7,16,128]{3,2,1,0:T(8,128)(2,1)}), bf16[8,7,16,128]{3,2,1,0:T(8,128)(2,1)S(1)}, u32[]{:S(2)}, u32[]{:S(2)}) async-start(bf16[8,7,16,128]{3,2,1,0:T(8,128)(2,1)} %shard_map.80), calls=%async_computation.1 | async-start | bytes 458752 | tf_op jit(solution)/shard_map/all_to_all | solution.py:382
  57.4 3.1 %collective-permute-start.2 = (bf16[6,32,512]{2,1,0:T(8,128)(2,1)S(1)}, bf16[6,32,512]{2,1,0:T(8,128)(2,1)S(1)}, u32[]{:S(2)}, u32[]{:S(2)}) collective-permute-start(bf16[6,32,512]{2,1,0:T(8,128)(2,1)S(1)} %get-tuple-element.45), channel_id=1, source_target_pairs={{0,2},{1,3},{2,0},{3,1},{4,6},{5,7},{6,4},{7,5},{8,10},{9,11},{10,... | collective-permute-start | bytes 589832 | tf_op jit(solution)/shard_map/ppermute | solution.py:429
  60.5 4.1 %collective-permute-start.3 = (bf16[6,32,512]{2,1,0:T(8,128)(2,1)S(1)}, bf16[6,32,512]{2,1,0:T(8,128)(2,1)S(1)}, u32[]{:S(2)}, u32[]{:S(2)}) collective-permute-start(bf16[6,32,512]{2,1,0:T(8,128)(2,1)S(1)} %get-tuple-element.46), channel_id=1, source_target_pairs={{0,1},{1,0},{2,3},{3,2},{4,5},{5,4},{6,7},{7,6},{8,9},{9,8},{10,11... | collective-permute-start | bytes 589832 | tf_op jit(solution)/shard_map/ppermute | solution.py:429
  64.5 2.5 %collective-permute-start.4 = (bf16[6,32,512]{2,1,0:T(8,128)(2,1)S(1)}, bf16[6,32,512]{2,1,0:T(8,128)(2,1)S(1)}, u32[]{:S(2)}, u32[]{:S(2)}) collective-permute-start(bf16[6,32,512]{2,1,0:T(8,128)(2,1)S(1)} %get-tuple-element.47), channel_id=1, source_target_pairs={{0,3},{1,2},{2,1},{3,0},{4,7},{5,6},{6,5},{7,4},{8,11},{9,10},{10,... | collective-permute-start | bytes 589832 | tf_op jit(solution)/shard_map/ppermute | solution.py:429
  67.1 0.0 collective-permute-done.2.refs_0_
  67.1 3.2 %collective-permute-done.3.refs_1_ = bf16[6,32,512]{2,1,0:T(8,128)(2,1)S(1)} collective-permute-done((bf16[6,32,512]{2,1,0:T(8,128)(2,1)S(1)}, bf16[6,32,512]{2,1,0:T(8,128)(2,1)S(1)}, u32[]{:S(2)}, u32[]{:S(2)}) %collective-permute-start.3) | collective-permute-done | bytes 196640 | tf_op jit(solution)/shard_map/ppermute | solution.py:429
  70.3 1.9 %collective-permute-done.4.refs_2_ = bf16[6,32,512]{2,1,0:T(8,128)(2,1)S(1)} collective-permute-done((bf16[6,32,512]{2,1,0:T(8,128)(2,1)S(1)}, bf16[6,32,512]{2,1,0:T(8,128)(2,1)S(1)}, u32[]{:S(2)}, u32[]{:S(2)}) %collective-permute-start.4) | collective-permute-done | bytes 196640 | tf_op jit(solution)/shard_map/ppermute | solution.py:429
  72.2 1.7 %all-to-all-done.1.pieces = bf16[8,7,16,128]{3,2,1,0:T(8,128)(2,1)S(1)} async-done(((bf16[8,7,16,128]{3,2,1,0:T(8,128)(2,1)}), bf16[8,7,16,128]{3,2,1,0:T(8,128)(2,1)S(1)}, u32[]{:S(2)}, u32[]{:S(2)}) %all-to-all-start.1) | async-done | bytes 229408 | tf_op jit(solution)/shard_map/all_to_all | solution.py:382
  73.8 0.8 shard_map.83
  74.6 8.4 %all-to-all-start.2 = ((bf16[16,7,16,128]{3,2,1,0:T(8,128)(2,1)}), bf16[16,7,16,128]{3,2,1,0:T(8,128)(2,1)S(1)}, u32[]{:S(2)}, u32[]{:S(2)}) async-start(bf16[16,7,16,128]{3,2,1,0:T(8,128)(2,1)} %shard_map.83), calls=%async_computation.2 | async-start | bytes 917504 | tf_op jit(solution)/shard_map/all_to_all | solution.py:382
  83.1 0.1 shard_map.81
  83.2 3.5 %collective-permute-start.5 = (bf16[32,512]{1,0:T(8,128)(2,1)S(1)}, bf16[32,512]{1,0:T(8,128)(2,1)S(1)}, u32[]{:S(2)}, u32[]{:S(2)}) collective-permute-start(bf16[32,512]{1,0:T(8,128)(2,1)S(1)} %get-tuple-element.52), channel_id=1, source_target_pairs={{4,8},{8,4},{12,16},{16,12},{20,24},{24,20},{28,32},{32,28},{36,40... | collective-permute-start | bytes 98312 | tf_op jit(solution)/shard_map/ppermute | solution.py:435
  86.7 1.9 %collective-permute-start.6 = (bf16[32,512]{1,0:T(8,128)(2,1)S(1)}, bf16[32,512]{1,0:T(8,128)(2,1)S(1)}, u32[]{:S(2)}, u32[]{:S(2)}) collective-permute-start(bf16[32,512]{1,0:T(8,128)(2,1)S(1)} %get-tuple-element.53), channel_id=1, source_target_pairs={{0,4},{4,0},{8,12},{12,8},{16,20},{20,16},{24,28},{28,24},{32,36},... | collective-permute-start | bytes 98312 | tf_op jit(solution)/shard_map/ppermute | solution.py:436
  88.6 2.3 %collective-permute-done.5.from_across = bf16[32,512]{1,0:T(8,128)(2,1)S(1)} collective-permute-done((bf16[32,512]{1,0:T(8,128)(2,1)S(1)}, bf16[32,512]{1,0:T(8,128)(2,1)S(1)}, u32[]{:S(2)}, u32[]{:S(2)}) %collective-permute-start.5) | collective-permute-done | bytes 32800 | tf_op jit(solution)/shard_map/ppermute | solution.py:435
  91.0 0.0 collective-permute-done.6.from_partner
  91.0 0.7 shard_map.82
  91.7 0.6 all-to-all-done.2
  92.2 1.0 %convert_multiply_fusion = f32[108,16,128]{2,1,0:T(8,128)} fusion(bf16[112,16,128]{2,1,0:T(8,128)(2,1)S(1)} %bitcast.12), kind=kLoop, calls=%fused_computation | loop fusion | flops 442368 | bytes 1327104 | tf_op jit(solution)/shard_map/mul | solution.py:438
Async XLA Ops:
  0.6 11.4 %copy-start = (s32[4,512]{1,0:T(4,128)S(1)}, s32[4,512]{1,0:T(4,128)}, u32[]{:S(2)}) copy-start(s32[4,512]{1,0:T(4,128)} %occupancy.7) | copy-start | bytes 24580
  0.6 22.7 %copy-start.1 = (bf16[64,27,128]{2,0,1:T(8,128)(2,1)S(1)}, bf16[64,27,128]{2,0,1:T(8,128)(2,1)}, u32[]{:S(2)}) copy-start(bf16[64,27,128]{2,0,1:T(8,128)(2,1)} %param.7) | copy-start | bytes 1327108
  12.1 11.3 %copy-start.2 = (bf16[4,64,512]{2,1,0:T(8,128)(2,1)S(1)}, bf16[4,64,512]{2,1,0:T(8,128)(2,1)}, u32[]{:S(2)}) copy-start(bf16[4,64,512]{2,1,0:T(8,128)(2,1)} %cotangent.3) | copy-start | bytes 786436
  12.2 11.2 %copy-start.3 = (s32[4,26]{1,0:T(4,128)S(1)}, s32[4,26]{1,0:T(4,128)}, u32[]{:S(2)}) copy-start(s32[4,26]{1,0:T(4,128)} %listed.5) | copy-start | bytes 1252
  12.2 14.5 %collective-permute-start = (bf16[128,512]{1,0:T(8,128)(2,1)S(1)}, bf16[128,512]{1,0:T(8,128)(2,1)S(1)}, u32[]{:S(2)}, u32[]{:S(2)}) collective-permute-start(bf16[128,512]{1,0:T(8,128)(2,1)S(1)} %get-tuple-element.30), channel_id=1, source_target_pairs={{4,8},{8,4},{12,16},{16,12},{20,24},{24,20},{28,32},{32,28},{36,40... | collective-permute-start | bytes 393224 | tf_op jit(solution)/shard_map/ppermute | solution.py:410
  19.2 7.5 %collective-permute-start.1 = (bf16[128,512]{1,0:T(8,128)(2,1)S(1)}, bf16[128,512]{1,0:T(8,128)(2,1)S(1)}, u32[]{:S(2)}, u32[]{:S(2)}) collective-permute-start(bf16[128,512]{1,0:T(8,128)(2,1)S(1)} %get-tuple-element.31), channel_id=1, source_target_pairs={{0,4},{4,0},{8,12},{12,8},{16,20},{20,16},{24,28},{28,24},{32,36},... | collective-permute-start | bytes 393224 | tf_op jit(solution)/shard_map/ppermute | solution.py:411
  30.5 17.2 %all-to-all-start = ((bf16[16,7,16,128]{3,2,1,0:T(8,128)(2,1)}), bf16[16,7,16,128]{3,2,1,0:T(8,128)(2,1)S(1)}, u32[]{:S(2)}, u32[]{:S(2)}) async-start(bf16[16,7,16,128]{3,2,1,0:T(8,128)(2,1)} %bitcast.3), calls=%async_computation | async-start | bytes 917504 | tf_op jit(solution)/shard_map/all_to_all | solution.py:382
  48.4 25.4 %all-to-all-start.1 = ((bf16[8,7,16,128]{3,2,1,0:T(8,128)(2,1)}), bf16[8,7,16,128]{3,2,1,0:T(8,128)(2,1)S(1)}, u32[]{:S(2)}, u32[]{:S(2)}) async-start(bf16[8,7,16,128]{3,2,1,0:T(8,128)(2,1)} %shard_map.80), calls=%async_computation.1 | async-start | bytes 458752 | tf_op jit(solution)/shard_map/all_to_all | solution.py:382
  57.4 9.7 %collective-permute-start.2 = (bf16[6,32,512]{2,1,0:T(8,128)(2,1)S(1)}, bf16[6,32,512]{2,1,0:T(8,128)(2,1)S(1)}, u32[]{:S(2)}, u32[]{:S(2)}) collective-permute-start(bf16[6,32,512]{2,1,0:T(8,128)(2,1)S(1)} %get-tuple-element.45), channel_id=1, source_target_pairs={{0,2},{1,3},{2,0},{3,1},{4,6},{5,7},{6,4},{7,5},{8,10},{9,11},{10,... | collective-permute-start | bytes 589832 | tf_op jit(solution)/shard_map/ppermute | solution.py:429
  60.5 9.8 %collective-permute-start.3 = (bf16[6,32,512]{2,1,0:T(8,128)(2,1)S(1)}, bf16[6,32,512]{2,1,0:T(8,128)(2,1)S(1)}, u32[]{:S(2)}, u32[]{:S(2)}) collective-permute-start(bf16[6,32,512]{2,1,0:T(8,128)(2,1)S(1)} %get-tuple-element.46), channel_id=1, source_target_pairs={{0,1},{1,0},{2,3},{3,2},{4,5},{5,4},{6,7},{7,6},{8,9},{9,8},{10,11... | collective-permute-start | bytes 589832 | tf_op jit(solution)/shard_map/ppermute | solution.py:429
  64.5 7.6 %collective-permute-start.4 = (bf16[6,32,512]{2,1,0:T(8,128)(2,1)S(1)}, bf16[6,32,512]{2,1,0:T(8,128)(2,1)S(1)}, u32[]{:S(2)}, u32[]{:S(2)}) collective-permute-start(bf16[6,32,512]{2,1,0:T(8,128)(2,1)S(1)} %get-tuple-element.47), channel_id=1, source_target_pairs={{0,3},{1,2},{2,1},{3,0},{4,7},{5,6},{6,5},{7,4},{8,11},{9,10},{10,... | collective-permute-start | bytes 589832 | tf_op jit(solution)/shard_map/ppermute | solution.py:429
  74.6 17.6 %all-to-all-start.2 = ((bf16[16,7,16,128]{3,2,1,0:T(8,128)(2,1)}), bf16[16,7,16,128]{3,2,1,0:T(8,128)(2,1)S(1)}, u32[]{:S(2)}, u32[]{:S(2)}) async-start(bf16[16,7,16,128]{3,2,1,0:T(8,128)(2,1)} %shard_map.83), calls=%async_computation.2 | async-start | bytes 917504 | tf_op jit(solution)/shard_map/all_to_all | solution.py:382
  83.2 7.8 %collective-permute-start.5 = (bf16[32,512]{1,0:T(8,128)(2,1)S(1)}, bf16[32,512]{1,0:T(8,128)(2,1)S(1)}, u32[]{:S(2)}, u32[]{:S(2)}) collective-permute-start(bf16[32,512]{1,0:T(8,128)(2,1)S(1)} %get-tuple-element.52), channel_id=1, source_target_pairs={{4,8},{8,4},{12,16},{16,12},{20,24},{24,20},{28,32},{32,28},{36,40... | collective-permute-start | bytes 98312 | tf_op jit(solution)/shard_map/ppermute | solution.py:435
  86.7 4.3 %collective-permute-start.6 = (bf16[32,512]{1,0:T(8,128)(2,1)S(1)}, bf16[32,512]{1,0:T(8,128)(2,1)S(1)}, u32[]{:S(2)}, u32[]{:S(2)}) collective-permute-start(bf16[32,512]{1,0:T(8,128)(2,1)S(1)} %get-tuple-element.53), channel_id=1, source_target_pairs={{0,4},{4,0},{8,12},{12,8},{16,20},{20,16},{24,28},{28,24},{32,36},... | collective-permute-start | bytes 98312 | tf_op jit(solution)/shard_map/ppermute | solution.py:436

commit v9 on v8

--- a/solution.py
+++ b/solution.py
@@ -16,6 +16,7 @@
 FLIPS = (2, 1, 3)
 VMEM = pl.BlockSpec(memory_space=pltpu.VMEM)
 SMEM = pl.BlockSpec(memory_space=pltpu.SMEM)
+HBM = pl.BlockSpec(memory_space=pltpu.HBM)
 PARAMS = pltpu.CompilerParams(vmem_limit_bytes=24 * 1024 * 1024)
 SMALL = pltpu.CompilerParams(vmem_limit_bytes=8 * 1024 * 1024)
 
@@ -148,8 +149,8 @@
 
 def outer_kernel(
     spot, listed, own, from_across, from_partner, cotangent, occupancy, inner, stacked, product,
-    activation, grads, tiles,
-    voxels, cube, patches,
+    activation_hbm, grads, tiles_hbm,
+    voxels, cube, patches, activation, tiles, semaphores,
 ):
     blocks = cotangent.shape[0]
     voxels[0 : blocks * 512, :] = own[...]
@@ -161,6 +162,21 @@
         activation[block] = forward_block(
             spot, listed, block, stacked, cotangent, occupancy, voxels, cube, patches, grads, place
         )
+    copies = [pltpu.make_async_copy(activation, activation_hbm, semaphores.at[0])]
+    copies[0].start()
+
+    def send(first, count):
+        rows = pl.ds(first, count)
+        copy = pltpu.make_async_copy(
+            tiles.at[rows], tiles_hbm.at[rows], semaphores.at[len(copies)]
+        )
+        copy.start()
+        copies.append(copy)
+
+    if tiles.shape[0] > 108:
+        for t in range(108, tiles.shape[0]):
+            tiles[t] = jnp.zeros((16, 128), BF16)
+        send(108, tiles.shape[0] - 108)
     for first in range(0, 9, 2):
         count = min(2, 9 - first)
         lanes = slice(first * 128, (first + count) * 128)
@@ -171,8 +187,10 @@
             for r in range(12):
                 corner = part[r * 16 : (r + 1) * 16, t * 128 : (t + 1) * 128]
                 tiles[(r // 4 * 9 + first + t) * 4 + r % 4] = corner.astype(BF16)
-    for t in range(108, tiles.shape[0]):
-        tiles[t] = jnp.zeros((16, 128), BF16)
+        for a in range(3):
+            send((a * 9 + first) * 4, count * 4)
+    for copy in copies:
+        copy.wait()
 
 
 def add_gradients(spot, listed, picked, blocks, stacked, grads, sums, wide):
@@ -285,8 +303,13 @@
             shape(tiles, 16, 128),
         ],
         in_specs=[SMEM] * 2 + [VMEM] * 8,
-        out_specs=[VMEM] * 3,
-        scratch_shapes=scratch_of(blocks, 2),
+        out_specs=[HBM, VMEM, HBM],
+        scratch_shapes=scratch_of(blocks, 2)
+        + [
+            pltpu.VMEM((blocks, out, 512), BF16),
+            pltpu.VMEM((tiles, 16, 128), BF16),
+            pltpu.SemaphoreType.DMA((17,)),
+        ],
         compiler_params=PARAMS,
         cost_estimate=pl.CostEstimate(flops=10**9, bytes_accessed=4 * 10**6, transcendentals=10**5),
     )(spot, listed, own, *rims, cotangent, occupancy, inner, stacked, product)

time: 93.8 us -> 93.8 us (level)
  no operation moved by 1% of the time
where the time goes in v9:
time: 93.8 us; the launch traced here: 93.2 us
  starting transfers between devices  51.9 us (55%)
  waiting for transfers between devices  14.7 us (16%)
  Pallas kernels  13.4 us (14%)
  blocking collectives  11.4 us (12%)
  other arithmetic  0.97 us (1%)
    all_to_all x3, starting transfers between devices, exchange(): return lax.all_to_all(pieces, 'space', 0, 0, axis_index_groups=groups)  25.5 us
    all_gather x1, blocking collectives, on_device(): gathered = lax.all_gather(features, 'chan', axis=0)  11.4 us
    ppermute x3, starting transfers between devices, on_device(): lax.ppermute(piece, 'chan', [(c, c ^ flip) for c in range(chan)])  9.67 us
    all_to_all x3, waiting for transfers between devices, exchange(): return lax.all_to_all(pieces, 'space', 0, 0, axis_index_groups=groups)  7.31 us
    ppermute x1, starting transfers between devices, on_device(): from_across = lax.ppermute(rim_across, 'space', across)  6.99 us
    ppermute x3, waiting for transfers between devices, on_device(): lax.ppermute(piece, 'chan', [(c, c ^ flip) for c in range(chan)])  5.08 us
    ppermute x1, starting transfers between devices, on_device(): from_partner = lax.ppermute(rim_partner, 'space', partner)  4.17 us
    pallas_call x1, Pallas kernels, call_backward(): pl.pallas_call(functools.partial(backward_kernel, blocks), out_shape=[sha...  4.02 us
  transfers between devices with their start and end apart: 10, of which 6 were waited for; matrix products, arithmetic and copies ran while one was open for 0% of the time, Pallas kernels for 9%

profile of v9, /device:TPU:1, one launch (start us, length us, event | category | flops | bytes accessed | tf_op | source)
XLA Modules:
  0.0 93.2 jit_solution(1312038106753263959)
XLA Ops:
  0.6 0.0 copy-start
  0.6 0.0 copy-start.1
  0.7 11.4 %all-gather = bf16[16,32,512]{2,1,0:T(8,128)(2,1)S(1)} all-gather(bf16[4,32,512]{2,1,0:T(8,128)(2,1)} %param.5), channel_id=2, replica_groups=mesh['space'=128,'chan'=4] {'chan'}, dimensions={0}, use_global_device_ids=true | all-gather | bytes 655360 | tf_op jit(solution)/shard_map/all_gather | solution.py:431
  12.1 0.0 copy-done
  12.1 0.0 copy-start.2
  12.1 0.1 shard_map.77
  12.2 0.0 copy-start.3
  12.2 7.0 %collective-permute-start = (bf16[128,512]{1,0:T(8,128)(2,1)S(1)}, bf16[128,512]{1,0:T(8,128)(2,1)S(1)}, u32[]{:S(2)}, u32[]{:S(2)}) collective-permute-start(bf16[128,512]{1,0:T(8,128)(2,1)S(1)} %get-tuple-element.30), channel_id=1, source_target_pairs={{4,8},{8,4},{12,16},{16,12},{20,24},{24,20},{28,32},{32,28},{36,40... | collective-permute-start | bytes 393224 | tf_op jit(solution)/shard_map/ppermute | solution.py:433
  19.2 4.2 %collective-permute-start.1 = (bf16[128,512]{1,0:T(8,128)(2,1)S(1)}, bf16[128,512]{1,0:T(8,128)(2,1)S(1)}, u32[]{:S(2)}, u32[]{:S(2)}) collective-permute-start(bf16[128,512]{1,0:T(8,128)(2,1)S(1)} %get-tuple-element.31), channel_id=1, source_target_pairs={{0,4},{4,0},{8,12},{12,8},{16,20},{20,16},{24,28},{28,24},{32,36},... | collective-permute-start | bytes 393224 | tf_op jit(solution)/shard_map/ppermute | solution.py:434
  23.3 0.0 copy-done.1
  23.4 0.0 copy-done.2
  23.4 0.0 copy-done.3
  23.4 3.2 %shard_map.76 = (bf16[2,64,512]{2,1,0:T(8,128)(2,1)S(1)}, bf16[192,1152]{1,0:T(8,128)(2,1)S(1)}, bf16[192,1280]{1,0:T(8,128)(2,1)S(1)}, f32[192,1152]{1,0:T(8,128)S(1)}, f32[2048,128]{1,0:T(8,128)S(1)}) custom-call(s32[1]{0:T(128)} %bitcast.spot, s32[4,26]{1,0:T(4,128)S(1)} %copy-done.3, bf16[4,4,32,512]{3,2,1,0:T(8,128)(2,1)S(1)} %bitcast.10, ...), custom_call_target="tpu_custom_call" | custom-call | flops 1000000000 | bytes 4000000 | tf_op jit(solution)/shard_map/pallas_call | solution.py:279
  26.6 0.0 collective-permute-done.from_across
  26.6 0.0 collective-permute-done.1.from_partner
  26.6 3.8 %shard_map.78 = (bf16[4,64,512]{2,1,0:T(8,128)(2,1)}, bf16[192,1280]{1,0:T(8,128)(2,1)S(1)}, bf16[112,16,128]{2,1,0:T(8,128)(2,1)}) custom-call(s32[1]{0:T(128)} %bitcast.spot, s32[4,26]{1,0:T(4,128)S(1)} %copy-done.3, f32[2048,128]{1,0:T(8,128)S(1)} %get-tuple-element.29.own, bf16[128,512]{1,0:T(8,128)(2,1)S(1)} %collective-permute-done.from_across, ...), custom_call_target="tpu_custom_call" | custom-call | flops 1000000000 | bytes 4000000 | tf_op jit(solution)/shard_map/pallas_call | solution.py:298
  30.4 8.1 %all-to-all-start = ((bf16[16,7,16,128]{3,2,1,0:T(8,128)(2,1)}), bf16[16,7,16,128]{3,2,1,0:T(8,128)(2,1)S(1)}, u32[]{:S(2)}, u32[]{:S(2)}) async-start(bf16[16,7,16,128]{3,2,1,0:T(8,128)(2,1)} %bitcast.3), calls=%async_computation | async-start | bytes 917504 | tf_op jit(solution)/shard_map/all_to_all | solution.py:405
  38.6 4.0 %shard_map.79 = (f32[6,32,512]{2,1,0:T(8,128)S(1)}, bf16[6,32,512]{2,1,0:T(8,128)(2,1)S(1)}, bf16[6,32,512]{2,1,0:T(8,128)(2,1)S(1)}, bf16[6,32,512]{2,1,0:T(8,128)(2,1)S(1)}) custom-call(s32[1]{0:T(128)} %bitcast.spot, s32[1]{0:T(128)} %bitcast.4.ring_spot, s32[4,26]{1,0:T(4,128)S(1)} %copy-done.3, bf16[192,1152]{1,0:T(8,128)(2,1)S(1)} %get-tuple-element.33.stacked, ...), custom_call_target="tpu_custom_call" | custom-call | flops 2000000000 | bytes 8000000 | tf_op jit(solution)/shard_map/pallas_call | solution.py:321
  42.6 5.1 %all-to-all-done.pieces = bf16[16,7,16,128]{3,2,1,0:T(8,128)(2,1)S(1)} async-done(((bf16[16,7,16,128]{3,2,1,0:T(8,128)(2,1)}), bf16[16,7,16,128]{3,2,1,0:T(8,128)(2,1)S(1)}, u32[]{:S(2)}, u32[]{:S(2)}) %all-to-all-start) | async-done | bytes 458784 | tf_op jit(solution)/shard_map/all_to_all | solution.py:405
  47.7 0.8 shard_map.80
  48.4 9.0 %all-to-all-start.1 = ((bf16[8,7,16,128]{3,2,1,0:T(8,128)(2,1)}), bf16[8,7,16,128]{3,2,1,0:T(8,128)(2,1)S(1)}, u32[]{:S(2)}, u32[]{:S(2)}) async-start(bf16[8,7,16,128]{3,2,1,0:T(8,128)(2,1)} %shard_map.80), calls=%async_computation.1 | async-start | bytes 458752 | tf_op jit(solution)/shard_map/all_to_all | solution.py:405
  57.4 3.1 %collective-permute-start.2 = (bf16[6,32,512]{2,1,0:T(8,128)(2,1)S(1)}, bf16[6,32,512]{2,1,0:T(8,128)(2,1)S(1)}, u32[]{:S(2)}, u32[]{:S(2)}) collective-permute-start(bf16[6,32,512]{2,1,0:T(8,128)(2,1)S(1)} %get-tuple-element.45), channel_id=1, source_target_pairs={{0,2},{1,3},{2,0},{3,1},{4,6},{5,7},{6,4},{7,5},{8,10},{9,11},{10,... | collective-permute-start | bytes 589832 | tf_op jit(solution)/shard_map/ppermute | solution.py:452
  60.5 4.1 %collective-permute-start.3 = (bf16[6,32,512]{2,1,0:T(8,128)(2,1)S(1)}, bf16[6,32,512]{2,1,0:T(8,128)(2,1)S(1)}, u32[]{:S(2)}, u32[]{:S(2)}) collective-permute-start(bf16[6,32,512]{2,1,0:T(8,128)(2,1)S(1)} %get-tuple-element.46), channel_id=1, source_target_pairs={{0,1},{1,0},{2,3},{3,2},{4,5},{5,4},{6,7},{7,6},{8,9},{9,8},{10,11... | collective-permute-start | bytes 589832 | tf_op jit(solution)/shard_map/ppermute | solution.py:452
  64.5 2.5 %collective-permute-start.4 = (bf16[6,32,512]{2,1,0:T(8,128)(2,1)S(1)}, bf16[6,32,512]{2,1,0:T(8,128)(2,1)S(1)}, u32[]{:S(2)}, u32[]{:S(2)}) collective-permute-start(bf16[6,32,512]{2,1,0:T(8,128)(2,1)S(1)} %get-tuple-element.47), channel_id=1, source_target_pairs={{0,3},{1,2},{2,1},{3,0},{4,7},{5,6},{6,5},{7,4},{8,11},{9,10},{10,... | collective-permute-start | bytes 589832 | tf_op jit(solution)/shard_map/ppermute | solution.py:452
  67.1 0.0 collective-permute-done.2.refs_0_
  67.1 3.2 %collective-permute-done.3.refs_1_ = bf16[6,32,512]{2,1,0:T(8,128)(2,1)S(1)} collective-permute-done((bf16[6,32,512]{2,1,0:T(8,128)(2,1)S(1)}, bf16[6,32,512]{2,1,0:T(8,128)(2,1)S(1)}, u32[]{:S(2)}, u32[]{:S(2)}) %collective-permute-start.3) | collective-permute-done | bytes 196640 | tf_op jit(solution)/shard_map/ppermute | solution.py:452
  70.3 1.9 %collective-permute-done.4.refs_2_ = bf16[6,32,512]{2,1,0:T(8,128)(2,1)S(1)} collective-permute-done((bf16[6,32,512]{2,1,0:T(8,128)(2,1)S(1)}, bf16[6,32,512]{2,1,0:T(8,128)(2,1)S(1)}, u32[]{:S(2)}, u32[]{:S(2)}) %collective-permute-start.4) | collective-permute-done | bytes 196640 | tf_op jit(solution)/shard_map/ppermute | solution.py:452
  72.2 1.7 %all-to-all-done.1.pieces = bf16[8,7,16,128]{3,2,1,0:T(8,128)(2,1)S(1)} async-done(((bf16[8,7,16,128]{3,2,1,0:T(8,128)(2,1)}), bf16[8,7,16,128]{3,2,1,0:T(8,128)(2,1)S(1)}, u32[]{:S(2)}, u32[]{:S(2)}) %all-to-all-start.1) | async-done | bytes 229408 | tf_op jit(solution)/shard_map/all_to_all | solution.py:405
  73.8 0.8 shard_map.83
  74.6 8.4 %all-to-all-start.2 = ((bf16[16,7,16,128]{3,2,1,0:T(8,128)(2,1)}), bf16[16,7,16,128]{3,2,1,0:T(8,128)(2,1)S(1)}, u32[]{:S(2)}, u32[]{:S(2)}) async-start(bf16[16,7,16,128]{3,2,1,0:T(8,128)(2,1)} %shard_map.83), calls=%async_computation.2 | async-start | bytes 917504 | tf_op jit(solution)/shard_map/all_to_all | solution.py:405
  83.1 0.1 shard_map.81
  83.2 3.5 %collective-permute-start.5 = (bf16[32,512]{1,0:T(8,128)(2,1)S(1)}, bf16[32,512]{1,0:T(8,128)(2,1)S(1)}, u32[]{:S(2)}, u32[]{:S(2)}) collective-permute-start(bf16[32,512]{1,0:T(8,128)(2,1)S(1)} %get-tuple-element.52), channel_id=1, source_target_pairs={{4,8},{8,4},{12,16},{16,12},{20,24},{24,20},{28,32},{32,28},{36,40... | collective-permute-start | bytes 98312 | tf_op jit(solution)/shard_map/ppermute | solution.py:458
  86.7 1.9 %collective-permute-start.6 = (bf16[32,512]{1,0:T(8,128)(2,1)S(1)}, bf16[32,512]{1,0:T(8,128)(2,1)S(1)}, u32[]{:S(2)}, u32[]{:S(2)}) collective-permute-start(bf16[32,512]{1,0:T(8,128)(2,1)S(1)} %get-tuple-element.53), channel_id=1, source_target_pairs={{0,4},{4,0},{8,12},{12,8},{16,20},{20,16},{24,28},{28,24},{32,36},... | collective-permute-start | bytes 98312 | tf_op jit(solution)/shard_map/ppermute | solution.py:459
  88.6 2.3 %collective-permute-done.5.from_across = bf16[32,512]{1,0:T(8,128)(2,1)S(1)} collective-permute-done((bf16[32,512]{1,0:T(8,128)(2,1)S(1)}, bf16[32,512]{1,0:T(8,128)(2,1)S(1)}, u32[]{:S(2)}, u32[]{:S(2)}) %collective-permute-start.5) | collective-permute-done | bytes 32800 | tf_op jit(solution)/shard_map/ppermute | solution.py:458
  91.0 0.0 collective-permute-done.6.from_partner
  91.0 0.7 shard_map.82
  91.7 0.6 all-to-all-done.2
  92.2 1.0 %convert_multiply_fusion = f32[108,16,128]{2,1,0:T(8,128)} fusion(bf16[112,16,128]{2,1,0:T(8,128)(2,1)S(1)} %bitcast.12), kind=kLoop, calls=%fused_computation | loop fusion | flops 442368 | bytes 1327104 | tf_op jit(solution)/shard_map/mul | solution.py:461
Async XLA Ops:
  0.6 11.4 %copy-start = (s32[4,512]{1,0:T(4,128)S(1)}, s32[4,512]{1,0:T(4,128)}, u32[]{:S(2)}) copy-start(s32[4,512]{1,0:T(4,128)} %occupancy.7) | copy-start | bytes 24580
  0.6 22.7 %copy-start.1 = (bf16[64,27,128]{2,0,1:T(8,128)(2,1)S(1)}, bf16[64,27,128]{2,0,1:T(8,128)(2,1)}, u32[]{:S(2)}) copy-start(bf16[64,27,128]{2,0,1:T(8,128)(2,1)} %param.7) | copy-start | bytes 1327108
  12.1 11.3 %copy-start.2 = (bf16[4,64,512]{2,1,0:T(8,128)(2,1)S(1)}, bf16[4,64,512]{2,1,0:T(8,128)(2,1)}, u32[]{:S(2)}) copy-start(bf16[4,64,512]{2,1,0:T(8,128)(2,1)} %cotangent.3) | copy-start | bytes 786436
  12.2 11.2 %copy-start.3 = (s32[4,26]{1,0:T(4,128)S(1)}, s32[4,26]{1,0:T(4,128)}, u32[]{:S(2)}) copy-start(s32[4,26]{1,0:T(4,128)} %listed.5) | copy-start | bytes 1252
  12.2 14.5 %collective-permute-start = (bf16[128,512]{1,0:T(8,128)(2,1)S(1)}, bf16[128,512]{1,0:T(8,128)(2,1)S(1)}, u32[]{:S(2)}, u32[]{:S(2)}) collective-permute-start(bf16[128,512]{1,0:T(8,128)(2,1)S(1)} %get-tuple-element.30), channel_id=1, source_target_pairs={{4,8},{8,4},{12,16},{16,12},{20,24},{24,20},{28,32},{32,28},{36,40... | collective-permute-start | bytes 393224 | tf_op jit(solution)/shard_map/ppermute | solution.py:433
  19.2 7.5 %collective-permute-start.1 = (bf16[128,512]{1,0:T(8,128)(2,1)S(1)}, bf16[128,512]{1,0:T(8,128)(2,1)S(1)}, u32[]{:S(2)}, u32[]{:S(2)}) collective-permute-start(bf16[128,512]{1,0:T(8,128)(2,1)S(1)} %get-tuple-element.31), channel_id=1, source_target_pairs={{0,4},{4,0},{8,12},{12,8},{16,20},{20,16},{24,28},{28,24},{32,36},... | collective-permute-start | bytes 393224 | tf_op jit(solution)/shard_map/ppermute | solution.py:434
  30.4 17.2 %all-to-all-start = ((bf16[16,7,16,128]{3,2,1,0:T(8,128)(2,1)}), bf16[16,7,16,128]{3,2,1,0:T(8,128)(2,1)S(1)}, u32[]{:S(2)}, u32[]{:S(2)}) async-start(bf16[16,7,16,128]{3,2,1,0:T(8,128)(2,1)} %bitcast.3), calls=%async_computation | async-start | bytes 917504 | tf_op jit(solution)/shard_map/all_to_all | solution.py:405
  48.4 25.4 %all-to-all-start.1 = ((bf16[8,7,16,128]{3,2,1,0:T(8,128)(2,1)}), bf16[8,7,16,128]{3,2,1,0:T(8,128)(2,1)S(1)}, u32[]{:S(2)}, u32[]{:S(2)}) async-start(bf16[8,7,16,128]{3,2,1,0:T(8,128)(2,1)} %shard_map.80), calls=%async_computation.1 | async-start | bytes 458752 | tf_op jit(solution)/shard_map/all_to_all | solution.py:405
  57.4 9.7 %collective-permute-start.2 = (bf16[6,32,512]{2,1,0:T(8,128)(2,1)S(1)}, bf16[6,32,512]{2,1,0:T(8,128)(2,1)S(1)}, u32[]{:S(2)}, u32[]{:S(2)}) collective-permute-start(bf16[6,32,512]{2,1,0:T(8,128)(2,1)S(1)} %get-tuple-element.45), channel_id=1, source_target_pairs={{0,2},{1,3},{2,0},{3,1},{4,6},{5,7},{6,4},{7,5},{8,10},{9,11},{10,... | collective-permute-start | bytes 589832 | tf_op jit(solution)/shard_map/ppermute | solution.py:452
  60.5 9.8 %collective-permute-start.3 = (bf16[6,32,512]{2,1,0:T(8,128)(2,1)S(1)}, bf16[6,32,512]{2,1,0:T(8,128)(2,1)S(1)}, u32[]{:S(2)}, u32[]{:S(2)}) collective-permute-start(bf16[6,32,512]{2,1,0:T(8,128)(2,1)S(1)} %get-tuple-element.46), channel_id=1, source_target_pairs={{0,1},{1,0},{2,3},{3,2},{4,5},{5,4},{6,7},{7,6},{8,9},{9,8},{10,11... | collective-permute-start | bytes 589832 | tf_op jit(solution)/shard_map/ppermute | solution.py:452
  64.5 7.6 %collective-permute-start.4 = (bf16[6,32,512]{2,1,0:T(8,128)(2,1)S(1)}, bf16[6,32,512]{2,1,0:T(8,128)(2,1)S(1)}, u32[]{:S(2)}, u32[]{:S(2)}) collective-permute-start(bf16[6,32,512]{2,1,0:T(8,128)(2,1)S(1)} %get-tuple-element.47), channel_id=1, source_target_pairs={{0,3},{1,2},{2,1},{3,0},{4,7},{5,6},{6,5},{7,4},{8,11},{9,10},{10,... | collective-permute-start | bytes 589832 | tf_op jit(solution)/shard_map/ppermute | solution.py:452
  74.6 17.6 %all-to-all-start.2 = ((bf16[16,7,16,128]{3,2,1,0:T(8,128)(2,1)}), bf16[16,7,16,128]{3,2,1,0:T(8,128)(2,1)S(1)}, u32[]{:S(2)}, u32[]{:S(2)}) async-start(bf16[16,7,16,128]{3,2,1,0:T(8,128)(2,1)} %shard_map.83), calls=%async_computation.2 | async-start | bytes 917504 | tf_op jit(solution)/shard_map/all_to_all | solution.py:405
  83.2 7.8 %collective-permute-start.5 = (bf16[32,512]{1,0:T(8,128)(2,1)S(1)}, bf16[32,512]{1,0:T(8,128)(2,1)S(1)}, u32[]{:S(2)}, u32[]{:S(2)}) collective-permute-start(bf16[32,512]{1,0:T(8,128)(2,1)S(1)} %get-tuple-element.52), channel_id=1, source_target_pairs={{4,8},{8,4},{12,16},{16,12},{20,24},{24,20},{28,32},{32,28},{36,40... | collective-permute-start | bytes 98312 | tf_op jit(solution)/shard_map/ppermute | solution.py:458
  86.7 4.3 %collective-permute-start.6 = (bf16[32,512]{1,0:T(8,128)(2,1)S(1)}, bf16[32,512]{1,0:T(8,128)(2,1)S(1)}, u32[]{:S(2)}, u32[]{:S(2)}) collective-permute-start(bf16[32,512]{1,0:T(8,128)(2,1)S(1)} %get-tuple-element.53), channel_id=1, source_target_pairs={{0,4},{4,0},{8,12},{12,8},{16,20},{20,16},{24,28},{28,24},{32,36},... | collective-permute-start | bytes 98312 | tf_op jit(solution)/shard_map/ppermute | solution.py:459
